TPU v7x, 32 devices: a whole 2x2x4 slice. The times are simulated.
32 devices in a mesh: vis: 2 (over x), grp: 8 (over z, core), enc: 2 (over y).
Axes of the slice: x: 2, y: 2, z: 4, core: 2. Of those that a mesh axis runs over, the one named last changes fastest.
Arguments:
- image_tokens: bfloat16 [8, 256, 6144], P('grp', None, 'enc'), may hold values from -8 to 8
- vision_gain: float32 [6144], P('enc'), may hold values from 0.1 to 1.9
- up_weight: bfloat16 [6144, 12288], P('enc', ('vis', 'grp')), may hold values from -0.078125 to 0.078125
- down_weight: bfloat16 [12288, 6144], P(('vis', 'grp'), 'enc'), may hold values from -0.0546875 to 0.0546875
- project_weight: bfloat16 [6144, 4096], P('enc', 'vis'), may hold values from -0.078125 to 0.078125
- encoder_gain: float32 [4096], P('vis'), may hold values from 0.1 to 1.9
- qkv_weight: bfloat16 [3, 4096, 2048], P(None, 'vis', 'enc'), may hold values from -0.6 to 0.6
- out_weight: bfloat16 [2048, 4096], P('enc', 'vis'), may hold values from -0.5 to 0.5
- captions: bfloat16 [32, 16, 4096], P('grp', 'enc', 'vis'), may hold values from -8 to 8
- cand_counts: int32 [8], replicated, may hold values from 1 to 12, 32 in all
- caption_lengths: int32 [32], P('grp'), may hold values from 1 to 16
Outputs:
- vision_out: bfloat16 [8, 256, 6144], P('grp', None, 'enc')
- caption_out: bfloat16 [32, 16, 4096], P('grp', 'enc', 'vis')
Inputs may be any that keep to these rules, and one draw needn't show every extreme that they name: `cand_counts`: every image has at least one candidate, the counts sum to 32 and the largest is 12.
All inputs are finite; a program needn't handle non-finite values.
Results may differ from a plain program's by a relative error of at most 0.035.
Values may be sent and summed in bfloat16 or wider, within the bound.
No kernel may reach another device: no remote copies, remote signals or barrier semaphores. Data moves between devices by JAX's collectives and lax.ppermute only.
A program may use at most 192 MiB of HBM per device.

v0:
```python
import functools

import jax
import jax.numpy as jnp
from jax import lax
from jax.experimental import pallas as pl
from jax.experimental.pallas import tpu as pltpu
from jax.sharding import PartitionSpec as P

DH = 256
CAP = 16
MOSTC = 12


EPSILON = 1e-06
FLOOR = -1e30


def dot(a, b):
    return jnp.dot(a, b, preferred_element_type=jnp.float32)


def wide(a):
    return a.astype(jnp.float32)


def slim(a):
    return a.astype(jnp.bfloat16)


def shifted(value, axis, step):
    count = lax.axis_size(axis)
    return lax.ppermute(value, axis, [(i, (i + step) % count) for i in range(count)])


def summed(value, axis):
    if lax.axis_size(axis) != 2:
        return lax.psum(value, axis)
    return value + shifted(value, axis, 1)


def joined(value, axis, dim):
    if lax.axis_size(axis) != 2:
        return lax.all_gather(value, axis, axis=dim, tiled=True)
    other = shifted(value, axis, 1)
    first = lax.axis_index(axis) == 0
    return jnp.concatenate(
        [jnp.where(first, value, other), jnp.where(first, other, value)], axis=dim
    )


TOKEN = (8, 128)
HBM = pl.BlockSpec(memory_space=pl.ANY)
VMEM = pl.BlockSpec(memory_space=pltpu.VMEM)
SMEM = pl.BlockSpec(memory_space=pltpu.SMEM)
LIGHT = pl.CostEstimate(flops=1024, bytes_accessed=1024, transcendentals=0)
PARAMS = pltpu.CompilerParams(vmem_limit_bytes=20 * 1024 * 1024)


def tile_of(size, most):
    return most if size % most == 0 else size


def pass_kernel(value_ref, token_ref, out_ref):
    pass


def passed(value, token):
    return pl.pallas_call(
        pass_kernel,
        in_specs=[HBM, HBM],
        out_specs=HBM,
        out_shape=jax.ShapeDtypeStruct(value.shape, value.dtype),
        input_output_aliases={0: 0},
        compiler_params=PARAMS,
        cost_estimate=LIGHT,
    )(value, token)


def up_kernel(cores, mine_ref, theirs_ref, *refs):
    weights, (out_ref, token_ref, rows_ref) = refs[:cores], refs[-3:]
    half = mine_ref.shape[0]
    units = weights[0].shape[1]
    tile = tile_of(units, 256)
    rows_ref[:half] = mine_ref[...]
    rows_ref[half:] = theirs_ref[...]
    token_ref[...] = jnp.zeros(TOKEN, jnp.float32)
    for core in range(cores):
        for first in range(0, units, tile):
            out_ref[:, core * units + first : core * units + first + tile] = slim(
                dot(rows_ref[...], weights[core][:, first : first + tile])
            )


def up_call(halves, weights, after):
    cores = len(weights)
    depth, units = weights[0].shape
    rows = 2 * halves[0].shape[0]
    return pl.pallas_call(
        functools.partial(up_kernel, cores),
        in_specs=[VMEM] * (2 + cores) + [HBM] * len(after),
        out_specs=[VMEM, VMEM],
        out_shape=[
            jax.ShapeDtypeStruct((rows, cores * units), jnp.bfloat16),
            jax.ShapeDtypeStruct(TOKEN, jnp.float32),
        ],
        scratch_shapes=[pltpu.VMEM((rows, depth), jnp.bfloat16)],
        compiler_params=PARAMS,
        cost_estimate=LIGHT,
    )(*halves, *weights, *after)


def down_kernel(cores, own_ref, other_ref, *refs):
    weights, (kept_ref, sent_ref, token_ref, total_ref) = refs[:cores], refs[-6:-2]
    hidden = refs[-2:]
    units, columns = weights[0].shape
    tile = tile_of(units, 256)
    half = kept_ref.shape[0]
    part = tile_of(columns, 512)
    token_ref[...] = jnp.zeros(TOKEN, jnp.float32)
    order = [(core, first) for core in range(cores) for first in range(0, units, tile)]

    def fill(at):
        core, first = order[at]
        columns_at = slice(core * units + first, core * units + first + tile)
        total = wide(own_ref[:, columns_at]) + wide(other_ref[:, columns_at])
        hidden[at % 2][...] = slim(0.5 * total * (1.0 + lax.erf(total * 0.5**0.5)))

    fill(0)
    for at, (core, first) in enumerate(order):
        for start in range(0, columns, part):
            term = dot(hidden[at % 2][...], weights[core][first : first + tile, start : start + part])
            if at:
                term = total_ref[:, start : start + part] + term
            if at + 1 < len(order):
                total_ref[:, start : start + part] = term
            else:
                kept_ref[:, start : start + part] = slim(term[:half])
                sent_ref[:, start : start + part] = slim(term[half:])
        if at + 1 < len(order):
            fill(at + 1)


def down_call(own, other, weights, after):
    cores = len(weights)
    units, columns = weights[0].shape
    tile = tile_of(units, 256)
    rows = own.shape[0]
    half = jax.ShapeDtypeStruct((rows // 2, columns), jnp.bfloat16)
    return pl.pallas_call(
        functools.partial(down_kernel, cores),
        in_specs=[VMEM] * (2 + cores) + [HBM] * len(after),
        out_specs=[VMEM, VMEM, VMEM],
        out_shape=[half, half, jax.ShapeDtypeStruct(TOKEN, jnp.float32)],
        scratch_shapes=[pltpu.VMEM((rows, columns), jnp.float32)]
        + [pltpu.VMEM((rows, tile), jnp.bfloat16)] * 2,
        compiler_params=PARAMS,
        cost_estimate=LIGHT,
    )(own, other, *weights, *after)


def project_kernel(rows_ref, weight_ref, out_ref):
    columns = weight_ref.shape[1]
    part = tile_of(columns, 512)
    for first in range(0, columns, part):
        out_ref[:, first : first + part] = slim(
            dot(rows_ref[...], weight_ref[:, first : first + part])
        )


def project_call(rows, weight):
    return pl.pallas_call(
        project_kernel,
        in_specs=[VMEM, VMEM],
        out_specs=VMEM,
        out_shape=jax.ShapeDtypeStruct((rows.shape[0], weight.shape[1]), jnp.bfloat16),
        compiler_params=PARAMS,
        cost_estimate=LIGHT,
    )(rows, weight)


def image_kernel(vis_ref, own_ref, other_ref, gain_ref, weight_ref, kept_ref, sent_ref, power_ref):
    share = weight_ref.shape[2] // 2
    full = wide(own_ref[...]) + wide(other_ref[...])
    power = jnp.sum(full * full, axis=1, keepdims=True)
    scaled = slim(full * gain_ref[...])
    power_ref[...] = jnp.broadcast_to(power, power_ref.shape)
    high = slim(power)
    middle = slim(power - wide(high))
    low = slim(power - wide(high) - wide(middle))
    lane = lax.broadcasted_iota(jnp.int32, (power.shape[0], 128), 1)
    parts = jnp.where(lane == 0, wide(high), jnp.where(lane == 1, wide(middle), wide(low)))
    sent_ref[:, 2 * share :] = slim(jnp.where(lane < 3, parts, 0.0))
    vis = vis_ref[0]
    for kind in range(2):
        columns = slice(kind * share, (kind + 1) * share)
        other = pl.ds(pl.multiple_of((1 - vis) * share, share), share)
        sent_ref[:, columns] = slim(dot(scaled, weight_ref[kind + 1, :, other]))
    for kind in range(2):
        columns = slice(kind * share, (kind + 1) * share)
        mine = pl.ds(pl.multiple_of(vis * share, share), share)
        kept_ref[:, columns] = dot(scaled, weight_ref[kind + 1, :, mine])


def image_call(own, other, gain, weight, spots):
    rows = own.shape[0]
    share = weight.shape[2] // 2
    return pl.pallas_call(
        image_kernel,
        in_specs=[pl.BlockSpec(memory_space=pltpu.SMEM)] + [VMEM] * 4,
        out_specs=[VMEM] * 3,
        out_shape=[
            jax.ShapeDtypeStruct((rows, 2 * share), jnp.float32),
            jax.ShapeDtypeStruct((rows, 2 * share + 128), jnp.bfloat16),
            jax.ShapeDtypeStruct((rows, 128), jnp.float32),
        ],
        compiler_params=PARAMS,
        cost_estimate=LIGHT,
    )(spots, own, other, gain[None], weight)


def heads_kernel(vis_ref, rows_ref, weight_ref, *refs):
    sent_ref, kept_ref, token_ref = refs[-3:]
    kinds, _, inner = weight_ref.shape
    share = inner // 2
    vis = vis_ref[0]
    token_ref[...] = jnp.zeros(TOKEN, jnp.float32)
    for which, out_ref in ((1 - vis, sent_ref), (vis, kept_ref)):
        for kind in range(kinds):
            heads = pl.ds(pl.multiple_of(which * share, share), share)
            term = dot(rows_ref[...], weight_ref[kind, :, heads])
            out_ref[:, kind * share : (kind + 1) * share] = term.astype(out_ref.dtype)


def heads_call(block, weight, spots, after):
    shape = (block.shape[0], weight.shape[0] * weight.shape[2] // 2)
    return pl.pallas_call(
        heads_kernel,
        in_specs=[pl.BlockSpec(memory_space=pltpu.SMEM), VMEM, VMEM] + [HBM] * len(after),
        out_specs=[VMEM, VMEM, VMEM],
        out_shape=[
            jax.ShapeDtypeStruct(shape, jnp.bfloat16),
            jax.ShapeDtypeStruct(shape, jnp.float32),
            jax.ShapeDtypeStruct(TOKEN, jnp.float32),
        ],
        compiler_params=PARAMS,
        cost_estimate=LIGHT,
    )(spots, block, weight, *after)


def add_kernel(count, *refs):
    out_ref, token_ref = refs[-2:]
    rows = out_ref.shape[0]
    step = tile_of(rows, 32)

    def body(at, carry):
        part = pl.ds(pl.multiple_of(at * step, step), step)
        total = wide(refs[0][part])
        for ref in refs[1:count]:
            total = total + wide(ref[part])
        out_ref[part] = slim(total)
        return carry

    lax.fori_loop(0, rows // step, body, 0)
    token_ref[...] = jnp.zeros(TOKEN, jnp.float32)


def add_call(values, after):
    return pl.pallas_call(
        functools.partial(add_kernel, len(values)),
        in_specs=[VMEM] * len(values) + [HBM] * len(after),
        out_specs=[VMEM, VMEM],
        out_shape=[
            jax.ShapeDtypeStruct(values[0].shape, jnp.bfloat16),
            jax.ShapeDtypeStruct(TOKEN, jnp.float32),
        ],
        compiler_params=PARAMS,
        cost_estimate=LIGHT,
    )(*values, *after)


def message_kernel(lengths_ref, kept_ref, other_ref, *refs):
    out_ref = refs[-1]
    rows, columns = kept_ref.shape
    out_ref[:, :columns] = slim(kept_ref[...] + wide(other_ref[...]))
    row = lax.broadcasted_iota(jnp.int32, (rows, 128), 0)
    live = jnp.zeros((rows, 128), jnp.float32)
    for cand in range(rows // CAP):
        inside = (row >= cand * CAP) & (row < cand * CAP + lengths_ref[cand])
        live = jnp.where(inside, 1.0, live)
    out_ref[:, columns:] = slim(live)


def message_call(lengths, kept, other, after):
    rows, columns = kept.shape
    return pl.pallas_call(
        message_kernel,
        in_specs=[SMEM, VMEM, VMEM] + [HBM] * len(after),
        out_specs=VMEM,
        out_shape=jax.ShapeDtypeStruct((rows, columns + 128), jnp.bfloat16),
        compiler_params=PARAMS,
        cost_estimate=LIGHT,
    )(lengths, kept, other, *after)


def stack_kernel(count, *refs):
    out_ref = refs[-1]
    rows = refs[0].shape[0]
    for at in range(count):
        out_ref[at * rows : (at + 1) * rows] = refs[at][...]


def stack_call(values):
    rows, columns = values[0].shape
    return pl.pallas_call(
        functools.partial(stack_kernel, len(values)),
        in_specs=[VMEM] * len(values),
        out_specs=VMEM,
        out_shape=jax.ShapeDtypeStruct((rows * len(values), columns), values[0].dtype),
        compiler_params=PARAMS,
        cost_estimate=LIGHT,
    )(*values)


def span_of(counts_ref, group, images):
    first, end = jnp.int32(0), jnp.int32(0)
    for image in range(images):
        first = first + jnp.where(image < group, counts_ref[image], 0)
        end = end + jnp.where(image <= group, counts_ref[image], 0)
    return first, end


def row_ids(index, place, core, places, word_rows, sign):
    step = index // word_rows
    at = lax.rem(place + sign * step + places, places)
    return (at * 2 + core) * word_rows + lax.rem(index, word_rows)


def near_kernel(places, spots_ref, counts_ref, own_ref, other_ref, *refs):
    out_ref, token_ref = refs[-2:]
    near_rows = out_ref.shape[0]
    rows = own_ref.shape[0]
    place, core, group = spots_ref[1], spots_ref[2], spots_ref[4]
    first, _ = span_of(counts_ref, group, counts_ref.shape[0])
    near_id = first * CAP + lax.broadcasted_iota(jnp.int32, (near_rows, rows), 0)
    column = lax.broadcasted_iota(jnp.int32, (near_rows, rows), 1)
    total = 0.0
    for core_at, ref in ((core, own_ref), (1 - core, other_ref)):
        pick = near_id == row_ids(column, place, core_at, places, rows // places, -1)
        total = total + dot(slim(jnp.where(pick, 1.0, 0.0)), ref[...])
    out_ref[...] = slim(total)
    token_ref[...] = jnp.zeros(TOKEN, jnp.float32)


def near_call(spots, counts, own, other, places, near_rows, after):
    return pl.pallas_call(
        functools.partial(near_kernel, places),
        in_specs=[SMEM, SMEM, VMEM, VMEM] + [HBM] * len(after),
        out_specs=[VMEM, VMEM],
        out_shape=[
            jax.ShapeDtypeStruct((near_rows, own.shape[1]), jnp.bfloat16),
            jax.ShapeDtypeStruct(TOKEN, jnp.float32),
        ],
        compiler_params=PARAMS,
        cost_estimate=LIGHT,
    )(spots, counts, own, other, *after)


def across(a, b):
    return lax.dot_general(a, b, (((1,), (1,)), ((), ())), preferred_element_type=jnp.float32)


def attend_kernel(places, word_rows, width, spots_ref, counts_ref, near_ref, *refs):
    parts, outs, result_ref = refs[:6], refs[6 : 6 + places], refs[-1]
    near_rows = near_ref.shape[0]
    share = result_ref.shape[1]
    place, core, group = spots_ref[1], spots_ref[2], spots_ref[4]
    first, end = span_of(counts_ref, group, counts_ref.shape[0])
    sources = []
    for kept_ref, got_ref, power_ref in (parts[:3], parts[3:]):
        power = power_ref[:, :1] + jnp.sum(
            wide(got_ref[:, 2 * share : 2 * share + 128]), axis=1, keepdims=True
        )
        scale = lax.rsqrt(power / width + EPSILON)
        total = slim((kept_ref[...] + wide(got_ref[:, : 2 * share])) * scale)
        sources.append((total[:, :share], total[:, share:], None))
    lane = lax.broadcasted_iota(jnp.int32, (16, 128), 1)
    pick = slim(jnp.where(lane == 0, 1.0, 0.0))
    live = across(pick, near_ref[:, 3 * share :])[:1]
    shape = (near_rows, near_rows)
    own = lax.broadcasted_iota(jnp.int32, shape, 0) // CAP == lax.broadcasted_iota(jnp.int32, shape, 1) // CAP
    allowed = own & (live > 0.5)
    sources.append((near_ref[:, share : 2 * share], near_ref[:, 2 * share : 3 * share], allowed))
    for head in range(share // DH):
        columns = slice(head * DH, (head + 1) * DH)
        query = near_ref[:, columns]
        scores = []
        for keys, _, mask in sources:
            score = across(query, keys[:, columns]) * DH ** (-0.5)
            scores.append(score if mask is None else jnp.where(mask, score, FLOOR))
        top = functools.reduce(
            jnp.maximum, [jnp.max(score, axis=1, keepdims=True) for score in scores]
        )
        total, mixed = 0.0, 0.0
        for score, (_, values, mask) in zip(scores, sources):
            weights = jnp.exp(score - top)
            if mask is not None:
                weights = jnp.where(mask, weights, 0.0)
            total = total + jnp.sum(weights, axis=1, keepdims=True)
            mixed = mixed + dot(slim(weights), values[:, columns])
        result_ref[:, columns] = slim(mixed / total)
    block = 2 * word_rows
    row = lax.broadcasted_iota(jnp.int32, (block, near_rows), 0)
    near_id = first * CAP + lax.broadcasted_iota(jnp.int32, (block, near_rows), 1)
    core_at = jnp.where(row < word_rows, core, 1 - core)
    for step, out_ref in enumerate(outs):
        home = lax.rem(place + step, places)
        ids = (home * 2 + core_at) * word_rows + lax.rem(row, word_rows)
        put = (ids == near_id) & (near_id < end * CAP)
        out_ref[...] = slim(dot(slim(jnp.where(put, 1.0, 0.0)), result_ref[...]))


def attend_call(spots, counts, near, pieces, places, word_rows, width):
    share = pieces[0].shape[1] // 2
    return pl.pallas_call(
        functools.partial(attend_kernel, places, word_rows, width),
        in_specs=[SMEM, SMEM] + [VMEM] * (1 + len(pieces)),
        out_specs=[VMEM] * places,
        out_shape=[jax.ShapeDtypeStruct((2 * word_rows, share), jnp.bfloat16)] * places,
        scratch_shapes=[pltpu.VMEM((near.shape[0], share), jnp.bfloat16)],
        compiler_params=PARAMS,
        cost_estimate=LIGHT,
    )(spots, counts, near, *pieces)


def land_kernel(*refs):
    kept_ref, given_ref = refs[-2:]
    rows = kept_ref.shape[0]
    total = wide(refs[0][...])
    for ref in refs[1:-2]:
        total = total + wide(ref[...])
    kept_ref[...] = slim(total[:rows])
    given_ref[...] = slim(total[rows:])


def land_call(values):
    rows, columns = values[0].shape
    return pl.pallas_call(
        land_kernel,
        in_specs=[VMEM] * len(values),
        out_specs=[VMEM, VMEM],
        out_shape=[jax.ShapeDtypeStruct((rows // 2, columns), jnp.bfloat16)] * 2,
        compiler_params=PARAMS,
        cost_estimate=LIGHT,
    )(*values)


def output_kernel(spots_ref, kept_ref, core_ref, vis_ref, both_ref, weight_ref, mine_ref, sent_ref):
    vis, enc = spots_ref[0], spots_ref[3]
    share = kept_ref.shape[1]
    own = slim(wide(kept_ref[...]) + wide(core_ref[...]))
    other = slim(wide(vis_ref[...]) + wide(both_ref[...]))
    slots = CAP // 2
    columns = weight_ref.shape[1]
    part = tile_of(columns, 512)
    for start in range(0, columns, part):
        span = slice(start, start + part)
        total = dot(own, weight_ref[pl.ds(pl.multiple_of(vis * share, share), share), span])
        total = total + dot(other, weight_ref[pl.ds(pl.multiple_of((1 - vis) * share, share), share), span])
        firsts = range(0, total.shape[0], CAP)
        low = jnp.concatenate([total[at : at + slots] for at in firsts])
        high = jnp.concatenate([total[at + slots : at + CAP] for at in firsts])
        mine_ref[:, span] = jnp.where(enc == 0, low, high)
        sent_ref[:, span] = slim(jnp.where(enc == 0, high, low))


def output_call(spots, pieces, weight):
    shape = (pieces[0].shape[0] // 2, weight.shape[1])
    return pl.pallas_call(
        output_kernel,
        in_specs=[SMEM] + [VMEM] * 5,
        out_specs=[VMEM, VMEM],
        out_shape=[
            jax.ShapeDtypeStruct(shape, jnp.float32),
            jax.ShapeDtypeStruct(shape, jnp.bfloat16),
        ],
        compiler_params=PARAMS,
        cost_estimate=LIGHT,
    )(spots, *pieces, weight)


def on_device(
    image_tokens,
    vision_gain,
    up_weight,
    down_weight,
    project_weight,
    encoder_gain,
    qkv_weight,
    out_weight,
    captions,
    cand_counts,
    caption_lengths,
):
    vis_count = lax.axis_size("vis")
    enc_count = lax.axis_size("enc")
    groups = lax.axis_size("grp")
    vis = lax.axis_index("vis")
    group = lax.axis_index("grp")
    rows, features = image_tokens.shape[1:]
    all_features = features * enc_count
    width = captions.shape[2] * vis_count
    pair = vis_count == 2
    part_rows = rows // vis_count

    cores = 2 if groups % 2 == 0 else 1
    places = groups // cores
    place, core = group // cores, group % cores
    core_swap = [(i, i ^ 1) for i in range(groups)]
    up_weights, down_weights = [up_weight], [down_weight]
    if cores == 2:
        up_weights.append(lax.ppermute(up_weight, "grp", core_swap))
        down_weights.append(lax.ppermute(down_weight, "grp", core_swap))
        if up_weight.shape[1] % 128:
            up_weights = [jnp.concatenate(up_weights, axis=1)]
            down_weights = [jnp.concatenate(down_weights)]

    def to_place(value, step):
        return lax.ppermute(
            value, "grp", [(i, (i + step * cores) % groups) for i in range(groups)]
        )

    def mine_of(value):
        return lax.dynamic_slice_in_dim(value, vis * part_rows, part_rows, axis=0)

    def halves_of(mine, value):
        if pair and value is None:
            return [mine, shifted(mine, "vis", 1)]
        if pair:
            return [mine, lax.dynamic_slice_in_dim(value, (1 - vis) * part_rows, part_rows, axis=0)]
        if value is None:
            value = lax.all_gather(mine, "vis", axis=0, tiled=True)
        return [value[: rows // 2], value[rows // 2 :]]

    token = []

    def gated(value):
        return value + token[0][0, 0].astype(value.dtype) if token else value

    words = wide(captions)
    word_power = summed(jnp.sum(words * words, axis=-1), "vis")
    tokens = wide(image_tokens[0])
    row_total, row_squares = summed(
        jnp.stack([jnp.sum(tokens, axis=-1), jnp.sum(tokens * tokens, axis=-1)]), "enc"
    )
    mean = row_total / all_features
    spread = row_squares / all_features - mean * mean
    normed = slim(
        (tokens - mean[:, None]) * lax.rsqrt(spread + EPSILON)[:, None] * vision_gain
    )
    my_tokens = mine_of(image_tokens[0])
    my_normed = mine_of(normed)

    inner = qkv_weight.shape[2]
    heads = inner // DH
    shares = vis_count if heads % vis_count == 0 else 1
    share = inner // shares
    fast = pair and shares == 2 and cores == 2 and enc_count == 2
    spots = jnp.stack([vis, place, core, lax.axis_index("enc"), group])
    word_normed = slim(words * lax.rsqrt(word_power / width + EPSILON)[..., None] * encoder_gain)
    all_words = joined(word_normed, "enc", 1)
    cand_local = all_words.shape[0]
    word_rows = cand_local * CAP
    flat_words = all_words.reshape(word_rows, all_words.shape[2])

    def head_weights(which):
        return lax.dynamic_slice_in_dim(qkv_weight, which * share, share, axis=2)

    def heads_of(block, weight):
        return jnp.einsum("rd,kdh->rkh", block, weight, preferred_element_type=jnp.float32)

    def head_sum(values):
        if shares == 1:
            return lax.psum(values, "vis")
        return lax.psum_scatter(values, "vis", scatter_dimension=2, tiled=True)

    arrived, blocks, pres, outs, backs = {}, {}, {}, {}, {}

    def forwarded(step):
        if step < places:
            here = passed(arrived[step], token[0]) if step > 1 else arrived[step]
            if step + 1 < places:
                arrived[step + 1] = to_place(here, 1)
            blocks[step] = halves_of(here, None)

    def up(step, *after):
        if step < places:
            pre, token[:] = (lambda got: (got[0], [got[1]]))(
                up_call(blocks[step], up_weights, [*token, *after])
            )
            if enc_count == 2:
                pres[step] = pre, shifted(pre, "enc", 1)
            else:
                pres[step] = pre, slim(lax.psum(wide(pre), "enc") - wide(pre))

    def down(step, *after):
        if step < places:
            kept, sent, next_token = down_call(*pres[step], down_weights, [*token, *after])
            token[:] = [next_token]
            if pair:
                outs[step] = kept, shifted(sent, "vis", 1)
            else:
                out = jnp.concatenate([kept, wide(sent)])
                kept = lax.psum_scatter(out, "vis", scatter_dimension=0, tiled=True)
                outs[step] = kept, jnp.zeros_like(kept, jnp.bfloat16)

    def back(step):
        if 0 < step < places:
            parts = [*outs[step], *([backs[step - 1]] if step > 1 else [])]
            total, next_token = add_call(parts, token)
            token[:] = [next_token]
            backs[step] = to_place(total, 1)

    if places > 1:
        arrived[1] = to_place(my_normed, 1)
    if fast:
        word_sent, word_kept, word_token = heads_call(
            flat_words, qkv_weight, spots, [my_normed, my_tokens]
        )
        token[:] = [word_token]
        word_other = shifted(word_sent, "vis", 1)
    else:
        word_kept = head_sum(heads_of(flat_words, qkv_weight)).reshape(word_rows, 3 * share)
        word_other = jnp.zeros_like(word_kept, jnp.bfloat16)
    forwarded(1)
    messages = []

    def hop():
        if len(messages) < places:
            messages.append(to_place(messages[-1], 1))
        return messages[-1]

    blocks[0] = halves_of(my_normed, normed)
    up(0)
    forwarded(2)
    messages.append(message_call(caption_lengths, word_kept, word_other, token))
    up(1, down_weights[-1], messages[0])
    down(0)
    forwarded(3)
    up(2, blocks[places - 1][0], hop())
    down(1)
    up(3, hop())
    down(2, hop())
    word_block = stack_call(messages)
    if cores == 2:
        word_blocks = [word_block, lax.ppermute(word_block, "grp", core_swap)]
    else:
        word_blocks = [word_block]
    back(1)
    for step in range(4, places):
        forwarded(step)
        up(step)
        down(step - 1)
    down(places - 1)
    for step in range(2, places):
        back(step)

    home = [my_tokens, *outs[0], *([backs[places - 1]] if places > 1 else [])]
    cands = groups * cand_local
    most = min(MOSTC, cands)
    if fast:
        near, near_token = near_call(
            spots, cand_counts, *word_blocks, places, most * CAP, token
        )
        my_vision, _ = add_call(home, [near_token])
        other_vision = shifted(my_vision, "vis", 1)
        pieces = []
        for block in (my_vision, other_vision):
            partial = project_call(block, project_weight)
            full = shifted(partial, "enc", 1)
            pieces.append(image_call(partial, full, encoder_gain, qkv_weight, spots))
        got = [shifted(sent, "vis", 1) for _, sent, _ in pieces]
        parts = []
        for here, there in ((0, 1), (1, 0)):
            parts += [pieces[here][0], got[there], pieces[here][2]]
        placed = attend_call(spots, cand_counts, near, parts, places, word_rows, width)
        landed = [to_place(part, step) if step else part for step, part in enumerate(placed)]
        kept, given = land_call(landed)
        across_both = [
            (v * groups + i, (1 - v) * groups + (i ^ 1)) for v in range(2) for i in range(groups)
        ]
        from_core = lax.ppermute(given, "grp", core_swap)
        from_both = lax.ppermute(given, ("vis", "grp"), across_both)
        from_vis = shifted(kept, "vis", 1)
        mine, sent = output_call(spots, [kept, from_core, from_vis, from_both], out_weight)
        words_out = (mine + wide(shifted(sent, "enc", 1))).reshape(words.shape)
        vision_rows = jnp.where(
            vis == 0,
            jnp.concatenate([my_vision, other_vision]),
            jnp.concatenate([other_vision, my_vision]),
        )
        return (vision_rows[None], slim(words + words_out))
    my_vision = slim(sum([wide(part) for part in home]))

    ends = jnp.cumsum(cand_counts)
    start = ends[group] - cand_counts[group]
    near_ids = start * CAP + jnp.arange(most * CAP, dtype=jnp.int32)
    owned = near_ids < ends[group] * CAP

    def ids_of(core_at, sign):
        steps = jnp.arange(places, dtype=jnp.int32)[:, None]
        first = ((place + sign * steps) % places * cores + core_at) * word_rows
        return (first + jnp.arange(word_rows, dtype=jnp.int32)[None]).reshape(-1)

    core_order = [core, 1 - core][:cores]
    near = 0.0
    for core_at, block in zip(core_order, word_blocks):
        pick = near_ids[:, None] == ids_of(core_at, -1)[None, :]
        near = near + dot(pick.astype(jnp.bfloat16), block)
    near = slim(near)
    place_ids = jnp.concatenate(
        [ids_of(core_at, 1).reshape(places, word_rows) for core_at in core_order], axis=1
    ).reshape(-1)
    put = slim((place_ids[:, None] == near_ids[None, :]) & owned[None, :])
    def embed(block):
        partial = dot(block, project_weight)
        if enc_count == 2:
            full = partial + wide(shifted(slim(partial), "enc", 1))
        else:
            full = lax.psum(partial, "enc")
        return slim(full * encoder_gain), jnp.sum(full * full, axis=-1)

    vision_rows = joined(my_vision, "vis", 0)
    scaled, power = embed(vision_rows)
    total = head_sum(heads_of(scaled, qkv_weight[1:]))
    power = lax.psum(power, "vis")
    image_kv = slim(total * lax.rsqrt(power / width + EPSILON)[:, None, None])

    live = near[:, 3 * share] > 0
    near = near[:, : 3 * share].reshape(most * CAP, 3, share // DH, DH)
    row_cand = jnp.arange(most * CAP, dtype=jnp.int32) // CAP
    own_allowed = (row_cand[:, None] == row_cand[None, :]) & live[None, :]
    image_kv = image_kv.reshape(rows, 2, share // DH, DH)
    query = near[:, 0]

    def scores_of(keys):
        return jnp.einsum(
            "qhd,khd->hqk", query, keys, preferred_element_type=jnp.float32
        ) * DH ** (-0.5)

    def mixed(weights, values):
        return jnp.einsum(
            "hqk,khd->hqd", slim(weights), values, preferred_element_type=jnp.float32
        )

    image_scores = scores_of(image_kv[:, 0])
    own_scores = jnp.where(own_allowed[None], scores_of(near[:, 1]), FLOOR)
    top = jnp.maximum(
        jnp.max(image_scores, axis=-1, keepdims=True), jnp.max(own_scores, axis=-1, keepdims=True)
    )
    image_weights = jnp.exp(image_scores - top)
    own_weights = jnp.where(own_allowed[None], jnp.exp(own_scores - top), 0.0)
    total = jnp.sum(image_weights, axis=-1, keepdims=True) + jnp.sum(
        own_weights, axis=-1, keepdims=True
    )
    result = (mixed(image_weights, image_kv[:, 1]) + mixed(own_weights, near[:, 2])) / total
    result = slim(result).transpose(1, 0, 2).reshape(most * CAP, share)
    spread_out = slim(dot(put, result)).reshape(places, cores * word_rows, share)
    landed = spread_out[0]
    for step in range(1, places):
        landed = landed + to_place(spread_out[step], step)
    kept = landed[:word_rows]
    attended = kept
    if cores == 2:
        given = landed[word_rows:]
        attended = kept + lax.ppermute(given, "grp", core_swap)
    if shares > 1:
        attended = lax.all_gather(attended, "vis", axis=1, tiled=True)
    partial_words = dot(attended, out_weight).reshape(cand_local, CAP, out_weight.shape[1])
    words_out = lax.psum_scatter(partial_words, "enc", scatter_dimension=1, tiled=True)
    caption_out = slim(words + words_out)
    return (vision_rows[None], caption_out)


def solution(mesh):
    return jax.shard_map(
        on_device,
        mesh=mesh,
        in_specs=(
            P("grp", None, "enc"),
            P("enc"),
            P("enc", ("vis", "grp")),
            P(("vis", "grp"), "enc"),
            P("enc", "vis"),
            P("vis"),
            P(None, "vis", "enc"),
            P("enc", "vis"),
            P("grp", "enc", "vis"),
            P(),
            P("grp"),
        ),
        out_specs=(P("grp", None, "enc"), P("grp", "enc", "vis")),
        check_vma=False,
    )
```

profile of v0, /device:TPU:0, one launch (start us, length us, event | category | flops | bytes accessed | tf_op | source)
XLA Modules:
  0.0 230.0 jit_solution(16447080480115979805)
XLA Ops:
  4.8 3.0 %collective-permute-start = (f32[2,256]{1,0:T(2,128)S(1)}, f32[2,256]{1,0:T(2,128)S(1)}, u32[]{:S(2)}, u32[]{:S(2)}) collective-permute-start(f32[2,256]{1,0:T(2,128)S(1)} %pad_maximum_fusion.1), channel_id=1, source_target_pairs={{0,1},{1,0},{2,3},{3,2},{4,5},{5,4},{6,7},{7,6},{8,9},{9,8},{10,11... | collective-permute-start | bytes 6152 | tf_op jit(solution)/shard_map/ppermute | solution.py:33
  9.4 2.1 collective-permute-done.2
  14.9 17.6 %collective-permute-done.6.mine_ref = bf16[128,3072]{1,0:T(8,128)(2,1)} collective-permute-done((bf16[128,3072]{1,0:T(8,128)(2,1)S(1)}, bf16[128,3072]{1,0:T(8,128)(2,1)}, u32[]{:S(2)}, u32[]{:S(2)}) %collective-permute-start.6) | collective-permute-done | bytes 786464 | tf_op jit(solution)/shard_map/ppermute | solution.py:529
  34.2 4.6 %copy-done = bf16[3,2048,1024]{2,1,0:T(8,128)(2,1)S(1)} copy-done((bf16[3,2048,1024]{2,1,0:T(8,128)(2,1)S(1)}, bf16[3,2048,1024]{2,1,0:T(8,128)(2,1)}, u32[]{:S(2)}) %copy-start) | copy-done | bytes 12582936
  38.8 2.9 %shard_map.122 = (bf16[64,1536]{1,0:T(8,128)(2,1)S(1)}, f32[64,1536]{1,0:T(8,128)S(1)}, f32[8,128]{1,0:T(8,128)S(1)}) custom-call(s32[5]{0:T(128)S(1)} %stack.35.vis_ref.spots_ref, bf16[64,2048]{1,0:T(8,128)(2,1)S(1)} %bitcast.41, bf16[3,2048,1024]{2,1,0:T(8,128)(2,1)S(1)} %copy-done, bf16[128,3072]{1,0:T(8,128)(2,1)S(1)} %get-tuple-element.95.refs_0_.mine_ref, ...), custom_call_target="tpu_custom_call" | custom-call | flops 1024 | bytes 1024 | tf_op jit(solution)/shard_map/pallas_call | solution.py:237
  42.3 4.9 %shard_map.123 = (bf16[256,1536]{1,0:T(8,128)(2,1)S(1)}, f32[8,128]{1,0:T(8,128)S(1)}) custom-call(bf16[128,3072]{1,0:T(8,128)(2,1)S(1)} %get-tuple-element.95.refs_0_.mine_ref, bf16[128,3072]{1,0:T(8,128)(2,1)S(1)} %get-tuple-element.94.theirs_ref, bf16[3072,768]{1,0:T(8,128)(2,1)S(1)} %bitcast.36, bf16[3072,768]{1,0:T(8,128)(2,1)} %collective-permute-done.1.refs_1_, ...), custom_call_target="tpu_custom_call" | custom-call | flops 1024 | bytes 1024 | tf_op jit(solution)/shard_map/pallas_call | solution.py:99
  47.8 5.2 %collective-permute-done.10.value_ref = bf16[128,3072]{1,0:T(8,128)(2,1)S(1)} collective-permute-done((bf16[128,3072]{1,0:T(8,128)(2,1)}, bf16[128,3072]{1,0:T(8,128)(2,1)S(1)}, u32[]{:S(2)}, u32[]{:S(2)}) %collective-permute-start.10) | collective-permute-done | bytes 786464 | tf_op jit(solution)/shard_map/ppermute | solution.py:529
  56.8 5.5 %shard_map.125 = (bf16[256,1536]{1,0:T(8,128)(2,1)S(1)}, f32[8,128]{1,0:T(8,128)S(1)}) custom-call(bf16[128,3072]{1,0:T(8,128)(2,1)} %collective-permute-done.6.mine_ref, bf16[128,3072]{1,0:T(8,128)(2,1)S(1)} %collective-permute-done.7.theirs_ref, bf16[3072,768]{1,0:T(8,128)(2,1)S(1)} %bitcast.36, bf16[3072,768]{1,0:T(8,128)(2,1)} %collective-permute-done.1.refs_1_, ...), custom_call_target="tpu_custom_call" | custom-call | flops 1024 | bytes 1024 | tf_op jit(solution)/shard_map/pallas_call | solution.py:99
  62.9 3.9 %collective-permute-done.4.other_ref = bf16[256,1536]{1,0:T(8,128)(2,1)S(1)} collective-permute-done((bf16[256,1536]{1,0:T(8,128)(2,1)S(1)}, bf16[256,1536]{1,0:T(8,128)(2,1)S(1)}, u32[]{:S(2)}, u32[]{:S(2)}) %collective-permute-start.4) | collective-permute-done | bytes 786464 | tf_op jit(solution)/shard_map/ppermute | solution.py:33
  66.8 5.0 %shard_map.126 = (bf16[128,3072]{1,0:T(8,128)(2,1)S(1)}, bf16[128,3072]{1,0:T(8,128)(2,1)S(1)}, f32[8,128]{1,0:T(8,128)S(1)}) custom-call(bf16[256,1536]{1,0:T(8,128)(2,1)S(1)} %get-tuple-element.49.own_ref, bf16[256,1536]{1,0:T(8,128)(2,1)S(1)} %collective-permute-done.4.other_ref, bf16[768,3072]{1,0:T(8,128)(2,1)S(1)} %bitcast.34, ...), custom_call_target="tpu_custom_call" | custom-call | flops 1024 | bytes 1024 | tf_op jit(solution)/shard_map/pallas_call | solution.py:150
  75.4 5.0 %shard_map.129 = (bf16[256,1536]{1,0:T(8,128)(2,1)S(1)}, f32[8,128]{1,0:T(8,128)S(1)}) custom-call(bf16[128,3072]{1,0:T(8,128)(2,1)S(1)} %shard_map.127.mine_ref, bf16[128,3072]{1,0:T(8,128)(2,1)S(1)} %collective-permute-done.14.theirs_ref, bf16[3072,768]{1,0:T(8,128)(2,1)S(1)} %bitcast.36, bf16[3072,768]{1,0:T(8,128)(2,1)} %collective-permute-done.1.refs_1_, ...), custom_call_target="tpu_custom_call" | custom-call | flops 1024 | bytes 1024 | tf_op jit(solution)/shard_map/pallas_call | solution.py:99
  82.9 5.1 %shard_map.130 = (bf16[128,3072]{1,0:T(8,128)(2,1)S(1)}, bf16[128,3072]{1,0:T(8,128)(2,1)S(1)}, f32[8,128]{1,0:T(8,128)S(1)}) custom-call(bf16[256,1536]{1,0:T(8,128)(2,1)S(1)} %get-tuple-element.57.own_ref, bf16[256,1536]{1,0:T(8,128)(2,1)S(1)} %collective-permute-done.13.other_ref, bf16[768,3072]{1,0:T(8,128)(2,1)S(1)} %bitcast.34, ...), custom_call_target="tpu_custom_call" | custom-call | flops 1024 | bytes 1024 | tf_op jit(solution)/shard_map/pallas_call | solution.py:150
  87.9 2.5 %collective-permute-start.18 = (bf16[128,3072]{1,0:T(8,128)(2,1)S(1)}, bf16[128,3072]{1,0:T(8,128)(2,1)S(1)}, u32[]{:S(2)}, u32[]{:S(2)}) collective-permute-start(bf16[128,3072]{1,0:T(8,128)(2,1)S(1)} %get-tuple-element.62), channel_id=1, source_target_pairs={{0,16},{16,0},{1,17},{17,1},{2,18},{18,2},{3,19},{19,3},{4,20},{20... | collective-permute-start | bytes 2359304 | tf_op jit(solution)/shard_map/ppermute | solution.py:33
  90.4 2.1 collective-permute-start.16
  92.5 6.4 %collective-permute-done.16.refs_3_.refs_2_ = bf16[64,1664]{1,0:T(8,128)(2,1)S(1)} collective-permute-done((bf16[64,1664]{1,0:T(8,128)(2,1)S(1)}, bf16[64,1664]{1,0:T(8,128)(2,1)S(1)}, u32[]{:S(2)}, u32[]{:S(2)}) %collective-permute-start.16) | collective-permute-done | bytes 213024 | tf_op jit(solution)/shard_map/ppermute | solution.py:529
  98.9 5.0 %shard_map.131 = (bf16[256,1536]{1,0:T(8,128)(2,1)S(1)}, f32[8,128]{1,0:T(8,128)S(1)}) custom-call(bf16[128,3072]{1,0:T(8,128)(2,1)S(1)} %shard_map.128.refs_3_.mine_ref, bf16[128,3072]{1,0:T(8,128)(2,1)S(1)} %collective-permute-done.12.theirs_ref, bf16[3072,768]{1,0:T(8,128)(2,1)S(1)} %bitcast.36, bf16[3072,768]{1,0:T(8,128)(2,1)} %collective-permute-done.1.refs_1_, ...), custom_call_target="tpu_custom_call" | custom-call | flops 1024 | bytes 1024 | tf_op jit(solution)/shard_map/pallas_call | solution.py:99
  106.6 5.1 %shard_map.132 = (bf16[128,3072]{1,0:T(8,128)(2,1)S(1)}, bf16[128,3072]{1,0:T(8,128)(2,1)S(1)}, f32[8,128]{1,0:T(8,128)S(1)}) custom-call(bf16[256,1536]{1,0:T(8,128)(2,1)S(1)} %get-tuple-element.63.own_ref, bf16[256,1536]{1,0:T(8,128)(2,1)S(1)} %collective-permute-done.19.other_ref, bf16[768,3072]{1,0:T(8,128)(2,1)S(1)} %bitcast.34, ...), custom_call_target="tpu_custom_call" | custom-call | flops 1024 | bytes 1024 | tf_op jit(solution)/shard_map/pallas_call | solution.py:150
  113.7 2.3 collective-permute-done.17.other_ref
  116.0 5.2 %shard_map.134 = (bf16[128,3072]{1,0:T(8,128)(2,1)S(1)}, bf16[128,3072]{1,0:T(8,128)(2,1)S(1)}, f32[8,128]{1,0:T(8,128)S(1)}) custom-call(bf16[256,1536]{1,0:T(8,128)(2,1)S(1)} %get-tuple-element.60.own_ref, bf16[256,1536]{1,0:T(8,128)(2,1)S(1)} %collective-permute-done.17.other_ref, bf16[768,3072]{1,0:T(8,128)(2,1)S(1)} %bitcast.34, ...), custom_call_target="tpu_custom_call" | custom-call | flops 1024 | bytes 1024 | tf_op jit(solution)/shard_map/pallas_call | solution.py:150
  122.7 8.2 %collective-permute-done.22.refs_1_ = bf16[128,3072]{1,0:T(8,128)(2,1)S(1)} collective-permute-done((bf16[128,3072]{1,0:T(8,128)(2,1)S(1)}, bf16[128,3072]{1,0:T(8,128)(2,1)S(1)}, u32[]{:S(2)}, u32[]{:S(2)}) %collective-permute-start.22) | collective-permute-done | bytes 786464 | tf_op jit(solution)/shard_map/ppermute | solution.py:33
  134.3 7.8 %collective-permute-done.21.refs_1_ = bf16[128,3072]{1,0:T(8,128)(2,1)S(1)} collective-permute-done((bf16[128,3072]{1,0:T(8,128)(2,1)S(1)}, bf16[128,3072]{1,0:T(8,128)(2,1)S(1)}, u32[]{:S(2)}, u32[]{:S(2)}) %collective-permute-start.21) | collective-permute-done | bytes 786464 | tf_op jit(solution)/shard_map/ppermute | solution.py:33
  142.1 11.5 %collective-permute-done.24.refs_2_ = bf16[128,3072]{1,0:T(8,128)(2,1)S(1)} collective-permute-done((bf16[128,3072]{1,0:T(8,128)(2,1)S(1)}, bf16[128,3072]{1,0:T(8,128)(2,1)S(1)}, u32[]{:S(2)}, u32[]{:S(2)}) %collective-permute-start.24) | collective-permute-done | bytes 786464 | tf_op jit(solution)/shard_map/ppermute | solution.py:529
  156.2 11.5 %collective-permute-done.25.refs_3_ = bf16[128,3072]{1,0:T(8,128)(2,1)S(1)} collective-permute-done((bf16[128,3072]{1,0:T(8,128)(2,1)S(1)}, bf16[128,3072]{1,0:T(8,128)(2,1)S(1)}, u32[]{:S(2)}, u32[]{:S(2)}) %collective-permute-start.25) | collective-permute-done | bytes 786464 | tf_op jit(solution)/shard_map/ppermute | solution.py:529
  173.3 10.6 %collective-permute-done.27.rows_ref = bf16[128,3072]{1,0:T(8,128)(2,1)S(1)} collective-permute-done((bf16[128,3072]{1,0:T(8,128)(2,1)S(1)}, bf16[128,3072]{1,0:T(8,128)(2,1)S(1)}, u32[]{:S(2)}, u32[]{:S(2)}) %collective-permute-start.27) | collective-permute-done | bytes 786464 | tf_op jit(solution)/shard_map/ppermute | solution.py:33
  188.3 2.0 collective-permute-start.31
  190.4 4.6 %collective-permute-done.29.other_ref = bf16[128,2048]{1,0:T(8,128)(2,1)S(1)} collective-permute-done((bf16[128,2048]{1,0:T(8,128)(2,1)S(1)}, bf16[128,2048]{1,0:T(8,128)(2,1)S(1)}, u32[]{:S(2)}, u32[]{:S(2)}) %collective-permute-start.29) | collective-permute-done | bytes 524320 | tf_op jit(solution)/shard_map/ppermute | solution.py:33
  197.9 5.8 %collective-permute-done.30.refs_1_ = bf16[128,1152]{1,0:T(8,128)(2,1)S(1)} collective-permute-done((bf16[128,1152]{1,0:T(8,128)(2,1)S(1)}, bf16[128,1152]{1,0:T(8,128)(2,1)S(1)}, u32[]{:S(2)}, u32[]{:S(2)}) %collective-permute-start.30) | collective-permute-done | bytes 294944 | tf_op jit(solution)/shard_map/ppermute | solution.py:33
  205.8 3.7 %collective-permute-start.34 = (bf16[128,512]{1,0:T(8,128)(2,1)S(1)}, bf16[128,512]{1,0:T(8,128)(2,1)S(1)}, u32[]{:S(2)}, u32[]{:S(2)}) collective-permute-start(bf16[128,512]{1,0:T(8,128)(2,1)S(1)} %get-tuple-element.89), channel_id=1, source_target_pairs={{0,12},{2,14},{4,0},{6,2},{8,4},{10,6},{12,8},{14,10},{1,13},{3,15... | collective-permute-start | bytes 393224 | tf_op jit(solution)/shard_map/ppermute | solution.py:529
  209.5 3.1 %collective-permute-done.32.refs_1_ = bf16[128,512]{1,0:T(8,128)(2,1)S(1)} collective-permute-done((bf16[128,512]{1,0:T(8,128)(2,1)S(1)}, bf16[128,512]{1,0:T(8,128)(2,1)S(1)}, u32[]{:S(2)}, u32[]{:S(2)}) %collective-permute-start.32) | collective-permute-done | bytes 131104 | tf_op jit(solution)/shard_map/ppermute | solution.py:529
  216.4 3.1 %collective-permute-done.36.vis_ref = bf16[64,512]{1,0:T(8,128)(2,1)S(1)} collective-permute-done((bf16[64,512]{1,0:T(8,128)(2,1)S(1)}, bf16[64,512]{1,0:T(8,128)(2,1)S(1)}, u32[]{:S(2)}, u32[]{:S(2)}) %collective-permute-start.36) | collective-permute-done | bytes 65568 | tf_op jit(solution)/shard_map/ppermute | solution.py:33
  220.0 2.2 copy-done.1
  226.4 2.9 %collective-permute-done.38 = bf16[32,2048]{1,0:T(8,128)(2,1)S(1)} collective-permute-done((bf16[32,2048]{1,0:T(8,128)(2,1)S(1)}, bf16[32,2048]{1,0:T(8,128)(2,1)S(1)}, u32[]{:S(2)}, u32[]{:S(2)}) %collective-permute-start.38) | collective-permute-done | bytes 131104 | tf_op jit(solution)/shard_map/ppermute | solution.py:33
  (130 shorter events, 58.5 us)
Async XLA Ops:
  0.7 41.6 %collective-permute-start.1 = (bf16[3072,768]{1,0:T(8,128)(2,1)}, bf16[3072,768]{1,0:T(8,128)(2,1)}, u32[]{:S(2)}, u32[]{:S(2)}) collective-permute-start(bf16[3072,768]{1,0:T(8,128)(2,1)} %refs_0_.13), channel_id=1, source_target_pairs={{0,2},{2,0},{4,6},{6,4},{8,10},{10,8},{12,14},{14,12},{1,3},{3,1},... | collective-permute-start | bytes 14155784 | tf_op jit(solution)/shard_map/ppermute | solution.py:522
  1.2 55.6 %collective-permute-start.5 = (bf16[768,3072]{1,0:T(8,128)(2,1)}, bf16[768,3072]{1,0:T(8,128)(2,1)}, u32[]{:S(2)}, u32[]{:S(2)}) collective-permute-start(bf16[768,3072]{1,0:T(8,128)(2,1)} %refs_0_.15), channel_id=1, source_target_pairs={{0,2},{2,0},{4,6},{6,4},{8,10},{10,8},{12,14},{14,12},{1,3},{3,1},... | collective-permute-start | bytes 14155784 | tf_op jit(solution)/shard_map/ppermute | solution.py:523
  12.4 20.1 %collective-permute-start.6 = (bf16[128,3072]{1,0:T(8,128)(2,1)S(1)}, bf16[128,3072]{1,0:T(8,128)(2,1)}, u32[]{:S(2)}, u32[]{:S(2)}) collective-permute-start(bf16[128,3072]{1,0:T(8,128)(2,1)S(1)} %get-tuple-element.95.refs_0_.mine_ref), channel_id=1, source_target_pairs={{0,4},{2,6},{4,8},{6,10},{8,12},{10,14},{12,0},{14,2},{1,5},{3,7},... | collective-permute-start | bytes 2359304 | tf_op jit(solution)/shard_map/ppermute | solution.py:529
  14.1 19.9 %collective-permute-start.3 = (bf16[4,8,2048]{2,1,0:T(8,128)(2,1)S(1)}, bf16[4,8,2048]{2,1,0:T(8,128)(2,1)S(1)}, u32[]{:S(2)}, u32[]{:S(2)}) collective-permute-start(bf16[4,8,2048]{2,1,0:T(8,128)(2,1)S(1)} %fusion.8), channel_id=1, source_target_pairs={{0,1},{1,0},{2,3},{3,2},{4,5},{5,4},{6,7},{7,6},{8,9},{9,8},{10,11... | collective-permute-start | bytes 393224 | tf_op jit(solution)/shard_map/ppermute | solution.py:33
  32.5 24.2 %collective-permute-start.7 = (bf16[128,3072]{1,0:T(8,128)(2,1)}, bf16[128,3072]{1,0:T(8,128)(2,1)S(1)}, u32[]{:S(2)}, u32[]{:S(2)}) collective-permute-start(bf16[128,3072]{1,0:T(8,128)(2,1)} %collective-permute-done.6.mine_ref), channel_id=1, source_target_pairs={{0,16},{16,0},{1,17},{17,1},{2,18},{18,2},{3,19},{19,3},{4,20},{20... | collective-permute-start | bytes 2359304 | tf_op jit(solution)/shard_map/ppermute | solution.py:33
  34.0 19.0 %collective-permute-start.10 = (bf16[128,3072]{1,0:T(8,128)(2,1)}, bf16[128,3072]{1,0:T(8,128)(2,1)S(1)}, u32[]{:S(2)}, u32[]{:S(2)}) collective-permute-start(bf16[128,3072]{1,0:T(8,128)(2,1)} %collective-permute-done.6.mine_ref), channel_id=1, source_target_pairs={{0,4},{2,6},{4,8},{6,10},{8,12},{10,14},{12,0},{14,2},{1,5},{3,7},... | collective-permute-start | bytes 2359304 | tf_op jit(solution)/shard_map/ppermute | solution.py:529
  41.6 13.0 %collective-permute-start.8 = (bf16[64,1536]{1,0:T(8,128)(2,1)S(1)}, bf16[64,1536]{1,0:T(8,128)(2,1)S(1)}, u32[]{:S(2)}, u32[]{:S(2)}) collective-permute-start(bf16[64,1536]{1,0:T(8,128)(2,1)S(1)} %get-tuple-element.52), channel_id=1, source_target_pairs={{0,16},{16,0},{1,17},{17,1},{2,18},{18,2},{3,19},{19,3},{4,20},{20... | collective-permute-start | bytes 589832 | tf_op jit(solution)/shard_map/ppermute | solution.py:33
  47.2 19.6 %collective-permute-start.4 = (bf16[256,1536]{1,0:T(8,128)(2,1)S(1)}, bf16[256,1536]{1,0:T(8,128)(2,1)S(1)}, u32[]{:S(2)}, u32[]{:S(2)}) collective-permute-start(bf16[256,1536]{1,0:T(8,128)(2,1)S(1)} %get-tuple-element.49.own_ref), channel_id=1, source_target_pairs={{0,1},{1,0},{2,3},{3,2},{4,5},{5,4},{6,7},{7,6},{8,9},{9,8},{10,11... | collective-permute-start | bytes 2359304 | tf_op jit(solution)/shard_map/ppermute | solution.py:33
  53.0 20.1 %collective-permute-start.11 = (bf16[128,3072]{1,0:T(8,128)(2,1)S(1)}, bf16[128,3072]{1,0:T(8,128)(2,1)S(1)}, u32[]{:S(2)}, u32[]{:S(2)}) collective-permute-start(bf16[128,3072]{1,0:T(8,128)(2,1)S(1)} %shard_map.127.mine_ref), channel_id=1, source_target_pairs={{0,4},{2,6},{4,8},{6,10},{8,12},{10,14},{12,0},{14,2},{1,5},{3,7},... | collective-permute-start | bytes 2359304 | tf_op jit(solution)/shard_map/ppermute | solution.py:529
  54.7 20.7 %collective-permute-start.14 = (bf16[128,3072]{1,0:T(8,128)(2,1)S(1)}, bf16[128,3072]{1,0:T(8,128)(2,1)S(1)}, u32[]{:S(2)}, u32[]{:S(2)}) collective-permute-start(bf16[128,3072]{1,0:T(8,128)(2,1)S(1)} %shard_map.127.mine_ref), channel_id=1, source_target_pairs={{0,16},{16,0},{1,17},{17,1},{2,18},{18,2},{3,19},{19,3},{4,20},{20... | collective-permute-start | bytes 2359304 | tf_op jit(solution)/shard_map/ppermute | solution.py:33
  62.3 20.6 %collective-permute-start.13 = (bf16[256,1536]{1,0:T(8,128)(2,1)S(1)}, bf16[256,1536]{1,0:T(8,128)(2,1)S(1)}, u32[]{:S(2)}, u32[]{:S(2)}) collective-permute-start(bf16[256,1536]{1,0:T(8,128)(2,1)S(1)} %get-tuple-element.57.own_ref), channel_id=1, source_target_pairs={{0,1},{1,0},{2,3},{3,2},{4,5},{5,4},{6,7},{7,6},{8,9},{9,8},{10,11... | collective-permute-start | bytes 2359304 | tf_op jit(solution)/shard_map/ppermute | solution.py:33
  62.8 12.5 %collective-permute-start.15 = (bf16[64,1664]{1,0:T(8,128)(2,1)S(1)}, bf16[64,1664]{1,0:T(8,128)(2,1)S(1)}, u32[]{:S(2)}, u32[]{:S(2)}) collective-permute-start(bf16[64,1664]{1,0:T(8,128)(2,1)S(1)} %shard_map.124.refs_4_.refs_0_), channel_id=1, source_target_pairs={{0,4},{2,6},{4,8},{6,10},{8,12},{10,14},{12,0},{14,2},{1,5},{3,7},... | collective-permute-start | bytes 638984 | tf_op jit(solution)/shard_map/ppermute | solution.py:529
  73.1 25.8 %collective-permute-start.12 = (bf16[128,3072]{1,0:T(8,128)(2,1)S(1)}, bf16[128,3072]{1,0:T(8,128)(2,1)S(1)}, u32[]{:S(2)}, u32[]{:S(2)}) collective-permute-start(bf16[128,3072]{1,0:T(8,128)(2,1)S(1)} %shard_map.128.refs_3_.mine_ref), channel_id=1, source_target_pairs={{0,16},{16,0},{1,17},{17,1},{2,18},{18,2},{3,19},{19,3},{4,20},{20... | collective-permute-start | bytes 2359304 | tf_op jit(solution)/shard_map/ppermute | solution.py:33
  80.4 26.2 %collective-permute-start.19 = (bf16[256,1536]{1,0:T(8,128)(2,1)S(1)}, bf16[256,1536]{1,0:T(8,128)(2,1)S(1)}, u32[]{:S(2)}, u32[]{:S(2)}) collective-permute-start(bf16[256,1536]{1,0:T(8,128)(2,1)S(1)} %get-tuple-element.63.own_ref), channel_id=1, source_target_pairs={{0,1},{1,0},{2,3},{3,2},{4,5},{5,4},{6,7},{7,6},{8,9},{9,8},{10,11... | collective-permute-start | bytes 2359304 | tf_op jit(solution)/shard_map/ppermute | solution.py:33
  87.9 25.3 %collective-permute-start.18 = (bf16[128,3072]{1,0:T(8,128)(2,1)S(1)}, bf16[128,3072]{1,0:T(8,128)(2,1)S(1)}, u32[]{:S(2)}, u32[]{:S(2)}) collective-permute-start(bf16[128,3072]{1,0:T(8,128)(2,1)S(1)} %get-tuple-element.62), channel_id=1, source_target_pairs={{0,16},{16,0},{1,17},{17,1},{2,18},{18,2},{3,19},{19,3},{4,20},{20... | collective-permute-start | bytes 2359304 | tf_op jit(solution)/shard_map/ppermute | solution.py:33
  90.4 8.5 %collective-permute-start.16 = (bf16[64,1664]{1,0:T(8,128)(2,1)S(1)}, bf16[64,1664]{1,0:T(8,128)(2,1)S(1)}, u32[]{:S(2)}, u32[]{:S(2)}) collective-permute-start(bf16[64,1664]{1,0:T(8,128)(2,1)S(1)} %collective-permute-done.15.refs_4_.refs_1_), channel_id=1, source_target_pairs={{0,4},{2,6},{4,8},{6,10},{8,12},{10,14},{12,0},{14,2},{1,5},{3,7},... | collective-permute-start | bytes 638984 | tf_op jit(solution)/shard_map/ppermute | solution.py:529
  98.9 7.6 %collective-permute-start.20 = (bf16[64,1664]{1,0:T(8,128)(2,1)S(1)}, bf16[64,1664]{1,0:T(8,128)(2,1)S(1)}, u32[]{:S(2)}, u32[]{:S(2)}) collective-permute-start(bf16[64,1664]{1,0:T(8,128)(2,1)S(1)} %collective-permute-done.16.refs_3_.refs_2_), channel_id=1, source_target_pairs={{0,4},{2,6},{4,8},{6,10},{8,12},{10,14},{12,0},{14,2},{1,5},{3,7},... | collective-permute-start | bytes 638984 | tf_op jit(solution)/shard_map/ppermute | solution.py:529
  103.9 12.1 %collective-permute-start.17 = (bf16[256,1536]{1,0:T(8,128)(2,1)S(1)}, bf16[256,1536]{1,0:T(8,128)(2,1)S(1)}, u32[]{:S(2)}, u32[]{:S(2)}) collective-permute-start(bf16[256,1536]{1,0:T(8,128)(2,1)S(1)} %get-tuple-element.60.own_ref), channel_id=1, source_target_pairs={{0,1},{1,0},{2,3},{3,2},{4,5},{5,4},{6,7},{7,6},{8,9},{9,8},{10,11... | collective-permute-start | bytes 2359304 | tf_op jit(solution)/shard_map/ppermute | solution.py:33
  111.6 19.3 %collective-permute-start.22 = (bf16[128,3072]{1,0:T(8,128)(2,1)S(1)}, bf16[128,3072]{1,0:T(8,128)(2,1)S(1)}, u32[]{:S(2)}, u32[]{:S(2)}) collective-permute-start(bf16[128,3072]{1,0:T(8,128)(2,1)S(1)} %get-tuple-element.70), channel_id=1, source_target_pairs={{0,16},{16,0},{1,17},{17,1},{2,18},{18,2},{3,19},{19,3},{4,20},{20... | collective-permute-start | bytes 2359304 | tf_op jit(solution)/shard_map/ppermute | solution.py:33
  113.4 19.5 %collective-permute-start.23 = (bf16[128,3072]{1,0:T(8,128)(2,1)S(1)}, bf16[128,3072]{1,0:T(8,128)(2,1)S(1)}, u32[]{:S(2)}, u32[]{:S(2)}) collective-permute-start(bf16[128,3072]{1,0:T(8,128)(2,1)S(1)} %get-tuple-element.71), channel_id=1, source_target_pairs={{0,4},{2,6},{4,8},{6,10},{8,12},{10,14},{12,0},{14,2},{1,5},{3,7},... | collective-permute-start | bytes 2359304 | tf_op jit(solution)/shard_map/ppermute | solution.py:529
  121.2 20.9 %collective-permute-start.21 = (bf16[128,3072]{1,0:T(8,128)(2,1)S(1)}, bf16[128,3072]{1,0:T(8,128)(2,1)S(1)}, u32[]{:S(2)}, u32[]{:S(2)}) collective-permute-start(bf16[128,3072]{1,0:T(8,128)(2,1)S(1)} %get-tuple-element.68), channel_id=1, source_target_pairs={{0,16},{16,0},{1,17},{17,1},{2,18},{18,2},{3,19},{19,3},{4,20},{20... | collective-permute-start | bytes 2359304 | tf_op jit(solution)/shard_map/ppermute | solution.py:33
  133.2 20.4 %collective-permute-start.24 = (bf16[128,3072]{1,0:T(8,128)(2,1)S(1)}, bf16[128,3072]{1,0:T(8,128)(2,1)S(1)}, u32[]{:S(2)}, u32[]{:S(2)}) collective-permute-start(bf16[128,3072]{1,0:T(8,128)(2,1)S(1)} %get-tuple-element.73), channel_id=1, source_target_pairs={{0,4},{2,6},{4,8},{6,10},{8,12},{10,14},{12,0},{14,2},{1,5},{3,7},... | collective-permute-start | bytes 2359304 | tf_op jit(solution)/shard_map/ppermute | solution.py:529
  133.4 20.6 %collective-permute-start.26 = (bf16[256,1664]{1,0:T(8,128)(2,1)S(1)}, bf16[256,1664]{1,0:T(8,128)(2,1)S(1)}, u32[]{:S(2)}, u32[]{:S(2)}) collective-permute-start(bf16[256,1664]{1,0:T(8,128)(2,1)S(1)} %shard_map.137.own_ref), channel_id=1, source_target_pairs={{0,2},{2,0},{4,6},{6,4},{8,10},{10,8},{12,14},{14,12},{1,3},{3,1},... | collective-permute-start | bytes 2555912 | tf_op jit(solution)/shard_map/ppermute | solution.py:656
  133.4 22.8 %collective-permute-start.9 = (bf16[128,3072]{1,0:T(8,128)(2,1)S(1)}, bf16[128,3072]{1,0:T(8,128)(2,1)S(1)}, u32[]{:S(2)}, u32[]{:S(2)}) collective-permute-start(bf16[128,3072]{1,0:T(8,128)(2,1)S(1)} %get-tuple-element.55), channel_id=1, source_target_pairs={{0,16},{16,0},{1,17},{17,1},{2,18},{18,2},{3,19},{19,3},{4,20},{20... | collective-permute-start | bytes 2359304 | tf_op jit(solution)/shard_map/ppermute | solution.py:33
  153.9 13.8 %collective-permute-start.25 = (bf16[128,3072]{1,0:T(8,128)(2,1)S(1)}, bf16[128,3072]{1,0:T(8,128)(2,1)S(1)}, u32[]{:S(2)}, u32[]{:S(2)}) collective-permute-start(bf16[128,3072]{1,0:T(8,128)(2,1)S(1)} %get-tuple-element.75), channel_id=1, source_target_pairs={{0,4},{2,6},{4,8},{6,10},{8,12},{10,14},{12,0},{14,2},{1,5},{3,7},... | collective-permute-start | bytes 2359304 | tf_op jit(solution)/shard_map/ppermute | solution.py:529
  168.8 15.2 %collective-permute-start.27 = (bf16[128,3072]{1,0:T(8,128)(2,1)S(1)}, bf16[128,3072]{1,0:T(8,128)(2,1)S(1)}, u32[]{:S(2)}, u32[]{:S(2)}) collective-permute-start(bf16[128,3072]{1,0:T(8,128)(2,1)S(1)} %get-tuple-element.78.rows_ref), channel_id=1, source_target_pairs={{0,16},{16,0},{1,17},{17,1},{2,18},{18,2},{3,19},{19,3},{4,20},{20... | collective-permute-start | bytes 2359304 | tf_op jit(solution)/shard_map/ppermute | solution.py:33
  171.6 14.8 %collective-permute-start.28 = (bf16[128,2048]{1,0:T(8,128)(2,1)S(1)}, bf16[128,2048]{1,0:T(8,128)(2,1)S(1)}, u32[]{:S(2)}, u32[]{:S(2)}) collective-permute-start(bf16[128,2048]{1,0:T(8,128)(2,1)S(1)} %shard_map.140.own_ref), channel_id=1, source_target_pairs={{0,1},{1,0},{2,3},{3,2},{4,5},{5,4},{6,7},{7,6},{8,9},{9,8},{10,11... | collective-permute-start | bytes 1572872 | tf_op jit(solution)/shard_map/ppermute | solution.py:33
  185.8 9.2 %collective-permute-start.29 = (bf16[128,2048]{1,0:T(8,128)(2,1)S(1)}, bf16[128,2048]{1,0:T(8,128)(2,1)S(1)}, u32[]{:S(2)}, u32[]{:S(2)}) collective-permute-start(bf16[128,2048]{1,0:T(8,128)(2,1)S(1)} %shard_map.142.own_ref), channel_id=1, source_target_pairs={{0,1},{1,0},{2,3},{3,2},{4,5},{5,4},{6,7},{7,6},{8,9},{9,8},{10,11... | collective-permute-start | bytes 1572872 | tf_op jit(solution)/shard_map/ppermute | solution.py:33
  188.3 9.6 %collective-permute-start.31 = (bf16[128,1152]{1,0:T(8,128)(2,1)S(1)}, bf16[128,1152]{1,0:T(8,128)(2,1)S(1)}, u32[]{:S(2)}, u32[]{:S(2)}) collective-permute-start(bf16[128,1152]{1,0:T(8,128)(2,1)S(1)} %get-tuple-element.84), channel_id=1, source_target_pairs={{0,16},{16,0},{1,17},{17,1},{2,18},{18,2},{3,19},{19,3},{4,20},{20... | collective-permute-start | bytes 884744 | tf_op jit(solution)/shard_map/ppermute | solution.py:33
  205.6 7.0 %collective-permute-start.32 = (bf16[128,512]{1,0:T(8,128)(2,1)S(1)}, bf16[128,512]{1,0:T(8,128)(2,1)S(1)}, u32[]{:S(2)}, u32[]{:S(2)}) collective-permute-start(bf16[128,512]{1,0:T(8,128)(2,1)S(1)} %get-tuple-element.87), channel_id=1, source_target_pairs={{0,4},{2,6},{4,8},{6,10},{8,12},{10,14},{12,0},{14,2},{1,5},{3,7},... | collective-permute-start | bytes 393224 | tf_op jit(solution)/shard_map/ppermute | solution.py:529
  205.6 8.7 %collective-permute-start.33 = (bf16[128,512]{1,0:T(8,128)(2,1)S(1)}, bf16[128,512]{1,0:T(8,128)(2,1)S(1)}, u32[]{:S(2)}, u32[]{:S(2)}) collective-permute-start(bf16[128,512]{1,0:T(8,128)(2,1)S(1)} %get-tuple-element.88), channel_id=1, source_target_pairs={{0,8},{2,10},{4,12},{6,14},{8,0},{10,2},{12,4},{14,6},{1,9},{3,11}... | collective-permute-start | bytes 393224 | tf_op jit(solution)/shard_map/ppermute | solution.py:529
  205.8 8.6 %collective-permute-start.34 = (bf16[128,512]{1,0:T(8,128)(2,1)S(1)}, bf16[128,512]{1,0:T(8,128)(2,1)S(1)}, u32[]{:S(2)}, u32[]{:S(2)}) collective-permute-start(bf16[128,512]{1,0:T(8,128)(2,1)S(1)} %get-tuple-element.89), channel_id=1, source_target_pairs={{0,12},{2,14},{4,0},{6,2},{8,4},{10,6},{12,8},{14,10},{1,13},{3,15... | collective-permute-start | bytes 393224 | tf_op jit(solution)/shard_map/ppermute | solution.py:529
  (26 other events, 357.2 us)
where the time goes:
time: 230 us
  waiting for transfers between devices  120 us (52%)
  Pallas kernels  57.9 us (25%)
  starting transfers between devices  37.4 us (16%)
  local copies, waits for them, and re-layouts  7.1 us (3%)
  other arithmetic  6.85 us (3%)
    ppermute x12, waiting for transfers between devices, to_place(): lax.ppermute(value, 'grp', [(i, (i + step * cores) % groups) for i in ran...  63.1 us
    ppermute x22, waiting for transfers between devices, shifted(): lax.ppermute(value, axis, [(i, (i + step) % count) for i in range(count)])  56 us
    ppermute x22, starting transfers between devices, shifted(): lax.ppermute(value, axis, [(i, (i + step) % count) for i in range(count)])  27.8 us
    pallas_call x4, Pallas kernels, up_call(): pl.pallas_call(functools.partial(up_kernel, cores), in_specs=[VMEM] * (2...  20.4 us
    pallas_call x4, Pallas kernels, down_call(): pl.pallas_call(functools.partial(down_kernel, cores), in_specs=[VMEM] * (...  20.3 us
    ppermute x12, starting transfers between devices, to_place(): lax.ppermute(value, 'grp', [(i, (i + step * cores) % groups) for i in ran...  8 us
    unnamed x38, local copies, waits for them, and re-layouts  6.85 us
  transfers between devices with their start and end apart: 39, of which 25 were waited for; matrix products, arithmetic and copies ran while one was open for 3% of the time, Pallas kernels for 23%

commit v1 on v0

--- a/solution.py
+++ b/solution.py
@@ -54,7 +54,7 @@
 VMEM = pl.BlockSpec(memory_space=pltpu.VMEM)
 SMEM = pl.BlockSpec(memory_space=pltpu.SMEM)
 LIGHT = pl.CostEstimate(flops=1024, bytes_accessed=1024, transcendentals=0)
-PARAMS = pltpu.CompilerParams(vmem_limit_bytes=20 * 1024 * 1024)
+PARAMS = pltpu.CompilerParams(vmem_limit_bytes=12 * 1024 * 1024)
 
 
 def tile_of(size, most):
@@ -81,7 +81,7 @@
     weights, (out_ref, token_ref, rows_ref) = refs[:cores], refs[-3:]
     half = mine_ref.shape[0]
     units = weights[0].shape[1]
-    tile = tile_of(units, 256)
+    tile = tile_of(units, 768)
     rows_ref[:half] = mine_ref[...]
     rows_ref[half:] = theirs_ref[...]
     token_ref[...] = jnp.zeros(TOKEN, jnp.float32)
@@ -116,7 +116,7 @@
     units, columns = weights[0].shape
     tile = tile_of(units, 256)
     half = kept_ref.shape[0]
-    part = tile_of(columns, 512)
+    part = tile_of(columns, 1536)
     token_ref[...] = jnp.zeros(TOKEN, jnp.float32)
     order = [(core, first) for core in range(cores) for first in range(0, units, tile)]
 
@@ -159,7 +159,8 @@
     )(own, other, *weights, *after)
 
 
-def project_kernel(rows_ref, weight_ref, out_ref):
+def project_kernel(rows_ref, weight_ref, *refs):
+    out_ref = refs[-1]
     columns = weight_ref.shape[1]
     part = tile_of(columns, 512)
     for first in range(0, columns, part):
@@ -168,15 +169,15 @@
         )
 
 
-def project_call(rows, weight):
+def project_call(rows, weight, after):
     return pl.pallas_call(
         project_kernel,
-        in_specs=[VMEM, VMEM],
+        in_specs=[VMEM, VMEM] + [VMEM] * len(after),
         out_specs=VMEM,
         out_shape=jax.ShapeDtypeStruct((rows.shape[0], weight.shape[1]), jnp.bfloat16),
         compiler_params=PARAMS,
         cost_estimate=LIGHT,
-    )(rows, weight)
+    )(rows, weight, *after)
 
 
 def image_kernel(vis_ref, own_ref, other_ref, gain_ref, weight_ref, kept_ref, sent_ref, power_ref):
@@ -588,7 +589,7 @@
 
     def forwarded(step):
         if step < places:
-            here = passed(arrived[step], token[0]) if step > 1 else arrived[step]
+            here = passed(arrived[step], token[0]) if step > 1 and token else arrived[step]
             if step + 1 < places:
                 arrived[step + 1] = to_place(here, 1)
             blocks[step] = halves_of(here, None)
@@ -645,18 +646,18 @@
     forwarded(2)
     messages.append(message_call(caption_lengths, word_kept, word_other, token))
     up(1, down_weights[-1], messages[0])
-    down(0)
     forwarded(3)
     up(2, blocks[places - 1][0], hop())
-    down(1)
-    up(3, hop())
+    down(1, hop())
+    down(0)
+    up(3)
     down(2, hop())
+    back(1)
     word_block = stack_call(messages)
     if cores == 2:
         word_blocks = [word_block, lax.ppermute(word_block, "grp", core_swap)]
     else:
         word_blocks = [word_block]
-    back(1)
     for step in range(4, places):
         forwarded(step)
         up(step)
@@ -676,7 +677,7 @@
         other_vision = shifted(my_vision, "vis", 1)
         pieces = []
         for block in (my_vision, other_vision):
-            partial = project_call(block, project_weight)
+            partial = project_call(block, project_weight, [out_weight])
             full = shifted(partial, "enc", 1)
             pieces.append(image_call(partial, full, encoder_gain, qkv_weight, spots))
         got = [shifted(sent, "vis", 1) for _, sent, _ in pieces]

time: 230 us -> 230 us (level)
  starting transfers between devices: 37.4 us -> 32.9 us
  waiting for transfers between devices: 120 us -> 123 us
    ppermute x22, waiting for transfers between devices: 56 us -> 78.8 us  [shifted(): lax.ppermute(value, axis, [(i, (i + step) % count) for i in range(count)])]
    ppermute x12, waiting for transfers between devices: 63.1 us -> 44.2 us  [to_place(): lax.ppermute(value, 'grp', [(i, (i + step * cores) % groups) for i in ran...]
    ppermute x22, starting transfers between devices: 27.8 us -> 24.5 us  [shifted(): lax.ppermute(value, axis, [(i, (i + step) % count) for i in range(count)])]
    unnamed x38 -> x40, local copies, waits for them, and re-layouts: 6.85 us -> 6.85 us
  transfers between devices with their start and end apart: 39 -> 39, of which waited for: 25 -> 20; matrix products, arithmetic and copies ran while one was open for 3% -> 3% of each run, Pallas kernels for 23% -> 23%
where the time goes in v1:
time: 230 us; the launch traced here: 229 us
  waiting for transfers between devices  123 us (53%)
  Pallas kernels  57.8 us (25%)
  starting transfers between devices  32.9 us (14%)
  local copies, waits for them, and re-layouts  7.1 us (3%)
  other arithmetic  6.84 us (3%)
    ppermute x22, waiting for transfers between devices, shifted(): lax.ppermute(value, axis, [(i, (i + step) % count) for i in range(count)])  78.8 us
    ppermute x12, waiting for transfers between devices, to_place(): lax.ppermute(value, 'grp', [(i, (i + step * cores) % groups) for i in ran...  44.2 us
    ppermute x22, starting transfers between devices, shifted(): lax.ppermute(value, axis, [(i, (i + step) % count) for i in range(count)])  24.5 us
    pallas_call x4, Pallas kernels, up_call(): pl.pallas_call(functools.partial(up_kernel, cores), in_specs=[VMEM] * (2...  20.4 us
    pallas_call x4, Pallas kernels, down_call(): pl.pallas_call(functools.partial(down_kernel, cores), in_specs=[VMEM] * (...  20.3 us
    unnamed x40, local copies, waits for them, and re-layouts  6.85 us
    ppermute x12, starting transfers between devices, to_place(): lax.ppermute(value, 'grp', [(i, (i + step * cores) % groups) for i in ran...  6.32 us
  transfers between devices with their start and end apart: 39, of which 20 were waited for; matrix products, arithmetic and copies ran while one was open for 3% of the time, Pallas kernels for 23%

profile of v1, /device:TPU:0, one launch (start us, length us, event | category | flops | bytes accessed | tf_op | source)
XLA Modules:
  0.0 229.3 jit_solution(5765370366358301199)
XLA Ops:
  4.8 3.0 %collective-permute-start = (f32[2,256]{1,0:T(2,128)S(1)}, f32[2,256]{1,0:T(2,128)S(1)}, u32[]{:S(2)}, u32[]{:S(2)}) collective-permute-start(f32[2,256]{1,0:T(2,128)S(1)} %pad_maximum_fusion.1), channel_id=1, source_target_pairs={{0,1},{1,0},{2,3},{3,2},{4,5},{5,4},{6,7},{7,6},{8,9},{9,8},{10,11... | collective-permute-start | bytes 6152 | tf_op jit(solution)/shard_map/ppermute | solution.py:33
  9.4 2.1 collective-permute-done.2
  14.9 17.6 %collective-permute-done.6.mine_ref = bf16[128,3072]{1,0:T(8,128)(2,1)} collective-permute-done((bf16[128,3072]{1,0:T(8,128)(2,1)S(1)}, bf16[128,3072]{1,0:T(8,128)(2,1)}, u32[]{:S(2)}, u32[]{:S(2)}) %collective-permute-start.6) | collective-permute-done | bytes 786464 | tf_op jit(solution)/shard_map/ppermute | solution.py:530
  34.2 4.6 %copy-done = bf16[3,2048,1024]{2,1,0:T(8,128)(2,1)S(1)} copy-done((bf16[3,2048,1024]{2,1,0:T(8,128)(2,1)S(1)}, bf16[3,2048,1024]{2,1,0:T(8,128)(2,1)}, u32[]{:S(2)}) %copy-start) | copy-done | bytes 12582936
  38.8 2.9 %shard_map.122 = (bf16[64,1536]{1,0:T(8,128)(2,1)S(1)}, f32[64,1536]{1,0:T(8,128)S(1)}, f32[8,128]{1,0:T(8,128)S(1)}) custom-call(s32[5]{0:T(128)S(1)} %stack.35.vis_ref.spots_ref, bf16[64,2048]{1,0:T(8,128)(2,1)S(1)} %bitcast.41, bf16[3,2048,1024]{2,1,0:T(8,128)(2,1)S(1)} %copy-done, bf16[128,3072]{1,0:T(8,128)(2,1)S(1)} %get-tuple-element.95.refs_0_.mine_ref, ...), custom_call_target="tpu_custom_call" | custom-call | flops 1024 | bytes 1024 | tf_op jit(solution)/shard_map/pallas_call | solution.py:238
  42.3 4.9 %shard_map.123 = (bf16[256,1536]{1,0:T(8,128)(2,1)S(1)}, f32[8,128]{1,0:T(8,128)S(1)}) custom-call(bf16[128,3072]{1,0:T(8,128)(2,1)S(1)} %get-tuple-element.95.refs_0_.mine_ref, bf16[128,3072]{1,0:T(8,128)(2,1)S(1)} %get-tuple-element.94.theirs_ref, bf16[3072,768]{1,0:T(8,128)(2,1)S(1)} %bitcast.36, bf16[3072,768]{1,0:T(8,128)(2,1)} %collective-permute-done.1.refs_1_, ...), custom_call_target="tpu_custom_call" | custom-call | flops 1024 | bytes 1024 | tf_op jit(solution)/shard_map/pallas_call | solution.py:99
  47.2 5.8 %collective-permute-done.10.value_ref = bf16[128,3072]{1,0:T(8,128)(2,1)S(1)} collective-permute-done((bf16[128,3072]{1,0:T(8,128)(2,1)}, bf16[128,3072]{1,0:T(8,128)(2,1)S(1)}, u32[]{:S(2)}, u32[]{:S(2)}) %collective-permute-start.10) | collective-permute-done | bytes 786464 | tf_op jit(solution)/shard_map/ppermute | solution.py:530
  53.5 2.6 %collective-permute-done.8.other_ref = bf16[64,1536]{1,0:T(8,128)(2,1)S(1)} collective-permute-done((bf16[64,1536]{1,0:T(8,128)(2,1)S(1)}, bf16[64,1536]{1,0:T(8,128)(2,1)S(1)}, u32[]{:S(2)}, u32[]{:S(2)}) %collective-permute-start.8) | collective-permute-done | bytes 196640 | tf_op jit(solution)/shard_map/ppermute | solution.py:33
  56.7 5.2 %shard_map.125 = (bf16[256,1536]{1,0:T(8,128)(2,1)S(1)}, f32[8,128]{1,0:T(8,128)S(1)}) custom-call(bf16[128,3072]{1,0:T(8,128)(2,1)} %collective-permute-done.6.mine_ref, bf16[128,3072]{1,0:T(8,128)(2,1)S(1)} %collective-permute-done.7.theirs_ref, bf16[3072,768]{1,0:T(8,128)(2,1)S(1)} %bitcast.36, bf16[3072,768]{1,0:T(8,128)(2,1)} %collective-permute-done.1.refs_1_, ...), custom_call_target="tpu_custom_call" | custom-call | flops 1024 | bytes 1024 | tf_op jit(solution)/shard_map/pallas_call | solution.py:99
  62.9 12.4 %collective-permute-done.13.refs_4_.refs_1_ = bf16[64,1664]{1,0:T(8,128)(2,1)S(1)} collective-permute-done((bf16[64,1664]{1,0:T(8,128)(2,1)S(1)}, bf16[64,1664]{1,0:T(8,128)(2,1)S(1)}, u32[]{:S(2)}, u32[]{:S(2)}) %collective-permute-start.13) | collective-permute-done | bytes 213024 | tf_op jit(solution)/shard_map/ppermute | solution.py:530
  76.9 5.3 %shard_map.128 = (bf16[256,1536]{1,0:T(8,128)(2,1)S(1)}, f32[8,128]{1,0:T(8,128)S(1)}) custom-call(bf16[128,3072]{1,0:T(8,128)(2,1)S(1)} %shard_map.126.mine_ref, bf16[128,3072]{1,0:T(8,128)(2,1)S(1)} %collective-permute-done.11.theirs_ref, bf16[3072,768]{1,0:T(8,128)(2,1)S(1)} %bitcast.36, bf16[3072,768]{1,0:T(8,128)(2,1)} %collective-permute-done.1.refs_1_, ...), custom_call_target="tpu_custom_call" | custom-call | flops 1024 | bytes 1024 | tf_op jit(solution)/shard_map/pallas_call | solution.py:99
  83.4 5.1 %shard_map.129 = (bf16[128,3072]{1,0:T(8,128)(2,1)S(1)}, bf16[128,3072]{1,0:T(8,128)(2,1)S(1)}, f32[8,128]{1,0:T(8,128)S(1)}) custom-call(bf16[256,1536]{1,0:T(8,128)(2,1)S(1)} %get-tuple-element.53.own_ref, bf16[256,1536]{1,0:T(8,128)(2,1)S(1)} %collective-permute-done.9.other_ref, bf16[768,3072]{1,0:T(8,128)(2,1)S(1)} %bitcast.34, ...), custom_call_target="tpu_custom_call" | custom-call | flops 1024 | bytes 1024 | tf_op jit(solution)/shard_map/pallas_call | solution.py:150
  89.7 6.2 %collective-permute-done.4.other_ref = bf16[256,1536]{1,0:T(8,128)(2,1)S(1)} collective-permute-done((bf16[256,1536]{1,0:T(8,128)(2,1)S(1)}, bf16[256,1536]{1,0:T(8,128)(2,1)S(1)}, u32[]{:S(2)}, u32[]{:S(2)}) %collective-permute-start.4) | collective-permute-done | bytes 786464 | tf_op jit(solution)/shard_map/ppermute | solution.py:33
  95.9 5.0 %shard_map.130 = (bf16[128,3072]{1,0:T(8,128)(2,1)S(1)}, bf16[128,3072]{1,0:T(8,128)(2,1)S(1)}, f32[8,128]{1,0:T(8,128)S(1)}) custom-call(bf16[256,1536]{1,0:T(8,128)(2,1)S(1)} %get-tuple-element.49.own_ref, bf16[256,1536]{1,0:T(8,128)(2,1)S(1)} %collective-permute-done.4.other_ref, bf16[768,3072]{1,0:T(8,128)(2,1)S(1)} %bitcast.34, ...), custom_call_target="tpu_custom_call" | custom-call | flops 1024 | bytes 1024 | tf_op jit(solution)/shard_map/pallas_call | solution.py:150
  101.0 5.0 %shard_map.131 = (bf16[256,1536]{1,0:T(8,128)(2,1)S(1)}, f32[8,128]{1,0:T(8,128)S(1)}) custom-call(bf16[128,3072]{1,0:T(8,128)(2,1)S(1)} %shard_map.127.refs_3_.mine_ref, bf16[128,3072]{1,0:T(8,128)(2,1)S(1)} %collective-permute-done.16.theirs_ref, bf16[3072,768]{1,0:T(8,128)(2,1)S(1)} %bitcast.36, bf16[3072,768]{1,0:T(8,128)(2,1)} %collective-permute-done.1.refs_1_, ...), custom_call_target="tpu_custom_call" | custom-call | flops 1024 | bytes 1024 | tf_op jit(solution)/shard_map/pallas_call | solution.py:99
  107.4 5.4 %collective-permute-done.19.other_ref = bf16[256,1536]{1,0:T(8,128)(2,1)S(1)} collective-permute-done((bf16[256,1536]{1,0:T(8,128)(2,1)S(1)}, bf16[256,1536]{1,0:T(8,128)(2,1)S(1)}, u32[]{:S(2)}, u32[]{:S(2)}) %collective-permute-start.19) | collective-permute-done | bytes 786464 | tf_op jit(solution)/shard_map/ppermute | solution.py:33
  112.7 5.0 %shard_map.132 = (bf16[128,3072]{1,0:T(8,128)(2,1)S(1)}, bf16[128,3072]{1,0:T(8,128)(2,1)S(1)}, f32[8,128]{1,0:T(8,128)S(1)}) custom-call(bf16[256,1536]{1,0:T(8,128)(2,1)S(1)} %get-tuple-element.63.own_ref, bf16[256,1536]{1,0:T(8,128)(2,1)S(1)} %collective-permute-done.19.other_ref, bf16[768,3072]{1,0:T(8,128)(2,1)S(1)} %bitcast.34, ...), custom_call_target="tpu_custom_call" | custom-call | flops 1024 | bytes 1024 | tf_op jit(solution)/shard_map/pallas_call | solution.py:150
  117.8 2.5 %collective-permute-start.22 = (bf16[128,3072]{1,0:T(8,128)(2,1)S(1)}, bf16[128,3072]{1,0:T(8,128)(2,1)S(1)}, u32[]{:S(2)}, u32[]{:S(2)}) collective-permute-start(bf16[128,3072]{1,0:T(8,128)(2,1)S(1)} %get-tuple-element.70), channel_id=1, source_target_pairs={{0,16},{16,0},{1,17},{17,1},{2,18},{18,2},{3,19},{19,3},{4,20},{20... | collective-permute-start | bytes 2359304 | tf_op jit(solution)/shard_map/ppermute | solution.py:33
  121.2 5.7 %collective-permute-done.17.other_ref = bf16[256,1536]{1,0:T(8,128)(2,1)S(1)} collective-permute-done((bf16[256,1536]{1,0:T(8,128)(2,1)S(1)}, bf16[256,1536]{1,0:T(8,128)(2,1)S(1)}, u32[]{:S(2)}, u32[]{:S(2)}) %collective-permute-start.17) | collective-permute-done | bytes 786464 | tf_op jit(solution)/shard_map/ppermute | solution.py:33
  126.9 5.2 %shard_map.134 = (bf16[128,3072]{1,0:T(8,128)(2,1)S(1)}, bf16[128,3072]{1,0:T(8,128)(2,1)S(1)}, f32[8,128]{1,0:T(8,128)S(1)}) custom-call(bf16[256,1536]{1,0:T(8,128)(2,1)S(1)} %get-tuple-element.60.own_ref, bf16[256,1536]{1,0:T(8,128)(2,1)S(1)} %collective-permute-done.17.other_ref, bf16[768,3072]{1,0:T(8,128)(2,1)S(1)} %bitcast.34, ...), custom_call_target="tpu_custom_call" | custom-call | flops 1024 | bytes 1024 | tf_op jit(solution)/shard_map/pallas_call | solution.py:150
  136.7 15.9 %collective-permute-done.21.refs_1_ = bf16[128,3072]{1,0:T(8,128)(2,1)S(1)} collective-permute-done((bf16[128,3072]{1,0:T(8,128)(2,1)S(1)}, bf16[128,3072]{1,0:T(8,128)(2,1)S(1)}, u32[]{:S(2)}, u32[]{:S(2)}) %collective-permute-start.21) | collective-permute-done | bytes 786464 | tf_op jit(solution)/shard_map/ppermute | solution.py:33
  154.2 11.8 %collective-permute-done.15.refs_2_ = bf16[128,3072]{1,0:T(8,128)(2,1)S(1)} collective-permute-done((bf16[128,3072]{1,0:T(8,128)(2,1)S(1)}, bf16[128,3072]{1,0:T(8,128)(2,1)S(1)}, u32[]{:S(2)}, u32[]{:S(2)}) %collective-permute-start.15) | collective-permute-done | bytes 786464 | tf_op jit(solution)/shard_map/ppermute | solution.py:33
  166.0 2.4 %collective-permute-done.25.refs_3_ = bf16[128,3072]{1,0:T(8,128)(2,1)S(1)} collective-permute-done((bf16[128,3072]{1,0:T(8,128)(2,1)S(1)}, bf16[128,3072]{1,0:T(8,128)(2,1)S(1)}, u32[]{:S(2)}, u32[]{:S(2)}) %collective-permute-start.25) | collective-permute-done | bytes 786464 | tf_op jit(solution)/shard_map/ppermute | solution.py:530
  173.4 9.9 %collective-permute-done.27.rows_ref = bf16[128,3072]{1,0:T(8,128)(2,1)S(1)} collective-permute-done((bf16[128,3072]{1,0:T(8,128)(2,1)S(1)}, bf16[128,3072]{1,0:T(8,128)(2,1)S(1)}, u32[]{:S(2)}, u32[]{:S(2)}) %collective-permute-start.27) | collective-permute-done | bytes 786464 | tf_op jit(solution)/shard_map/ppermute | solution.py:33
  188.3 6.0 %collective-permute-done.29.other_ref = bf16[128,2048]{1,0:T(8,128)(2,1)S(1)} collective-permute-done((bf16[128,2048]{1,0:T(8,128)(2,1)S(1)}, bf16[128,2048]{1,0:T(8,128)(2,1)S(1)}, u32[]{:S(2)}, u32[]{:S(2)}) %collective-permute-start.29) | collective-permute-done | bytes 524320 | tf_op jit(solution)/shard_map/ppermute | solution.py:33
  196.7 6.3 %collective-permute-done.30.refs_1_ = bf16[128,1152]{1,0:T(8,128)(2,1)S(1)} collective-permute-done((bf16[128,1152]{1,0:T(8,128)(2,1)S(1)}, bf16[128,1152]{1,0:T(8,128)(2,1)S(1)}, u32[]{:S(2)}, u32[]{:S(2)}) %collective-permute-start.30) | collective-permute-done | bytes 294944 | tf_op jit(solution)/shard_map/ppermute | solution.py:33
  203.0 1.9 shard_map.144
  206.6 2.2 collective-permute-start.34
  208.7 3.1 %collective-permute-done.32.refs_1_ = bf16[128,512]{1,0:T(8,128)(2,1)S(1)} collective-permute-done((bf16[128,512]{1,0:T(8,128)(2,1)S(1)}, bf16[128,512]{1,0:T(8,128)(2,1)S(1)}, u32[]{:S(2)}, u32[]{:S(2)}) %collective-permute-start.32) | collective-permute-done | bytes 131104 | tf_op jit(solution)/shard_map/ppermute | solution.py:530
  215.7 3.1 %collective-permute-done.36.vis_ref = bf16[64,512]{1,0:T(8,128)(2,1)S(1)} collective-permute-done((bf16[64,512]{1,0:T(8,128)(2,1)S(1)}, bf16[64,512]{1,0:T(8,128)(2,1)S(1)}, u32[]{:S(2)}, u32[]{:S(2)}) %collective-permute-start.36) | collective-permute-done | bytes 65568 | tf_op jit(solution)/shard_map/ppermute | solution.py:33
  219.3 2.2 copy-done.2
  224.9 3.7 %collective-permute-done.38 = bf16[32,2048]{1,0:T(8,128)(2,1)S(1)} collective-permute-done((bf16[32,2048]{1,0:T(8,128)(2,1)S(1)}, bf16[32,2048]{1,0:T(8,128)(2,1)S(1)}, u32[]{:S(2)}, u32[]{:S(2)}) %collective-permute-start.38) | collective-permute-done | bytes 131104 | tf_op jit(solution)/shard_map/ppermute | solution.py:33
  (132 shorter events, 48.0 us)
Async XLA Ops:
  0.7 41.6 %collective-permute-start.1 = (bf16[3072,768]{1,0:T(8,128)(2,1)}, bf16[3072,768]{1,0:T(8,128)(2,1)}, u32[]{:S(2)}, u32[]{:S(2)}) collective-permute-start(bf16[3072,768]{1,0:T(8,128)(2,1)} %refs_0_.15), channel_id=1, source_target_pairs={{0,2},{2,0},{4,6},{6,4},{8,10},{10,8},{12,14},{14,12},{1,3},{3,1},... | collective-permute-start | bytes 14155784 | tf_op jit(solution)/shard_map/ppermute | solution.py:523
  1.2 55.6 %collective-permute-start.5 = (bf16[768,3072]{1,0:T(8,128)(2,1)}, bf16[768,3072]{1,0:T(8,128)(2,1)}, u32[]{:S(2)}, u32[]{:S(2)}) collective-permute-start(bf16[768,3072]{1,0:T(8,128)(2,1)} %refs_0_.17), channel_id=1, source_target_pairs={{0,2},{2,0},{4,6},{6,4},{8,10},{10,8},{12,14},{14,12},{1,3},{3,1},... | collective-permute-start | bytes 14155784 | tf_op jit(solution)/shard_map/ppermute | solution.py:524
  12.4 20.1 %collective-permute-start.6 = (bf16[128,3072]{1,0:T(8,128)(2,1)S(1)}, bf16[128,3072]{1,0:T(8,128)(2,1)}, u32[]{:S(2)}, u32[]{:S(2)}) collective-permute-start(bf16[128,3072]{1,0:T(8,128)(2,1)S(1)} %get-tuple-element.95.refs_0_.mine_ref), channel_id=1, source_target_pairs={{0,4},{2,6},{4,8},{6,10},{8,12},{10,14},{12,0},{14,2},{1,5},{3,7},... | collective-permute-start | bytes 2359304 | tf_op jit(solution)/shard_map/ppermute | solution.py:530
  14.1 19.9 %collective-permute-start.3 = (bf16[4,8,2048]{2,1,0:T(8,128)(2,1)S(1)}, bf16[4,8,2048]{2,1,0:T(8,128)(2,1)S(1)}, u32[]{:S(2)}, u32[]{:S(2)}) collective-permute-start(bf16[4,8,2048]{2,1,0:T(8,128)(2,1)S(1)} %fusion.8), channel_id=1, source_target_pairs={{0,1},{1,0},{2,3},{3,2},{4,5},{5,4},{6,7},{7,6},{8,9},{9,8},{10,11... | collective-permute-start | bytes 393224 | tf_op jit(solution)/shard_map/ppermute | solution.py:33
  32.5 24.2 %collective-permute-start.7 = (bf16[128,3072]{1,0:T(8,128)(2,1)}, bf16[128,3072]{1,0:T(8,128)(2,1)S(1)}, u32[]{:S(2)}, u32[]{:S(2)}) collective-permute-start(bf16[128,3072]{1,0:T(8,128)(2,1)} %collective-permute-done.6.mine_ref), channel_id=1, source_target_pairs={{0,16},{16,0},{1,17},{17,1},{2,18},{18,2},{3,19},{19,3},{4,20},{20... | collective-permute-start | bytes 2359304 | tf_op jit(solution)/shard_map/ppermute | solution.py:33
  34.0 19.0 %collective-permute-start.10 = (bf16[128,3072]{1,0:T(8,128)(2,1)}, bf16[128,3072]{1,0:T(8,128)(2,1)S(1)}, u32[]{:S(2)}, u32[]{:S(2)}) collective-permute-start(bf16[128,3072]{1,0:T(8,128)(2,1)} %collective-permute-done.6.mine_ref), channel_id=1, source_target_pairs={{0,4},{2,6},{4,8},{6,10},{8,12},{10,14},{12,0},{14,2},{1,5},{3,7},... | collective-permute-start | bytes 2359304 | tf_op jit(solution)/shard_map/ppermute | solution.py:530
  41.6 14.5 %collective-permute-start.8 = (bf16[64,1536]{1,0:T(8,128)(2,1)S(1)}, bf16[64,1536]{1,0:T(8,128)(2,1)S(1)}, u32[]{:S(2)}, u32[]{:S(2)}) collective-permute-start(bf16[64,1536]{1,0:T(8,128)(2,1)S(1)} %get-tuple-element.52), channel_id=1, source_target_pairs={{0,16},{16,0},{1,17},{17,1},{2,18},{18,2},{3,19},{19,3},{4,20},{20... | collective-permute-start | bytes 589832 | tf_op jit(solution)/shard_map/ppermute | solution.py:33
  53.0 22.9 %collective-permute-start.12 = (bf16[128,3072]{1,0:T(8,128)(2,1)S(1)}, bf16[128,3072]{1,0:T(8,128)(2,1)S(1)}, u32[]{:S(2)}, u32[]{:S(2)}) collective-permute-start(bf16[128,3072]{1,0:T(8,128)(2,1)S(1)} %shard_map.126.mine_ref), channel_id=1, source_target_pairs={{0,4},{2,6},{4,8},{6,10},{8,12},{10,14},{12,0},{14,2},{1,5},{3,7},... | collective-permute-start | bytes 2359304 | tf_op jit(solution)/shard_map/ppermute | solution.py:530
  53.0 24.0 %collective-permute-start.11 = (bf16[128,3072]{1,0:T(8,128)(2,1)S(1)}, bf16[128,3072]{1,0:T(8,128)(2,1)S(1)}, u32[]{:S(2)}, u32[]{:S(2)}) collective-permute-start(bf16[128,3072]{1,0:T(8,128)(2,1)S(1)} %shard_map.126.mine_ref), channel_id=1, source_target_pairs={{0,16},{16,0},{1,17},{17,1},{2,18},{18,2},{3,19},{19,3},{4,20},{20... | collective-permute-start | bytes 2359304 | tf_op jit(solution)/shard_map/ppermute | solution.py:33
  61.9 21.4 %collective-permute-start.9 = (bf16[256,1536]{1,0:T(8,128)(2,1)S(1)}, bf16[256,1536]{1,0:T(8,128)(2,1)S(1)}, u32[]{:S(2)}, u32[]{:S(2)}) collective-permute-start(bf16[256,1536]{1,0:T(8,128)(2,1)S(1)} %get-tuple-element.53.own_ref), channel_id=1, source_target_pairs={{0,1},{1,0},{2,3},{3,2},{4,5},{5,4},{6,7},{7,6},{8,9},{9,8},{10,11... | collective-permute-start | bytes 2359304 | tf_op jit(solution)/shard_map/ppermute | solution.py:33
  62.9 12.4 %collective-permute-start.13 = (bf16[64,1664]{1,0:T(8,128)(2,1)S(1)}, bf16[64,1664]{1,0:T(8,128)(2,1)S(1)}, u32[]{:S(2)}, u32[]{:S(2)}) collective-permute-start(bf16[64,1664]{1,0:T(8,128)(2,1)S(1)} %shard_map.124.refs_4_.refs_0_), channel_id=1, source_target_pairs={{0,4},{2,6},{4,8},{6,10},{8,12},{10,14},{12,0},{14,2},{1,5},{3,7},... | collective-permute-start | bytes 638984 | tf_op jit(solution)/shard_map/ppermute | solution.py:530
  75.4 8.0 %collective-permute-start.14 = (bf16[64,1664]{1,0:T(8,128)(2,1)S(1)}, bf16[64,1664]{1,0:T(8,128)(2,1)S(1)}, u32[]{:S(2)}, u32[]{:S(2)}) collective-permute-start(bf16[64,1664]{1,0:T(8,128)(2,1)S(1)} %collective-permute-done.13.refs_4_.refs_1_), channel_id=1, source_target_pairs={{0,4},{2,6},{4,8},{6,10},{8,12},{10,14},{12,0},{14,2},{1,5},{3,7},... | collective-permute-start | bytes 638984 | tf_op jit(solution)/shard_map/ppermute | solution.py:530
  75.4 20.5 %collective-permute-start.4 = (bf16[256,1536]{1,0:T(8,128)(2,1)S(1)}, bf16[256,1536]{1,0:T(8,128)(2,1)S(1)}, u32[]{:S(2)}, u32[]{:S(2)}) collective-permute-start(bf16[256,1536]{1,0:T(8,128)(2,1)S(1)} %get-tuple-element.49.own_ref), channel_id=1, source_target_pairs={{0,1},{1,0},{2,3},{3,2},{4,5},{5,4},{6,7},{7,6},{8,9},{9,8},{10,11... | collective-permute-start | bytes 2359304 | tf_op jit(solution)/shard_map/ppermute | solution.py:33
  75.9 25.0 %collective-permute-start.16 = (bf16[128,3072]{1,0:T(8,128)(2,1)S(1)}, bf16[128,3072]{1,0:T(8,128)(2,1)S(1)}, u32[]{:S(2)}, u32[]{:S(2)}) collective-permute-start(bf16[128,3072]{1,0:T(8,128)(2,1)S(1)} %shard_map.127.refs_3_.mine_ref), channel_id=1, source_target_pairs={{0,16},{16,0},{1,17},{17,1},{2,18},{18,2},{3,19},{19,3},{4,20},{20... | collective-permute-start | bytes 2359304 | tf_op jit(solution)/shard_map/ppermute | solution.py:33
  82.3 30.4 %collective-permute-start.19 = (bf16[256,1536]{1,0:T(8,128)(2,1)S(1)}, bf16[256,1536]{1,0:T(8,128)(2,1)S(1)}, u32[]{:S(2)}, u32[]{:S(2)}) collective-permute-start(bf16[256,1536]{1,0:T(8,128)(2,1)S(1)} %get-tuple-element.63.own_ref), channel_id=1, source_target_pairs={{0,1},{1,0},{2,3},{3,2},{4,5},{5,4},{6,7},{7,6},{8,9},{9,8},{10,11... | collective-permute-start | bytes 2359304 | tf_op jit(solution)/shard_map/ppermute | solution.py:33
  88.5 31.8 %collective-permute-start.18 = (bf16[128,3072]{1,0:T(8,128)(2,1)S(1)}, bf16[128,3072]{1,0:T(8,128)(2,1)S(1)}, u32[]{:S(2)}, u32[]{:S(2)}) collective-permute-start(bf16[128,3072]{1,0:T(8,128)(2,1)S(1)} %get-tuple-element.62), channel_id=1, source_target_pairs={{0,16},{16,0},{1,17},{17,1},{2,18},{18,2},{3,19},{19,3},{4,20},{20... | collective-permute-start | bytes 2359304 | tf_op jit(solution)/shard_map/ppermute | solution.py:33
  89.7 17.7 %collective-permute-start.20 = (bf16[64,1664]{1,0:T(8,128)(2,1)S(1)}, bf16[64,1664]{1,0:T(8,128)(2,1)S(1)}, u32[]{:S(2)}, u32[]{:S(2)}) collective-permute-start(bf16[64,1664]{1,0:T(8,128)(2,1)S(1)} %collective-permute-done.14.refs_3_.refs_2_), channel_id=1, source_target_pairs={{0,4},{2,6},{4,8},{6,10},{8,12},{10,14},{12,0},{14,2},{1,5},{3,7},... | collective-permute-start | bytes 638984 | tf_op jit(solution)/shard_map/ppermute | solution.py:530
  105.9 21.0 %collective-permute-start.17 = (bf16[256,1536]{1,0:T(8,128)(2,1)S(1)}, bf16[256,1536]{1,0:T(8,128)(2,1)S(1)}, u32[]{:S(2)}, u32[]{:S(2)}) collective-permute-start(bf16[256,1536]{1,0:T(8,128)(2,1)S(1)} %get-tuple-element.60.own_ref), channel_id=1, source_target_pairs={{0,1},{1,0},{2,3},{3,2},{4,5},{5,4},{6,7},{7,6},{8,9},{9,8},{10,11... | collective-permute-start | bytes 2359304 | tf_op jit(solution)/shard_map/ppermute | solution.py:33
  117.8 15.9 %collective-permute-start.22 = (bf16[128,3072]{1,0:T(8,128)(2,1)S(1)}, bf16[128,3072]{1,0:T(8,128)(2,1)S(1)}, u32[]{:S(2)}, u32[]{:S(2)}) collective-permute-start(bf16[128,3072]{1,0:T(8,128)(2,1)S(1)} %get-tuple-element.70), channel_id=1, source_target_pairs={{0,16},{16,0},{1,17},{17,1},{2,18},{18,2},{3,19},{19,3},{4,20},{20... | collective-permute-start | bytes 2359304 | tf_op jit(solution)/shard_map/ppermute | solution.py:33
  120.5 14.1 %collective-permute-start.23 = (bf16[128,3072]{1,0:T(8,128)(2,1)S(1)}, bf16[128,3072]{1,0:T(8,128)(2,1)S(1)}, u32[]{:S(2)}, u32[]{:S(2)}) collective-permute-start(bf16[128,3072]{1,0:T(8,128)(2,1)S(1)} %get-tuple-element.71), channel_id=1, source_target_pairs={{0,4},{2,6},{4,8},{6,10},{8,12},{10,14},{12,0},{14,2},{1,5},{3,7},... | collective-permute-start | bytes 2359304 | tf_op jit(solution)/shard_map/ppermute | solution.py:530
  132.1 20.5 %collective-permute-start.21 = (bf16[128,3072]{1,0:T(8,128)(2,1)S(1)}, bf16[128,3072]{1,0:T(8,128)(2,1)S(1)}, u32[]{:S(2)}, u32[]{:S(2)}) collective-permute-start(bf16[128,3072]{1,0:T(8,128)(2,1)S(1)} %get-tuple-element.68), channel_id=1, source_target_pairs={{0,16},{16,0},{1,17},{17,1},{2,18},{18,2},{3,19},{19,3},{4,20},{20... | collective-permute-start | bytes 2359304 | tf_op jit(solution)/shard_map/ppermute | solution.py:33
  135.0 17.7 %collective-permute-start.24 = (bf16[128,3072]{1,0:T(8,128)(2,1)S(1)}, bf16[128,3072]{1,0:T(8,128)(2,1)S(1)}, u32[]{:S(2)}, u32[]{:S(2)}) collective-permute-start(bf16[128,3072]{1,0:T(8,128)(2,1)S(1)} %get-tuple-element.73), channel_id=1, source_target_pairs={{0,4},{2,6},{4,8},{6,10},{8,12},{10,14},{12,0},{14,2},{1,5},{3,7},... | collective-permute-start | bytes 2359304 | tf_op jit(solution)/shard_map/ppermute | solution.py:530
  135.1 18.0 %collective-permute-start.26 = (bf16[256,1664]{1,0:T(8,128)(2,1)S(1)}, bf16[256,1664]{1,0:T(8,128)(2,1)S(1)}, u32[]{:S(2)}, u32[]{:S(2)}) collective-permute-start(bf16[256,1664]{1,0:T(8,128)(2,1)S(1)} %shard_map.137.own_ref), channel_id=1, source_target_pairs={{0,2},{2,0},{4,6},{6,4},{8,10},{10,8},{12,14},{14,12},{1,3},{3,1},... | collective-permute-start | bytes 2555912 | tf_op jit(solution)/shard_map/ppermute | solution.py:658
  135.2 30.8 %collective-permute-start.15 = (bf16[128,3072]{1,0:T(8,128)(2,1)S(1)}, bf16[128,3072]{1,0:T(8,128)(2,1)S(1)}, u32[]{:S(2)}, u32[]{:S(2)}) collective-permute-start(bf16[128,3072]{1,0:T(8,128)(2,1)S(1)} %get-tuple-element.58), channel_id=1, source_target_pairs={{0,16},{16,0},{1,17},{17,1},{2,18},{18,2},{3,19},{19,3},{4,20},{20... | collective-permute-start | bytes 2359304 | tf_op jit(solution)/shard_map/ppermute | solution.py:33
  153.0 15.4 %collective-permute-start.25 = (bf16[128,3072]{1,0:T(8,128)(2,1)S(1)}, bf16[128,3072]{1,0:T(8,128)(2,1)S(1)}, u32[]{:S(2)}, u32[]{:S(2)}) collective-permute-start(bf16[128,3072]{1,0:T(8,128)(2,1)S(1)} %get-tuple-element.75), channel_id=1, source_target_pairs={{0,4},{2,6},{4,8},{6,10},{8,12},{10,14},{12,0},{14,2},{1,5},{3,7},... | collective-permute-start | bytes 2359304 | tf_op jit(solution)/shard_map/ppermute | solution.py:530
  169.4 13.9 %collective-permute-start.27 = (bf16[128,3072]{1,0:T(8,128)(2,1)S(1)}, bf16[128,3072]{1,0:T(8,128)(2,1)S(1)}, u32[]{:S(2)}, u32[]{:S(2)}) collective-permute-start(bf16[128,3072]{1,0:T(8,128)(2,1)S(1)} %get-tuple-element.78.rows_ref), channel_id=1, source_target_pairs={{0,16},{16,0},{1,17},{17,1},{2,18},{18,2},{3,19},{19,3},{4,20},{20... | collective-permute-start | bytes 2359304 | tf_op jit(solution)/shard_map/ppermute | solution.py:33
  172.8 12.5 %collective-permute-start.28 = (bf16[128,2048]{1,0:T(8,128)(2,1)S(1)}, bf16[128,2048]{1,0:T(8,128)(2,1)S(1)}, u32[]{:S(2)}, u32[]{:S(2)}) collective-permute-start(bf16[128,2048]{1,0:T(8,128)(2,1)S(1)} %shard_map.140.own_ref), channel_id=1, source_target_pairs={{0,1},{1,0},{2,3},{3,2},{4,5},{5,4},{6,7},{7,6},{8,9},{9,8},{10,11... | collective-permute-start | bytes 1572872 | tf_op jit(solution)/shard_map/ppermute | solution.py:33
  185.1 9.2 %collective-permute-start.29 = (bf16[128,2048]{1,0:T(8,128)(2,1)S(1)}, bf16[128,2048]{1,0:T(8,128)(2,1)S(1)}, u32[]{:S(2)}, u32[]{:S(2)}) collective-permute-start(bf16[128,2048]{1,0:T(8,128)(2,1)S(1)} %shard_map.142.own_ref), channel_id=1, source_target_pairs={{0,1},{1,0},{2,3},{3,2},{4,5},{5,4},{6,7},{7,6},{8,9},{9,8},{10,11... | collective-permute-start | bytes 1572872 | tf_op jit(solution)/shard_map/ppermute | solution.py:33
  187.2 9.5 %collective-permute-start.31 = (bf16[128,1152]{1,0:T(8,128)(2,1)S(1)}, bf16[128,1152]{1,0:T(8,128)(2,1)S(1)}, u32[]{:S(2)}, u32[]{:S(2)}) collective-permute-start(bf16[128,1152]{1,0:T(8,128)(2,1)S(1)} %get-tuple-element.84), channel_id=1, source_target_pairs={{0,16},{16,0},{1,17},{17,1},{2,18},{18,2},{3,19},{19,3},{4,20},{20... | collective-permute-start | bytes 884744 | tf_op jit(solution)/shard_map/ppermute | solution.py:33
  204.9 7.0 %collective-permute-start.32 = (bf16[128,512]{1,0:T(8,128)(2,1)S(1)}, bf16[128,512]{1,0:T(8,128)(2,1)S(1)}, u32[]{:S(2)}, u32[]{:S(2)}) collective-permute-start(bf16[128,512]{1,0:T(8,128)(2,1)S(1)} %get-tuple-element.87), channel_id=1, source_target_pairs={{0,4},{2,6},{4,8},{6,10},{8,12},{10,14},{12,0},{14,2},{1,5},{3,7},... | collective-permute-start | bytes 393224 | tf_op jit(solution)/shard_map/ppermute | solution.py:530
  204.9 8.7 %collective-permute-start.33 = (bf16[128,512]{1,0:T(8,128)(2,1)S(1)}, bf16[128,512]{1,0:T(8,128)(2,1)S(1)}, u32[]{:S(2)}, u32[]{:S(2)}) collective-permute-start(bf16[128,512]{1,0:T(8,128)(2,1)S(1)} %get-tuple-element.88), channel_id=1, source_target_pairs={{0,8},{2,10},{4,12},{6,14},{8,0},{10,2},{12,4},{14,6},{1,9},{3,11}... | collective-permute-start | bytes 393224 | tf_op jit(solution)/shard_map/ppermute | solution.py:530
  206.6 7.1 %collective-permute-start.34 = (bf16[128,512]{1,0:T(8,128)(2,1)S(1)}, bf16[128,512]{1,0:T(8,128)(2,1)S(1)}, u32[]{:S(2)}, u32[]{:S(2)}) collective-permute-start(bf16[128,512]{1,0:T(8,128)(2,1)S(1)} %get-tuple-element.89), channel_id=1, source_target_pairs={{0,12},{2,14},{4,0},{6,2},{8,4},{10,6},{12,8},{14,10},{1,13},{3,15... | collective-permute-start | bytes 393224 | tf_op jit(solution)/shard_map/ppermute | solution.py:530
  (27 other events, 344.3 us)

commit v2 on v1

--- a/solution.py
+++ b/solution.py
@@ -77,11 +77,30 @@
     )(value, token)
 
 
+def hold_kernel(value_ref, *refs):
+    out_ref, sem = refs[-2:]
+    copy = pltpu.make_async_copy(value_ref, out_ref, sem)
+    copy.start()
+    copy.wait()
+
+
+def held_call(value, after):
+    return pl.pallas_call(
+        hold_kernel,
+        in_specs=[HBM] * (1 + len(after)),
+        out_specs=VMEM,
+        out_shape=jax.ShapeDtypeStruct(value.shape, value.dtype),
+        scratch_shapes=[pltpu.SemaphoreType.DMA],
+        compiler_params=PARAMS,
+        cost_estimate=LIGHT,
+    )(value, *after)
+
+
 def up_kernel(cores, mine_ref, theirs_ref, *refs):
     weights, (out_ref, token_ref, rows_ref) = refs[:cores], refs[-3:]
     half = mine_ref.shape[0]
     units = weights[0].shape[1]
-    tile = tile_of(units, 768)
+    tile = tile_of(units, 256)
     rows_ref[:half] = mine_ref[...]
     rows_ref[half:] = theirs_ref[...]
     token_ref[...] = jnp.zeros(TOKEN, jnp.float32)
@@ -172,7 +191,7 @@
 def project_call(rows, weight, after):
     return pl.pallas_call(
         project_kernel,
-        in_specs=[VMEM, VMEM] + [VMEM] * len(after),
+        in_specs=[VMEM, VMEM] + [HBM] * len(after),
         out_specs=VMEM,
         out_shape=jax.ShapeDtypeStruct((rows.shape[0], weight.shape[1]), jnp.bfloat16),
         compiler_params=PARAMS,
@@ -636,33 +655,40 @@
     forwarded(1)
     messages = []
 
-    def hop():
-        if len(messages) < places:
-            messages.append(to_place(messages[-1], 1))
-        return messages[-1]
+    def hops():
+        for step in range(1, places):
+            back_one = step > 1 and step == places - 1
+            messages.append(
+                to_place(messages[0], -1) if back_one else to_place(messages[-1], 1)
+            )
 
     blocks[0] = halves_of(my_normed, normed)
+    if fast:
+        up_weights[-1] = held_call(up_weights[-1], token)
     up(0)
     forwarded(2)
     messages.append(message_call(caption_lengths, word_kept, word_other, token))
-    up(1, down_weights[-1], messages[0])
+    up(1, messages[0])
+    hops()
+    if fast:
+        down_weights[-1] = held_call(down_weights[-1], token)
+    down(0)
     forwarded(3)
-    up(2, blocks[places - 1][0], hop())
-    down(1, hop())
-    down(0)
+    up(2, blocks[places - 1][0], *messages[1:2])
+    down(1)
     up(3)
-    down(2, hop())
+    down(2, *messages[2:])
     back(1)
+    for step in range(4, places):
+        forwarded(step)
+        up(step)
+        down(step - 1)
+    down(places - 1)
     word_block = stack_call(messages)
     if cores == 2:
         word_blocks = [word_block, lax.ppermute(word_block, "grp", core_swap)]
     else:
         word_blocks = [word_block]
-    for step in range(4, places):
-        forwarded(step)
-        up(step)
-        down(step - 1)
-    down(places - 1)
     for step in range(2, places):
         back(step)
 
@@ -673,11 +699,12 @@
         near, near_token = near_call(
             spots, cand_counts, *word_blocks, places, most * CAP, token
         )
-        my_vision, _ = add_call(home, [near_token])
+        final_weight = held_call(out_weight, [near_token])
+        my_vision, _ = add_call(home, [near_token, final_weight])
         other_vision = shifted(my_vision, "vis", 1)
         pieces = []
         for block in (my_vision, other_vision):
-            partial = project_call(block, project_weight, [out_weight])
+            partial = project_call(block, project_weight, [])
             full = shifted(partial, "enc", 1)
             pieces.append(image_call(partial, full, encoder_gain, qkv_weight, spots))
         got = [shifted(sent, "vis", 1) for _, sent, _ in pieces]
@@ -693,7 +720,7 @@
         from_core = lax.ppermute(given, "grp", core_swap)
         from_both = lax.ppermute(given, ("vis", "grp"), across_both)
         from_vis = shifted(kept, "vis", 1)
-        mine, sent = output_call(spots, [kept, from_core, from_vis, from_both], out_weight)
+        mine, sent = output_call(spots, [kept, from_core, from_vis, from_both], final_weight)
         words_out = (mine + wide(shifted(sent, "enc", 1))).reshape(words.shape)
         vision_rows = jnp.where(
             vis == 0,

time: 230 us -> 220 us (0.957)
  Pallas kernels: 57.8 us -> 44.2 us
  starting transfers between devices: 32.9 us -> 38.2 us
    ppermute x12, waiting for transfers between devices: 44.2 us -> 33.8 us  [to_place(): lax.ppermute(value, 'grp', [(i, (i + step * cores) % groups) for i in ran...]
    pallas_call x4, Pallas kernels: 20.4 us -> 10.6 us  [up_call(): pl.pallas_call(functools.partial(up_kernel, cores), in_specs=[VMEM] * (2...]
    pallas_call x4, Pallas kernels: 20.3 us -> 11.1 us  [down_call(): pl.pallas_call(functools.partial(down_kernel, cores), in_specs=[VMEM] * (...]
    ppermute x22, waiting for transfers between devices: 78.8 us -> 85.5 us  [shifted(): lax.ppermute(value, axis, [(i, (i + step) % count) for i in range(count)])]
    pallas_call x2 -> x5, Pallas kernels: 3.61 us -> 8.98 us  [the longest x3 5.28 us: held_call(): pl.pallas_call(hold_kernel, in_specs=[HBM] * (1 + len(after)), out_specs=...]
    ppermute x12, starting transfers between devices: 6.32 us -> 11.5 us  [to_place(): lax.ppermute(value, 'grp', [(i, (i + step * cores) % groups) for i in ran...]
    unnamed x40 -> x42, local copies, waits for them, and re-layouts: 6.85 us -> 8.07 us
  transfers between devices with their start and end apart: 39 -> 39, of which waited for: 20 -> 26; matrix products, arithmetic and copies ran while one was open for 3% -> 3% of each run, Pallas kernels for 23% -> 18%
where the time goes in v2:
time: 220 us; the launch traced here: 219 us
  waiting for transfers between devices  121 us (55%)
  Pallas kernels  44.2 us (20%)
  starting transfers between devices  38.2 us (17%)
  local copies, waits for them, and re-layouts  8.32 us (4%)
  other arithmetic  6.85 us (3%)
    ppermute x22, waiting for transfers between devices, shifted(): lax.ppermute(value, axis, [(i, (i + step) % count) for i in range(count)])  85.5 us
    ppermute x12, waiting for transfers between devices, to_place(): lax.ppermute(value, 'grp', [(i, (i + step * cores) % groups) for i in ran...  33.8 us
    ppermute x22, starting transfers between devices, shifted(): lax.ppermute(value, axis, [(i, (i + step) % count) for i in range(count)])  25.8 us
    ppermute x12, starting transfers between devices, to_place(): lax.ppermute(value, 'grp', [(i, (i + step * cores) % groups) for i in ran...  11.5 us
    pallas_call x4, Pallas kernels, down_call(): pl.pallas_call(functools.partial(down_kernel, cores), in_specs=[VMEM] * (...  11.1 us
    pallas_call x4, Pallas kernels, up_call(): pl.pallas_call(functools.partial(up_kernel, cores), in_specs=[VMEM] * (2...  10.6 us
    unnamed x42, local copies, waits for them, and re-layouts  8.07 us
    pallas_call x3, Pallas kernels, held_call(): pl.pallas_call(hold_kernel, in_specs=[HBM] * (1 + len(after)), out_specs=...  5.28 us
  transfers between devices with their start and end apart: 39, of which 26 were waited for; matrix products, arithmetic and copies ran while one was open for 3% of the time, Pallas kernels for 18%

profile of v2, /device:TPU:0, one launch (start us, length us, event | category | flops | bytes accessed | tf_op | source)
XLA Modules:
  0.0 219.3 jit_solution(13371319756014688783)
XLA Ops:
  4.8 3.0 %collective-permute-start = (f32[2,256]{1,0:T(2,128)S(1)}, f32[2,256]{1,0:T(2,128)S(1)}, u32[]{:S(2)}, u32[]{:S(2)}) collective-permute-start(f32[2,256]{1,0:T(2,128)S(1)} %pad_maximum_fusion.1), channel_id=1, source_target_pairs={{0,1},{1,0},{2,3},{3,2},{4,5},{5,4},{6,7},{7,6},{8,9},{9,8},{10,11... | collective-permute-start | bytes 6152 | tf_op jit(solution)/shard_map/ppermute | solution.py:33
  9.4 2.1 collective-permute-done.2
  14.9 17.5 %collective-permute-done.6.mine_ref = bf16[128,3072]{1,0:T(8,128)(2,1)S(1)} collective-permute-done((bf16[128,3072]{1,0:T(8,128)(2,1)S(1)}, bf16[128,3072]{1,0:T(8,128)(2,1)S(1)}, u32[]{:S(2)}, u32[]{:S(2)}) %collective-permute-start.6) | collective-permute-done | bytes 786464 | tf_op jit(solution)/shard_map/ppermute | solution.py:549
  34.1 4.6 %copy-done = bf16[3,2048,1024]{2,1,0:T(8,128)(2,1)S(1)} copy-done((bf16[3,2048,1024]{2,1,0:T(8,128)(2,1)S(1)}, bf16[3,2048,1024]{2,1,0:T(8,128)(2,1)}, u32[]{:S(2)}) %copy-start) | copy-done | bytes 12582936
  38.7 2.9 %shard_map.122 = (bf16[64,1536]{1,0:T(8,128)(2,1)S(1)}, f32[64,1536]{1,0:T(8,128)S(1)}, f32[8,128]{1,0:T(8,128)S(1)}) custom-call(s32[5]{0:T(128)S(1)} %stack.35.vis_ref.spots_ref, bf16[64,2048]{1,0:T(8,128)(2,1)S(1)} %bitcast.41, bf16[3,2048,1024]{2,1,0:T(8,128)(2,1)S(1)} %copy-done, bf16[128,3072]{1,0:T(8,128)(2,1)S(1)} %get-tuple-element.95.refs_0_.mine_ref, ...), custom_call_target="tpu_custom_call" | custom-call | flops 1024 | bytes 1024 | tf_op jit(solution)/shard_map/pallas_call | solution.py:257
  42.1 2.5 %shard_map.123.refs_1_ = bf16[3072,768]{1,0:T(8,128)(2,1)S(1)} custom-call(bf16[3072,768]{1,0:T(8,128)(2,1)} %collective-permute-done.1.value_ref, f32[8,128]{1,0:T(8,128)S(1)} %get-tuple-element.48.refs_0_.refs_2_), custom_call_target="tpu_custom_call" | custom-call | flops 1024 | bytes 1024 | tf_op jit(solution)/shard_map/pallas_call | solution.py:88
  45.9 2.7 %shard_map.124 = (bf16[256,1536]{1,0:T(8,128)(2,1)S(1)}, f32[8,128]{1,0:T(8,128)S(1)}) custom-call(bf16[128,3072]{1,0:T(8,128)(2,1)S(1)} %get-tuple-element.95.refs_0_.mine_ref, bf16[128,3072]{1,0:T(8,128)(2,1)S(1)} %get-tuple-element.94.theirs_ref, bf16[3072,768]{1,0:T(8,128)(2,1)S(1)} %bitcast.36, bf16[3072,768]{1,0:T(8,128)(2,1)S(1)} %shard_map.123.refs_1_, ...), custom_call_target="tpu_custom_call" | custom-call | flops 1024 | bytes 1024 | tf_op jit(solution)/shard_map/pallas_call | solution.py:118
  49.1 3.6 %collective-permute-done.10.value_ref = bf16[128,3072]{1,0:T(8,128)(2,1)S(1)} collective-permute-done((bf16[128,3072]{1,0:T(8,128)(2,1)S(1)}, bf16[128,3072]{1,0:T(8,128)(2,1)S(1)}, u32[]{:S(2)}, u32[]{:S(2)}) %collective-permute-start.10) | collective-permute-done | bytes 786464 | tf_op jit(solution)/shard_map/ppermute | solution.py:549
  56.4 2.6 %shard_map.126 = (bf16[256,1536]{1,0:T(8,128)(2,1)S(1)}, f32[8,128]{1,0:T(8,128)S(1)}) custom-call(bf16[128,3072]{1,0:T(8,128)(2,1)S(1)} %collective-permute-done.6.mine_ref, bf16[128,3072]{1,0:T(8,128)(2,1)S(1)} %collective-permute-done.7.theirs_ref, bf16[3072,768]{1,0:T(8,128)(2,1)S(1)} %bitcast.36, bf16[3072,768]{1,0:T(8,128)(2,1)S(1)} %shard_map.123.refs_1_, ...), custom_call_target="tpu_custom_call" | custom-call | flops 1024 | bytes 1024 | tf_op jit(solution)/shard_map/pallas_call | solution.py:118
  59.7 2.5 %shard_map.127.refs_1_ = bf16[768,3072]{1,0:T(8,128)(2,1)S(1)} custom-call(bf16[768,3072]{1,0:T(8,128)(2,1)} %collective-permute-done.5.value_ref, f32[8,128]{1,0:T(8,128)S(1)} %get-tuple-element.53.refs_0_.refs_2_), custom_call_target="tpu_custom_call" | custom-call | flops 1024 | bytes 1024 | tf_op jit(solution)/shard_map/pallas_call | solution.py:88
  62.2 6.9 %collective-permute-done.4.other_ref = bf16[256,1536]{1,0:T(8,128)(2,1)S(1)} collective-permute-done((bf16[256,1536]{1,0:T(8,128)(2,1)S(1)}, bf16[256,1536]{1,0:T(8,128)(2,1)S(1)}, u32[]{:S(2)}, u32[]{:S(2)}) %collective-permute-start.4) | collective-permute-done | bytes 786464 | tf_op jit(solution)/shard_map/ppermute | solution.py:33
  69.1 2.8 %shard_map.128 = (bf16[128,3072]{1,0:T(8,128)(2,1)S(1)}, bf16[128,3072]{1,0:T(8,128)(2,1)S(1)}, f32[8,128]{1,0:T(8,128)S(1)}) custom-call(bf16[256,1536]{1,0:T(8,128)(2,1)S(1)} %get-tuple-element.49.own_ref, bf16[256,1536]{1,0:T(8,128)(2,1)S(1)} %collective-permute-done.4.other_ref, bf16[768,3072]{1,0:T(8,128)(2,1)S(1)} %bitcast.34, ...), custom_call_target="tpu_custom_call" | custom-call | flops 1024 | bytes 1024 | tf_op jit(solution)/shard_map/pallas_call | solution.py:169
  75.1 2.6 %shard_map.131 = (bf16[256,1536]{1,0:T(8,128)(2,1)S(1)}, f32[8,128]{1,0:T(8,128)S(1)}) custom-call(bf16[128,3072]{1,0:T(8,128)(2,1)S(1)} %shard_map.129.mine_ref, bf16[128,3072]{1,0:T(8,128)(2,1)S(1)} %collective-permute-done.14.theirs_ref, bf16[3072,768]{1,0:T(8,128)(2,1)S(1)} %bitcast.36, bf16[3072,768]{1,0:T(8,128)(2,1)S(1)} %shard_map.123.refs_1_, ...), custom_call_target="tpu_custom_call" | custom-call | flops 1024 | bytes 1024 | tf_op jit(solution)/shard_map/pallas_call | solution.py:118
  78.3 7.6 %collective-permute-done.13.other_ref = bf16[256,1536]{1,0:T(8,128)(2,1)S(1)} collective-permute-done((bf16[256,1536]{1,0:T(8,128)(2,1)S(1)}, bf16[256,1536]{1,0:T(8,128)(2,1)S(1)}, u32[]{:S(2)}, u32[]{:S(2)}) %collective-permute-start.13) | collective-permute-done | bytes 786464 | tf_op jit(solution)/shard_map/ppermute | solution.py:33
  85.9 2.8 %shard_map.132 = (bf16[128,3072]{1,0:T(8,128)(2,1)S(1)}, bf16[128,3072]{1,0:T(8,128)(2,1)S(1)}, f32[8,128]{1,0:T(8,128)S(1)}) custom-call(bf16[256,1536]{1,0:T(8,128)(2,1)S(1)} %get-tuple-element.57.own_ref, bf16[256,1536]{1,0:T(8,128)(2,1)S(1)} %collective-permute-done.13.other_ref, bf16[768,3072]{1,0:T(8,128)(2,1)S(1)} %bitcast.34, ...), custom_call_target="tpu_custom_call" | custom-call | flops 1024 | bytes 1024 | tf_op jit(solution)/shard_map/pallas_call | solution.py:169
  90.3 3.8 %collective-permute-start.20 = (bf16[64,1664]{1,0:T(8,128)(2,1)S(1)}, bf16[64,1664]{1,0:T(8,128)(2,1)S(1)}, u32[]{:S(2)}, u32[]{:S(2)}) collective-permute-start(bf16[64,1664]{1,0:T(8,128)(2,1)S(1)} %shard_map.125.refs_3_.refs_0_), channel_id=1, source_target_pairs={{0,12},{2,14},{4,0},{6,2},{8,4},{10,6},{12,8},{14,10},{1,13},{3,15... | collective-permute-start | bytes 638984 | tf_op jit(solution)/shard_map/ppermute | solution.py:549
  94.1 2.6 %shard_map.133 = (bf16[256,1536]{1,0:T(8,128)(2,1)S(1)}, f32[8,128]{1,0:T(8,128)S(1)}) custom-call(bf16[128,3072]{1,0:T(8,128)(2,1)S(1)} %shard_map.130.refs_3_.mine_ref, bf16[128,3072]{1,0:T(8,128)(2,1)S(1)} %collective-permute-done.12.theirs_ref, bf16[3072,768]{1,0:T(8,128)(2,1)S(1)} %bitcast.36, bf16[3072,768]{1,0:T(8,128)(2,1)S(1)} %shard_map.123.refs_1_, ...), custom_call_target="tpu_custom_call" | custom-call | flops 1024 | bytes 1024 | tf_op jit(solution)/shard_map/pallas_call | solution.py:118
  97.5 4.2 %collective-permute-done.19.refs_3_.refs_2_ = bf16[64,1664]{1,0:T(8,128)(2,1)S(1)} collective-permute-done((bf16[64,1664]{1,0:T(8,128)(2,1)S(1)}, bf16[64,1664]{1,0:T(8,128)(2,1)S(1)}, u32[]{:S(2)}, u32[]{:S(2)}) %collective-permute-start.19) | collective-permute-done | bytes 213024 | tf_op jit(solution)/shard_map/ppermute | solution.py:549
  102.8 2.8 %shard_map.134 = (bf16[128,3072]{1,0:T(8,128)(2,1)S(1)}, bf16[128,3072]{1,0:T(8,128)(2,1)S(1)}, f32[8,128]{1,0:T(8,128)S(1)}) custom-call(bf16[256,1536]{1,0:T(8,128)(2,1)S(1)} %get-tuple-element.63.own_ref, bf16[256,1536]{1,0:T(8,128)(2,1)S(1)} %collective-permute-done.18.other_ref, bf16[768,3072]{1,0:T(8,128)(2,1)S(1)} %bitcast.34, ...), custom_call_target="tpu_custom_call" | custom-call | flops 1024 | bytes 1024 | tf_op jit(solution)/shard_map/pallas_call | solution.py:169
  108.9 6.9 %collective-permute-done.16.other_ref = bf16[256,1536]{1,0:T(8,128)(2,1)S(1)} collective-permute-done((bf16[256,1536]{1,0:T(8,128)(2,1)S(1)}, bf16[256,1536]{1,0:T(8,128)(2,1)S(1)}, u32[]{:S(2)}, u32[]{:S(2)}) %collective-permute-start.16) | collective-permute-done | bytes 786464 | tf_op jit(solution)/shard_map/ppermute | solution.py:33
  115.8 2.8 %shard_map.136 = (bf16[128,3072]{1,0:T(8,128)(2,1)S(1)}, bf16[128,3072]{1,0:T(8,128)(2,1)S(1)}, f32[8,128]{1,0:T(8,128)S(1)}) custom-call(bf16[256,1536]{1,0:T(8,128)(2,1)S(1)} %get-tuple-element.60.own_ref, bf16[256,1536]{1,0:T(8,128)(2,1)S(1)} %collective-permute-done.16.other_ref, bf16[768,3072]{1,0:T(8,128)(2,1)S(1)} %bitcast.34, ...), custom_call_target="tpu_custom_call" | custom-call | flops 1024 | bytes 1024 | tf_op jit(solution)/shard_map/pallas_call | solution.py:169
  120.1 4.8 %collective-permute-done.22.refs_1_ = bf16[128,3072]{1,0:T(8,128)(2,1)S(1)} collective-permute-done((bf16[128,3072]{1,0:T(8,128)(2,1)S(1)}, bf16[128,3072]{1,0:T(8,128)(2,1)S(1)}, u32[]{:S(2)}, u32[]{:S(2)}) %collective-permute-start.22) | collective-permute-done | bytes 786464 | tf_op jit(solution)/shard_map/ppermute | solution.py:33
  127.0 14.7 %collective-permute-done.21.refs_1_ = bf16[128,3072]{1,0:T(8,128)(2,1)S(1)} collective-permute-done((bf16[128,3072]{1,0:T(8,128)(2,1)S(1)}, bf16[128,3072]{1,0:T(8,128)(2,1)S(1)}, u32[]{:S(2)}, u32[]{:S(2)}) %collective-permute-start.21) | collective-permute-done | bytes 786464 | tf_op jit(solution)/shard_map/ppermute | solution.py:33
  143.6 11.4 %collective-permute-done.9.refs_2_ = bf16[128,3072]{1,0:T(8,128)(2,1)S(1)} collective-permute-done((bf16[128,3072]{1,0:T(8,128)(2,1)S(1)}, bf16[128,3072]{1,0:T(8,128)(2,1)S(1)}, u32[]{:S(2)}, u32[]{:S(2)}) %collective-permute-start.9) | collective-permute-done | bytes 786464 | tf_op jit(solution)/shard_map/ppermute | solution.py:33
  161.2 10.7 %collective-permute-done.27.rows_ref = bf16[128,3072]{1,0:T(8,128)(2,1)S(1)} collective-permute-done((bf16[128,3072]{1,0:T(8,128)(2,1)S(1)}, bf16[128,3072]{1,0:T(8,128)(2,1)S(1)}, u32[]{:S(2)}, u32[]{:S(2)}) %collective-permute-start.27) | collective-permute-done | bytes 786464 | tf_op jit(solution)/shard_map/ppermute | solution.py:33
  177.8 5.2 %collective-permute-done.29.other_ref = bf16[128,2048]{1,0:T(8,128)(2,1)S(1)} collective-permute-done((bf16[128,2048]{1,0:T(8,128)(2,1)S(1)}, bf16[128,2048]{1,0:T(8,128)(2,1)S(1)}, u32[]{:S(2)}, u32[]{:S(2)}) %collective-permute-start.29) | collective-permute-done | bytes 524320 | tf_op jit(solution)/shard_map/ppermute | solution.py:33
  186.4 5.3 %collective-permute-done.30.refs_1_ = bf16[128,1152]{1,0:T(8,128)(2,1)S(1)} collective-permute-done((bf16[128,1152]{1,0:T(8,128)(2,1)S(1)}, bf16[128,1152]{1,0:T(8,128)(2,1)S(1)}, u32[]{:S(2)}, u32[]{:S(2)}) %collective-permute-start.30) | collective-permute-done | bytes 294944 | tf_op jit(solution)/shard_map/ppermute | solution.py:33
  195.0 2.2 collective-permute-start.33
  200.5 2.8 %collective-permute-done.33.refs_2_ = bf16[128,512]{1,0:T(8,128)(2,1)S(1)} collective-permute-done((bf16[128,512]{1,0:T(8,128)(2,1)S(1)}, bf16[128,512]{1,0:T(8,128)(2,1)S(1)}, u32[]{:S(2)}, u32[]{:S(2)}) %collective-permute-start.33) | collective-permute-done | bytes 131104 | tf_op jit(solution)/shard_map/ppermute | solution.py:549
  205.5 2.6 %collective-permute-done.36.vis_ref = bf16[64,512]{1,0:T(8,128)(2,1)S(1)} collective-permute-done((bf16[64,512]{1,0:T(8,128)(2,1)S(1)}, bf16[64,512]{1,0:T(8,128)(2,1)S(1)}, u32[]{:S(2)}, u32[]{:S(2)}) %collective-permute-start.36) | collective-permute-done | bytes 65568 | tf_op jit(solution)/shard_map/ppermute | solution.py:33
  209.4 2.2 copy-done.2
  215.1 3.5 %collective-permute-done.38 = bf16[32,2048]{1,0:T(8,128)(2,1)S(1)} collective-permute-done((bf16[32,2048]{1,0:T(8,128)(2,1)S(1)}, bf16[32,2048]{1,0:T(8,128)(2,1)S(1)}, u32[]{:S(2)}, u32[]{:S(2)}) %collective-permute-start.38) | collective-permute-done | bytes 131104 | tf_op jit(solution)/shard_map/ppermute | solution.py:33
  (137 shorter events, 62.9 us)
Async XLA Ops:
  0.7 41.5 %collective-permute-start.1 = (bf16[3072,768]{1,0:T(8,128)(2,1)}, bf16[3072,768]{1,0:T(8,128)(2,1)}, u32[]{:S(2)}, u32[]{:S(2)}) collective-permute-start(bf16[3072,768]{1,0:T(8,128)(2,1)} %refs_0_.13), channel_id=1, source_target_pairs={{0,2},{2,0},{4,6},{6,4},{8,10},{10,8},{12,14},{14,12},{1,3},{3,1},... | collective-permute-start | bytes 14155784 | tf_op jit(solution)/shard_map/ppermute | solution.py:542
  1.2 58.5 %collective-permute-start.5 = (bf16[768,3072]{1,0:T(8,128)(2,1)}, bf16[768,3072]{1,0:T(8,128)(2,1)}, u32[]{:S(2)}, u32[]{:S(2)}) collective-permute-start(bf16[768,3072]{1,0:T(8,128)(2,1)} %refs_0_.15), channel_id=1, source_target_pairs={{0,2},{2,0},{4,6},{6,4},{8,10},{10,8},{12,14},{14,12},{1,3},{3,1},... | collective-permute-start | bytes 14155784 | tf_op jit(solution)/shard_map/ppermute | solution.py:543
  12.4 20.0 %collective-permute-start.6 = (bf16[128,3072]{1,0:T(8,128)(2,1)S(1)}, bf16[128,3072]{1,0:T(8,128)(2,1)S(1)}, u32[]{:S(2)}, u32[]{:S(2)}) collective-permute-start(bf16[128,3072]{1,0:T(8,128)(2,1)S(1)} %get-tuple-element.95.refs_0_.mine_ref), channel_id=1, source_target_pairs={{0,4},{2,6},{4,8},{6,10},{8,12},{10,14},{12,0},{14,2},{1,5},{3,7},... | collective-permute-start | bytes 2359304 | tf_op jit(solution)/shard_map/ppermute | solution.py:549
  14.1 19.8 %collective-permute-start.3 = (bf16[4,8,2048]{2,1,0:T(8,128)(2,1)S(1)}, bf16[4,8,2048]{2,1,0:T(8,128)(2,1)S(1)}, u32[]{:S(2)}, u32[]{:S(2)}) collective-permute-start(bf16[4,8,2048]{2,1,0:T(8,128)(2,1)S(1)} %fusion.8), channel_id=1, source_target_pairs={{0,1},{1,0},{2,3},{3,2},{4,5},{5,4},{6,7},{7,6},{8,9},{9,8},{10,11... | collective-permute-start | bytes 393224 | tf_op jit(solution)/shard_map/ppermute | solution.py:33
  32.4 24.0 %collective-permute-start.7 = (bf16[128,3072]{1,0:T(8,128)(2,1)S(1)}, bf16[128,3072]{1,0:T(8,128)(2,1)S(1)}, u32[]{:S(2)}, u32[]{:S(2)}) collective-permute-start(bf16[128,3072]{1,0:T(8,128)(2,1)S(1)} %collective-permute-done.6.mine_ref), channel_id=1, source_target_pairs={{0,16},{16,0},{1,17},{17,1},{2,18},{18,2},{3,19},{19,3},{4,20},{20... | collective-permute-start | bytes 2359304 | tf_op jit(solution)/shard_map/ppermute | solution.py:33
  33.9 18.8 %collective-permute-start.10 = (bf16[128,3072]{1,0:T(8,128)(2,1)S(1)}, bf16[128,3072]{1,0:T(8,128)(2,1)S(1)}, u32[]{:S(2)}, u32[]{:S(2)}) collective-permute-start(bf16[128,3072]{1,0:T(8,128)(2,1)S(1)} %collective-permute-done.6.mine_ref), channel_id=1, source_target_pairs={{0,4},{2,6},{4,8},{6,10},{8,12},{10,14},{12,0},{14,2},{1,5},{3,7},... | collective-permute-start | bytes 2359304 | tf_op jit(solution)/shard_map/ppermute | solution.py:549
  41.5 12.8 %collective-permute-start.8 = (bf16[64,1536]{1,0:T(8,128)(2,1)S(1)}, bf16[64,1536]{1,0:T(8,128)(2,1)S(1)}, u32[]{:S(2)}, u32[]{:S(2)}) collective-permute-start(bf16[64,1536]{1,0:T(8,128)(2,1)S(1)} %get-tuple-element.52), channel_id=1, source_target_pairs={{0,16},{16,0},{1,17},{17,1},{2,18},{18,2},{3,19},{19,3},{4,20},{20... | collective-permute-start | bytes 589832 | tf_op jit(solution)/shard_map/ppermute | solution.py:33
  48.5 20.5 %collective-permute-start.4 = (bf16[256,1536]{1,0:T(8,128)(2,1)S(1)}, bf16[256,1536]{1,0:T(8,128)(2,1)S(1)}, u32[]{:S(2)}, u32[]{:S(2)}) collective-permute-start(bf16[256,1536]{1,0:T(8,128)(2,1)S(1)} %get-tuple-element.49.own_ref), channel_id=1, source_target_pairs={{0,1},{1,0},{2,3},{3,2},{4,5},{5,4},{6,7},{7,6},{8,9},{9,8},{10,11... | collective-permute-start | bytes 2359304 | tf_op jit(solution)/shard_map/ppermute | solution.py:33
  52.7 20.1 %collective-permute-start.11 = (bf16[128,3072]{1,0:T(8,128)(2,1)S(1)}, bf16[128,3072]{1,0:T(8,128)(2,1)S(1)}, u32[]{:S(2)}, u32[]{:S(2)}) collective-permute-start(bf16[128,3072]{1,0:T(8,128)(2,1)S(1)} %shard_map.129.mine_ref), channel_id=1, source_target_pairs={{0,4},{2,6},{4,8},{6,10},{8,12},{10,14},{12,0},{14,2},{1,5},{3,7},... | collective-permute-start | bytes 2359304 | tf_op jit(solution)/shard_map/ppermute | solution.py:549
  54.3 20.7 %collective-permute-start.14 = (bf16[128,3072]{1,0:T(8,128)(2,1)S(1)}, bf16[128,3072]{1,0:T(8,128)(2,1)S(1)}, u32[]{:S(2)}, u32[]{:S(2)}) collective-permute-start(bf16[128,3072]{1,0:T(8,128)(2,1)S(1)} %shard_map.129.mine_ref), channel_id=1, source_target_pairs={{0,16},{16,0},{1,17},{17,1},{2,18},{18,2},{3,19},{19,3},{4,20},{20... | collective-permute-start | bytes 2359304 | tf_op jit(solution)/shard_map/ppermute | solution.py:33
  59.1 26.8 %collective-permute-start.13 = (bf16[256,1536]{1,0:T(8,128)(2,1)S(1)}, bf16[256,1536]{1,0:T(8,128)(2,1)S(1)}, u32[]{:S(2)}, u32[]{:S(2)}) collective-permute-start(bf16[256,1536]{1,0:T(8,128)(2,1)S(1)} %get-tuple-element.57.own_ref), channel_id=1, source_target_pairs={{0,1},{1,0},{2,3},{3,2},{4,5},{5,4},{6,7},{7,6},{8,9},{9,8},{10,11... | collective-permute-start | bytes 2359304 | tf_op jit(solution)/shard_map/ppermute | solution.py:33
  59.7 15.4 %collective-permute-start.15 = (bf16[64,1664]{1,0:T(8,128)(2,1)S(1)}, bf16[64,1664]{1,0:T(8,128)(2,1)S(1)}, u32[]{:S(2)}, u32[]{:S(2)}) collective-permute-start(bf16[64,1664]{1,0:T(8,128)(2,1)S(1)} %shard_map.125.refs_3_.refs_0_), channel_id=1, source_target_pairs={{0,4},{2,6},{4,8},{6,10},{8,12},{10,14},{12,0},{14,2},{1,5},{3,7},... | collective-permute-start | bytes 638984 | tf_op jit(solution)/shard_map/ppermute | solution.py:549
  72.8 21.3 %collective-permute-start.12 = (bf16[128,3072]{1,0:T(8,128)(2,1)S(1)}, bf16[128,3072]{1,0:T(8,128)(2,1)S(1)}, u32[]{:S(2)}, u32[]{:S(2)}) collective-permute-start(bf16[128,3072]{1,0:T(8,128)(2,1)S(1)} %shard_map.130.refs_3_.mine_ref), channel_id=1, source_target_pairs={{0,16},{16,0},{1,17},{17,1},{2,18},{18,2},{3,19},{19,3},{4,20},{20... | collective-permute-start | bytes 2359304 | tf_op jit(solution)/shard_map/ppermute | solution.py:33
  77.7 25.1 %collective-permute-start.18 = (bf16[256,1536]{1,0:T(8,128)(2,1)S(1)}, bf16[256,1536]{1,0:T(8,128)(2,1)S(1)}, u32[]{:S(2)}, u32[]{:S(2)}) collective-permute-start(bf16[256,1536]{1,0:T(8,128)(2,1)S(1)} %get-tuple-element.63.own_ref), channel_id=1, source_target_pairs={{0,1},{1,0},{2,3},{3,2},{4,5},{5,4},{6,7},{7,6},{8,9},{9,8},{10,11... | collective-permute-start | bytes 2359304 | tf_op jit(solution)/shard_map/ppermute | solution.py:33
  88.7 19.4 %collective-permute-start.17 = (bf16[128,3072]{1,0:T(8,128)(2,1)S(1)}, bf16[128,3072]{1,0:T(8,128)(2,1)S(1)}, u32[]{:S(2)}, u32[]{:S(2)}) collective-permute-start(bf16[128,3072]{1,0:T(8,128)(2,1)S(1)} %get-tuple-element.62), channel_id=1, source_target_pairs={{0,16},{16,0},{1,17},{17,1},{2,18},{18,2},{3,19},{19,3},{4,20},{20... | collective-permute-start | bytes 2359304 | tf_op jit(solution)/shard_map/ppermute | solution.py:33
  90.3 7.2 %collective-permute-start.20 = (bf16[64,1664]{1,0:T(8,128)(2,1)S(1)}, bf16[64,1664]{1,0:T(8,128)(2,1)S(1)}, u32[]{:S(2)}, u32[]{:S(2)}) collective-permute-start(bf16[64,1664]{1,0:T(8,128)(2,1)S(1)} %shard_map.125.refs_3_.refs_0_), channel_id=1, source_target_pairs={{0,12},{2,14},{4,0},{6,2},{8,4},{10,6},{12,8},{14,10},{1,13},{3,15... | collective-permute-start | bytes 638984 | tf_op jit(solution)/shard_map/ppermute | solution.py:549
  94.1 7.6 %collective-permute-start.19 = (bf16[64,1664]{1,0:T(8,128)(2,1)S(1)}, bf16[64,1664]{1,0:T(8,128)(2,1)S(1)}, u32[]{:S(2)}, u32[]{:S(2)}) collective-permute-start(bf16[64,1664]{1,0:T(8,128)(2,1)S(1)} %collective-permute-done.15.refs_4_.refs_1_), channel_id=1, source_target_pairs={{0,4},{2,6},{4,8},{6,10},{8,12},{10,14},{12,0},{14,2},{1,5},{3,7},... | collective-permute-start | bytes 638984 | tf_op jit(solution)/shard_map/ppermute | solution.py:549
  96.7 19.1 %collective-permute-start.16 = (bf16[256,1536]{1,0:T(8,128)(2,1)S(1)}, bf16[256,1536]{1,0:T(8,128)(2,1)S(1)}, u32[]{:S(2)}, u32[]{:S(2)}) collective-permute-start(bf16[256,1536]{1,0:T(8,128)(2,1)S(1)} %get-tuple-element.60.own_ref), channel_id=1, source_target_pairs={{0,1},{1,0},{2,3},{3,2},{4,5},{5,4},{6,7},{7,6},{8,9},{9,8},{10,11... | collective-permute-start | bytes 2359304 | tf_op jit(solution)/shard_map/ppermute | solution.py:33
  105.6 19.4 %collective-permute-start.22 = (bf16[128,3072]{1,0:T(8,128)(2,1)S(1)}, bf16[128,3072]{1,0:T(8,128)(2,1)S(1)}, u32[]{:S(2)}, u32[]{:S(2)}) collective-permute-start(bf16[128,3072]{1,0:T(8,128)(2,1)S(1)} %get-tuple-element.70), channel_id=1, source_target_pairs={{0,16},{16,0},{1,17},{17,1},{2,18},{18,2},{3,19},{19,3},{4,20},{20... | collective-permute-start | bytes 2359304 | tf_op jit(solution)/shard_map/ppermute | solution.py:33
  108.3 16.7 %collective-permute-start.23 = (bf16[128,3072]{1,0:T(8,128)(2,1)S(1)}, bf16[128,3072]{1,0:T(8,128)(2,1)S(1)}, u32[]{:S(2)}, u32[]{:S(2)}) collective-permute-start(bf16[128,3072]{1,0:T(8,128)(2,1)S(1)} %get-tuple-element.71), channel_id=1, source_target_pairs={{0,4},{2,6},{4,8},{6,10},{8,12},{10,14},{12,0},{14,2},{1,5},{3,7},... | collective-permute-start | bytes 2359304 | tf_op jit(solution)/shard_map/ppermute | solution.py:549
  118.6 23.2 %collective-permute-start.21 = (bf16[128,3072]{1,0:T(8,128)(2,1)S(1)}, bf16[128,3072]{1,0:T(8,128)(2,1)S(1)}, u32[]{:S(2)}, u32[]{:S(2)}) collective-permute-start(bf16[128,3072]{1,0:T(8,128)(2,1)S(1)} %get-tuple-element.68), channel_id=1, source_target_pairs={{0,16},{16,0},{1,17},{17,1},{2,18},{18,2},{3,19},{19,3},{4,20},{20... | collective-permute-start | bytes 2359304 | tf_op jit(solution)/shard_map/ppermute | solution.py:33
  125.3 16.5 %collective-permute-start.24 = (bf16[128,3072]{1,0:T(8,128)(2,1)S(1)}, bf16[128,3072]{1,0:T(8,128)(2,1)S(1)}, u32[]{:S(2)}, u32[]{:S(2)}) collective-permute-start(bf16[128,3072]{1,0:T(8,128)(2,1)S(1)} %get-tuple-element.73), channel_id=1, source_target_pairs={{0,4},{2,6},{4,8},{6,10},{8,12},{10,14},{12,0},{14,2},{1,5},{3,7},... | collective-permute-start | bytes 2359304 | tf_op jit(solution)/shard_map/ppermute | solution.py:549
  125.4 16.8 %collective-permute-start.26 = (bf16[256,1664]{1,0:T(8,128)(2,1)S(1)}, bf16[256,1664]{1,0:T(8,128)(2,1)S(1)}, u32[]{:S(2)}, u32[]{:S(2)}) collective-permute-start(bf16[256,1664]{1,0:T(8,128)(2,1)S(1)} %shard_map.139.own_ref), channel_id=1, source_target_pairs={{0,2},{2,0},{4,6},{6,4},{8,10},{10,8},{12,14},{14,12},{1,3},{3,1},... | collective-permute-start | bytes 2555912 | tf_op jit(solution)/shard_map/ppermute | solution.py:689
  125.5 29.5 %collective-permute-start.9 = (bf16[128,3072]{1,0:T(8,128)(2,1)S(1)}, bf16[128,3072]{1,0:T(8,128)(2,1)S(1)}, u32[]{:S(2)}, u32[]{:S(2)}) collective-permute-start(bf16[128,3072]{1,0:T(8,128)(2,1)S(1)} %get-tuple-element.55), channel_id=1, source_target_pairs={{0,16},{16,0},{1,17},{17,1},{2,18},{18,2},{3,19},{19,3},{4,20},{20... | collective-permute-start | bytes 2359304 | tf_op jit(solution)/shard_map/ppermute | solution.py:33
  142.1 14.1 %collective-permute-start.25 = (bf16[128,3072]{1,0:T(8,128)(2,1)S(1)}, bf16[128,3072]{1,0:T(8,128)(2,1)S(1)}, u32[]{:S(2)}, u32[]{:S(2)}) collective-permute-start(bf16[128,3072]{1,0:T(8,128)(2,1)S(1)} %get-tuple-element.75), channel_id=1, source_target_pairs={{0,4},{2,6},{4,8},{6,10},{8,12},{10,14},{12,0},{14,2},{1,5},{3,7},... | collective-permute-start | bytes 2359304 | tf_op jit(solution)/shard_map/ppermute | solution.py:549
  157.2 14.7 %collective-permute-start.27 = (bf16[128,3072]{1,0:T(8,128)(2,1)S(1)}, bf16[128,3072]{1,0:T(8,128)(2,1)S(1)}, u32[]{:S(2)}, u32[]{:S(2)}) collective-permute-start(bf16[128,3072]{1,0:T(8,128)(2,1)S(1)} %get-tuple-element.78.rows_ref), channel_id=1, source_target_pairs={{0,16},{16,0},{1,17},{17,1},{2,18},{18,2},{3,19},{19,3},{4,20},{20... | collective-permute-start | bytes 2359304 | tf_op jit(solution)/shard_map/ppermute | solution.py:33
  160.6 14.2 %collective-permute-start.28 = (bf16[128,2048]{1,0:T(8,128)(2,1)S(1)}, bf16[128,2048]{1,0:T(8,128)(2,1)S(1)}, u32[]{:S(2)}, u32[]{:S(2)}) collective-permute-start(bf16[128,2048]{1,0:T(8,128)(2,1)S(1)} %shard_map.143.own_ref), channel_id=1, source_target_pairs={{0,1},{1,0},{2,3},{3,2},{4,5},{5,4},{6,7},{7,6},{8,9},{9,8},{10,11... | collective-permute-start | bytes 1572872 | tf_op jit(solution)/shard_map/ppermute | solution.py:33
  173.8 9.2 %collective-permute-start.29 = (bf16[128,2048]{1,0:T(8,128)(2,1)S(1)}, bf16[128,2048]{1,0:T(8,128)(2,1)S(1)}, u32[]{:S(2)}, u32[]{:S(2)}) collective-permute-start(bf16[128,2048]{1,0:T(8,128)(2,1)S(1)} %shard_map.145.own_ref), channel_id=1, source_target_pairs={{0,1},{1,0},{2,3},{3,2},{4,5},{5,4},{6,7},{7,6},{8,9},{9,8},{10,11... | collective-permute-start | bytes 1572872 | tf_op jit(solution)/shard_map/ppermute | solution.py:33
  176.7 9.7 %collective-permute-start.31 = (bf16[128,1152]{1,0:T(8,128)(2,1)S(1)}, bf16[128,1152]{1,0:T(8,128)(2,1)S(1)}, u32[]{:S(2)}, u32[]{:S(2)}) collective-permute-start(bf16[128,1152]{1,0:T(8,128)(2,1)S(1)} %get-tuple-element.84), channel_id=1, source_target_pairs={{0,16},{16,0},{1,17},{17,1},{2,18},{18,2},{3,19},{19,3},{4,20},{20... | collective-permute-start | bytes 884744 | tf_op jit(solution)/shard_map/ppermute | solution.py:33
  184.9 6.8 %collective-permute-start.30 = (bf16[128,1152]{1,0:T(8,128)(2,1)S(1)}, bf16[128,1152]{1,0:T(8,128)(2,1)S(1)}, u32[]{:S(2)}, u32[]{:S(2)}) collective-permute-start(bf16[128,1152]{1,0:T(8,128)(2,1)S(1)} %get-tuple-element.81), channel_id=1, source_target_pairs={{0,16},{16,0},{1,17},{17,1},{2,18},{18,2},{3,19},{19,3},{4,20},{20... | collective-permute-start | bytes 884744 | tf_op jit(solution)/shard_map/ppermute | solution.py:33
  193.6 6.9 %collective-permute-start.32 = (bf16[128,512]{1,0:T(8,128)(2,1)S(1)}, bf16[128,512]{1,0:T(8,128)(2,1)S(1)}, u32[]{:S(2)}, u32[]{:S(2)}) collective-permute-start(bf16[128,512]{1,0:T(8,128)(2,1)S(1)} %get-tuple-element.87), channel_id=1, source_target_pairs={{0,4},{2,6},{4,8},{6,10},{8,12},{10,14},{12,0},{14,2},{1,5},{3,7},... | collective-permute-start | bytes 393224 | tf_op jit(solution)/shard_map/ppermute | solution.py:549
  195.0 8.3 %collective-permute-start.33 = (bf16[128,512]{1,0:T(8,128)(2,1)S(1)}, bf16[128,512]{1,0:T(8,128)(2,1)S(1)}, u32[]{:S(2)}, u32[]{:S(2)}) collective-permute-start(bf16[128,512]{1,0:T(8,128)(2,1)S(1)} %get-tuple-element.88), channel_id=1, source_target_pairs={{0,8},{2,10},{4,12},{6,14},{8,0},{10,2},{12,4},{14,6},{1,9},{3,11}... | collective-permute-start | bytes 393224 | tf_op jit(solution)/shard_map/ppermute | solution.py:549
  (28 other events, 271.3 us)

commit v3 on v2

--- a/solution.py
+++ b/solution.py
@@ -567,8 +567,6 @@
     def gated(value):
         return value + token[0][0, 0].astype(value.dtype) if token else value
 
-    words = wide(captions)
-    word_power = summed(jnp.sum(words * words, axis=-1), "vis")
     tokens = wide(image_tokens[0])
     row_total, row_squares = summed(
         jnp.stack([jnp.sum(tokens, axis=-1), jnp.sum(tokens * tokens, axis=-1)]), "enc"
@@ -580,6 +578,8 @@
     )
     my_tokens = mine_of(image_tokens[0])
     my_normed = mine_of(normed)
+    words = wide(captions) + wide(my_normed[0, 0]) * 0.0
+    word_power = summed(jnp.sum(words * words, axis=-1), "vis")
 
     inner = qkv_weight.shape[2]
     heads = inner // DH
@@ -665,32 +665,36 @@
     blocks[0] = halves_of(my_normed, normed)
     if fast:
         up_weights[-1] = held_call(up_weights[-1], token)
-    up(0)
-    forwarded(2)
-    messages.append(message_call(caption_lengths, word_kept, word_other, token))
+    messages.append(
+        message_call(caption_lengths, word_kept, word_other, [*token, up_weights[-1]])
+    )
     up(1, messages[0])
     hops()
+    forwarded(2)
     if fast:
         down_weights[-1] = held_call(down_weights[-1], token)
-    down(0)
+    down(1)
     forwarded(3)
     up(2, blocks[places - 1][0], *messages[1:2])
-    down(1)
+    back(1)
     up(3)
     down(2, *messages[2:])
-    back(1)
+    up(0, *[backs[step] for step in backs])
     for step in range(4, places):
         forwarded(step)
         up(step)
         down(step - 1)
     down(places - 1)
+    for step in range(2, places - 1):
+        back(step)
+    down(0)
     word_block = stack_call(messages)
     if cores == 2:
         word_blocks = [word_block, lax.ppermute(word_block, "grp", core_swap)]
     else:
         word_blocks = [word_block]
-    for step in range(2, places):
-        back(step)
+    if places > 2:
+        back(places - 1)
 
     home = [my_tokens, *outs[0], *([backs[places - 1]] if places > 1 else [])]
     cands = groups * cand_local

time: 220 us -> 231 us (1.050)
  starting transfers between devices: 38.2 us -> 45.2 us
  other arithmetic: 6.85 us -> 9.59 us
    ppermute x22, waiting for transfers between devices: 85.5 us -> 95 us  [shifted(): lax.ppermute(value, axis, [(i, (i + step) % count) for i in range(count)])]
    ppermute x12, waiting for transfers between devices: 33.8 us -> 28 us  [to_place(): lax.ppermute(value, 'grp', [(i, (i + step * cores) % groups) for i in ran...]
    ppermute x12, starting transfers between devices: 11.5 us -> 15.4 us  [to_place(): lax.ppermute(value, 'grp', [(i, (i + step * cores) % groups) for i in ran...]
  transfers between devices with their start and end apart: 39 -> 39, of which waited for: 26 -> 24; matrix products, arithmetic and copies ran while one was open for 3% -> 4% of each run, Pallas kernels for 18% -> 17%
where the time goes in v3:
time: 231 us
  waiting for transfers between devices  123 us (53%)
  starting transfers between devices  45.2 us (20%)
  Pallas kernels  44.1 us (19%)
  other arithmetic  9.59 us (4%)
  local copies, waits for them, and re-layouts  7.09 us (3%)
    ppermute x22, waiting for transfers between devices, shifted(): lax.ppermute(value, axis, [(i, (i + step) % count) for i in range(count)])  95 us
    ppermute x22, starting transfers between devices, shifted(): lax.ppermute(value, axis, [(i, (i + step) % count) for i in range(count)])  28 us
    ppermute x12, waiting for transfers between devices, to_place(): lax.ppermute(value, 'grp', [(i, (i + step * cores) % groups) for i in ran...  28 us
    ppermute x12, starting transfers between devices, to_place(): lax.ppermute(value, 'grp', [(i, (i + step * cores) % groups) for i in ran...  15.4 us
    pallas_call x4, Pallas kernels, down_call(): pl.pallas_call(functools.partial(down_kernel, cores), in_specs=[VMEM] * (...  11.1 us
    pallas_call x4, Pallas kernels, up_call(): pl.pallas_call(functools.partial(up_kernel, cores), in_specs=[VMEM] * (2...  10.6 us
    unnamed x42, local copies, waits for them, and re-layouts  6.85 us
    pallas_call x3, Pallas kernels, held_call(): pl.pallas_call(hold_kernel, in_specs=[HBM] * (1 + len(after)), out_specs=...  5.14 us
  transfers between devices with their start and end apart: 39, of which 24 were waited for; matrix products, arithmetic and copies ran while one was open for 4% of the time, Pallas kernels for 17%

profile of v3, /device:TPU:0, one launch (start us, length us, event | category | flops | bytes accessed | tf_op | source)
XLA Modules:
  0.0 230.6 jit_solution(15656017191346086687)
XLA Ops:
  4.8 3.0 %collective-permute-start = (f32[2,256]{1,0:T(2,128)S(1)}, f32[2,256]{1,0:T(2,128)S(1)}, u32[]{:S(2)}, u32[]{:S(2)}) collective-permute-start(f32[2,256]{1,0:T(2,128)S(1)} %pad_maximum_fusion.1), channel_id=1, source_target_pairs={{0,1},{1,0},{2,3},{3,2},{4,5},{5,4},{6,7},{7,6},{8,9},{9,8},{10,11... | collective-permute-start | bytes 6152 | tf_op jit(solution)/shard_map/ppermute | solution.py:33
  17.8 15.6 %collective-permute-done.4.mine_ref = bf16[128,3072]{1,0:T(8,128)(2,1)S(1)} collective-permute-done((bf16[128,3072]{1,0:T(8,128)(2,1)S(1)}, bf16[128,3072]{1,0:T(8,128)(2,1)S(1)}, u32[]{:S(2)}, u32[]{:S(2)}) %collective-permute-start.4) | collective-permute-done | bytes 786464 | tf_op jit(solution)/shard_map/ppermute | solution.py:549
  34.7 4.6 %copy-done = bf16[3,2048,1024]{2,1,0:T(8,128)(2,1)S(1)} copy-done((bf16[3,2048,1024]{2,1,0:T(8,128)(2,1)S(1)}, bf16[3,2048,1024]{2,1,0:T(8,128)(2,1)}, u32[]{:S(2)}) %copy-start) | copy-done | bytes 12582936
  39.3 2.9 %shard_map.122 = (bf16[64,1536]{1,0:T(8,128)(2,1)S(1)}, f32[64,1536]{1,0:T(8,128)S(1)}, f32[8,128]{1,0:T(8,128)S(1)}) custom-call(s32[5]{0:T(128)S(1)} %stack.35.vis_ref.spots_ref, bf16[64,2048]{1,0:T(8,128)(2,1)S(1)} %bitcast.44, bf16[3,2048,1024]{2,1,0:T(8,128)(2,1)S(1)} %copy-done, bf16[128,3072]{1,0:T(8,128)(2,1)S(1)} %get-tuple-element.95.refs_0_.mine_ref, ...), custom_call_target="tpu_custom_call" | custom-call | flops 1024 | bytes 1024 | tf_op jit(solution)/shard_map/pallas_call | solution.py:257
  43.7 2.5 %shard_map.123.refs_1_ = bf16[3072,768]{1,0:T(8,128)(2,1)S(1)} custom-call(bf16[3072,768]{1,0:T(8,128)(2,1)} %collective-permute-done.1.value_ref, f32[8,128]{1,0:T(8,128)S(1)} %get-tuple-element.48.refs_0_.refs_2_), custom_call_target="tpu_custom_call" | custom-call | flops 1024 | bytes 1024 | tf_op jit(solution)/shard_map/pallas_call | solution.py:88
  46.2 8.7 %collective-permute-done.7.other_ref = bf16[64,1536]{1,0:T(8,128)(2,1)S(1)} collective-permute-done((bf16[64,1536]{1,0:T(8,128)(2,1)S(1)}, bf16[64,1536]{1,0:T(8,128)(2,1)S(1)}, u32[]{:S(2)}, u32[]{:S(2)}) %collective-permute-start.7) | collective-permute-done | bytes 196640 | tf_op jit(solution)/shard_map/ppermute | solution.py:33
  55.5 2.6 %shard_map.125 = (bf16[256,1536]{1,0:T(8,128)(2,1)S(1)}, f32[8,128]{1,0:T(8,128)S(1)}) custom-call(bf16[128,3072]{1,0:T(8,128)(2,1)S(1)} %collective-permute-done.4.mine_ref, bf16[128,3072]{1,0:T(8,128)(2,1)S(1)} %collective-permute-done.6.theirs_ref, bf16[3072,768]{1,0:T(8,128)(2,1)S(1)} %bitcast.39, bf16[3072,768]{1,0:T(8,128)(2,1)S(1)} %shard_map.123.refs_1_, ...), custom_call_target="tpu_custom_call" | custom-call | flops 1024 | bytes 1024 | tf_op jit(solution)/shard_map/pallas_call | solution.py:118
  62.9 2.3 %shard_map.127.refs_1_ = bf16[768,3072]{1,0:T(8,128)(2,1)S(1)} custom-call(bf16[768,3072]{1,0:T(8,128)(2,1)} %collective-permute-done.10.value_ref, f32[8,128]{1,0:T(8,128)S(1)} %get-tuple-element.51.token_ref.refs_0_.refs_2_), custom_call_target="tpu_custom_call" | custom-call | flops 1024 | bytes 1024 | tf_op jit(solution)/shard_map/pallas_call | solution.py:88
  65.3 9.3 %collective-permute-done.9.other_ref = bf16[256,1536]{1,0:T(8,128)(2,1)S(1)} collective-permute-done((bf16[256,1536]{1,0:T(8,128)(2,1)S(1)}, bf16[256,1536]{1,0:T(8,128)(2,1)S(1)}, u32[]{:S(2)}, u32[]{:S(2)}) %collective-permute-start.9) | collective-permute-done | bytes 786464 | tf_op jit(solution)/shard_map/ppermute | solution.py:33
  74.6 2.8 %shard_map.128 = (bf16[128,3072]{1,0:T(8,128)(2,1)S(1)}, bf16[128,3072]{1,0:T(8,128)(2,1)S(1)}, f32[8,128]{1,0:T(8,128)S(1)}) custom-call(bf16[256,1536]{1,0:T(8,128)(2,1)S(1)} %get-tuple-element.52.own_ref, bf16[256,1536]{1,0:T(8,128)(2,1)S(1)} %collective-permute-done.9.other_ref, bf16[768,3072]{1,0:T(8,128)(2,1)S(1)} %bitcast.37, ...), custom_call_target="tpu_custom_call" | custom-call | flops 1024 | bytes 1024 | tf_op jit(solution)/shard_map/pallas_call | solution.py:169
  82.3 2.6 %shard_map.130 = (bf16[256,1536]{1,0:T(8,128)(2,1)S(1)}, f32[8,128]{1,0:T(8,128)S(1)}) custom-call(bf16[128,3072]{1,0:T(8,128)(2,1)S(1)} %shard_map.126.mine_ref, bf16[128,3072]{1,0:T(8,128)(2,1)S(1)} %collective-permute-done.8.theirs_ref, bf16[3072,768]{1,0:T(8,128)(2,1)S(1)} %bitcast.39, bf16[3072,768]{1,0:T(8,128)(2,1)S(1)} %shard_map.123.refs_1_, ...), custom_call_target="tpu_custom_call" | custom-call | flops 1024 | bytes 1024 | tf_op jit(solution)/shard_map/pallas_call | solution.py:118
  87.5 10.4 %collective-permute-done.15.refs_1_ = bf16[128,3072]{1,0:T(8,128)(2,1)S(1)} collective-permute-done((bf16[128,3072]{1,0:T(8,128)(2,1)S(1)}, bf16[128,3072]{1,0:T(8,128)(2,1)S(1)}, u32[]{:S(2)}, u32[]{:S(2)}) %collective-permute-start.15) | collective-permute-done | bytes 786464 | tf_op jit(solution)/shard_map/ppermute | solution.py:33
  98.9 11.0 %collective-permute-done.14.theirs_ref = bf16[128,3072]{1,0:T(8,128)(2,1)S(1)} collective-permute-done((bf16[128,3072]{1,0:T(8,128)(2,1)S(1)}, bf16[128,3072]{1,0:T(8,128)(2,1)S(1)}, u32[]{:S(2)}, u32[]{:S(2)}) %collective-permute-start.14) | collective-permute-done | bytes 786464 | tf_op jit(solution)/shard_map/ppermute | solution.py:33
  109.9 2.6 %shard_map.132 = (bf16[256,1536]{1,0:T(8,128)(2,1)S(1)}, f32[8,128]{1,0:T(8,128)S(1)}) custom-call(bf16[128,3072]{1,0:T(8,128)(2,1)S(1)} %shard_map.129.refs_3_.mine_ref, bf16[128,3072]{1,0:T(8,128)(2,1)S(1)} %collective-permute-done.14.theirs_ref, bf16[3072,768]{1,0:T(8,128)(2,1)S(1)} %bitcast.39, bf16[3072,768]{1,0:T(8,128)(2,1)S(1)} %shard_map.123.refs_1_, ...), custom_call_target="tpu_custom_call" | custom-call | flops 1024 | bytes 1024 | tf_op jit(solution)/shard_map/pallas_call | solution.py:118
  113.9 2.8 %shard_map.133 = (bf16[128,3072]{1,0:T(8,128)(2,1)S(1)}, bf16[128,3072]{1,0:T(8,128)(2,1)S(1)}, f32[8,128]{1,0:T(8,128)S(1)}) custom-call(bf16[256,1536]{1,0:T(8,128)(2,1)S(1)} %get-tuple-element.54.own_ref, bf16[256,1536]{1,0:T(8,128)(2,1)S(1)} %collective-permute-done.13.other_ref, bf16[768,3072]{1,0:T(8,128)(2,1)S(1)} %bitcast.37, ...), custom_call_target="tpu_custom_call" | custom-call | flops 1024 | bytes 1024 | tf_op jit(solution)/shard_map/pallas_call | solution.py:169
  117.3 2.7 %shard_map.134 = (bf16[256,1536]{1,0:T(8,128)(2,1)S(1)}, f32[8,128]{1,0:T(8,128)S(1)}) custom-call(bf16[128,3072]{1,0:T(8,128)(2,1)S(1)} %get-tuple-element.95.refs_0_.mine_ref, bf16[128,3072]{1,0:T(8,128)(2,1)S(1)} %get-tuple-element.94.theirs_ref, bf16[3072,768]{1,0:T(8,128)(2,1)S(1)} %bitcast.39, bf16[3072,768]{1,0:T(8,128)(2,1)S(1)} %shard_map.123.refs_1_, ...), custom_call_target="tpu_custom_call" | custom-call | flops 1024 | bytes 1024 | tf_op jit(solution)/shard_map/pallas_call | solution.py:118
  121.2 11.9 %collective-permute-done.21.other_ref = bf16[256,1536]{1,0:T(8,128)(2,1)S(1)} collective-permute-done((bf16[256,1536]{1,0:T(8,128)(2,1)S(1)}, bf16[256,1536]{1,0:T(8,128)(2,1)S(1)}, u32[]{:S(2)}, u32[]{:S(2)}) %collective-permute-start.21) | collective-permute-done | bytes 786464 | tf_op jit(solution)/shard_map/ppermute | solution.py:33
  133.1 2.8 %shard_map.135 = (bf16[128,3072]{1,0:T(8,128)(2,1)S(1)}, bf16[128,3072]{1,0:T(8,128)(2,1)S(1)}, f32[8,128]{1,0:T(8,128)S(1)}) custom-call(bf16[256,1536]{1,0:T(8,128)(2,1)S(1)} %get-tuple-element.65.own_ref, bf16[256,1536]{1,0:T(8,128)(2,1)S(1)} %collective-permute-done.21.other_ref, bf16[768,3072]{1,0:T(8,128)(2,1)S(1)} %bitcast.37, ...), custom_call_target="tpu_custom_call" | custom-call | flops 1024 | bytes 1024 | tf_op jit(solution)/shard_map/pallas_call | solution.py:169
  138.6 5.6 %collective-permute-done.19.other_ref = bf16[256,1536]{1,0:T(8,128)(2,1)S(1)} collective-permute-done((bf16[256,1536]{1,0:T(8,128)(2,1)S(1)}, bf16[256,1536]{1,0:T(8,128)(2,1)S(1)}, u32[]{:S(2)}, u32[]{:S(2)}) %collective-permute-start.19) | collective-permute-done | bytes 786464 | tf_op jit(solution)/shard_map/ppermute | solution.py:33
  144.1 2.8 %shard_map.137 = (bf16[128,3072]{1,0:T(8,128)(2,1)S(1)}, bf16[128,3072]{1,0:T(8,128)(2,1)S(1)}, f32[8,128]{1,0:T(8,128)S(1)}) custom-call(bf16[256,1536]{1,0:T(8,128)(2,1)S(1)} %get-tuple-element.62.own_ref, bf16[256,1536]{1,0:T(8,128)(2,1)S(1)} %collective-permute-done.19.other_ref, bf16[768,3072]{1,0:T(8,128)(2,1)S(1)} %bitcast.37, ...), custom_call_target="tpu_custom_call" | custom-call | flops 1024 | bytes 1024 | tf_op jit(solution)/shard_map/pallas_call | solution.py:169
  148.0 3.3 %collective-permute-done.23.refs_1_ = bf16[128,3072]{1,0:T(8,128)(2,1)S(1)} collective-permute-done((bf16[128,3072]{1,0:T(8,128)(2,1)S(1)}, bf16[128,3072]{1,0:T(8,128)(2,1)S(1)}, u32[]{:S(2)}, u32[]{:S(2)}) %collective-permute-start.23) | collective-permute-done | bytes 786464 | tf_op jit(solution)/shard_map/ppermute | solution.py:33
  151.2 2.7 %collective-permute-done.24.refs_2_ = bf16[128,3072]{1,0:T(8,128)(2,1)S(1)} collective-permute-done((bf16[128,3072]{1,0:T(8,128)(2,1)S(1)}, bf16[128,3072]{1,0:T(8,128)(2,1)S(1)}, u32[]{:S(2)}, u32[]{:S(2)}) %collective-permute-start.24) | collective-permute-done | bytes 786464 | tf_op jit(solution)/shard_map/ppermute | solution.py:549
  156.0 8.8 %collective-permute-done.22.refs_2_ = bf16[128,3072]{1,0:T(8,128)(2,1)S(1)} collective-permute-done((bf16[128,3072]{1,0:T(8,128)(2,1)S(1)}, bf16[128,3072]{1,0:T(8,128)(2,1)S(1)}, u32[]{:S(2)}, u32[]{:S(2)}) %collective-permute-start.22) | collective-permute-done | bytes 786464 | tf_op jit(solution)/shard_map/ppermute | solution.py:33
  164.8 3.5 %collective-permute-done.25.refs_3_ = bf16[128,3072]{1,0:T(8,128)(2,1)S(1)} collective-permute-done((bf16[128,3072]{1,0:T(8,128)(2,1)S(1)}, bf16[128,3072]{1,0:T(8,128)(2,1)S(1)}, u32[]{:S(2)}, u32[]{:S(2)}) %collective-permute-start.25) | collective-permute-done | bytes 786464 | tf_op jit(solution)/shard_map/ppermute | solution.py:549
  174.9 8.1 %collective-permute-done.27.rows_ref = bf16[128,3072]{1,0:T(8,128)(2,1)S(1)} collective-permute-done((bf16[128,3072]{1,0:T(8,128)(2,1)S(1)}, bf16[128,3072]{1,0:T(8,128)(2,1)S(1)}, u32[]{:S(2)}, u32[]{:S(2)}) %collective-permute-start.27) | collective-permute-done | bytes 786464 | tf_op jit(solution)/shard_map/ppermute | solution.py:33
  189.7 4.4 %collective-permute-done.29.other_ref = bf16[128,2048]{1,0:T(8,128)(2,1)S(1)} collective-permute-done((bf16[128,2048]{1,0:T(8,128)(2,1)S(1)}, bf16[128,2048]{1,0:T(8,128)(2,1)S(1)}, u32[]{:S(2)}, u32[]{:S(2)}) %collective-permute-start.29) | collective-permute-done | bytes 524320 | tf_op jit(solution)/shard_map/ppermute | solution.py:33
  198.1 4.8 %collective-permute-done.30.refs_1_ = bf16[128,1152]{1,0:T(8,128)(2,1)S(1)} collective-permute-done((bf16[128,1152]{1,0:T(8,128)(2,1)S(1)}, bf16[128,1152]{1,0:T(8,128)(2,1)S(1)}, u32[]{:S(2)}, u32[]{:S(2)}) %collective-permute-start.30) | collective-permute-done | bytes 294944 | tf_op jit(solution)/shard_map/ppermute | solution.py:33
  205.4 3.3 %collective-permute-start.33 = (bf16[128,512]{1,0:T(8,128)(2,1)S(1)}, bf16[128,512]{1,0:T(8,128)(2,1)S(1)}, u32[]{:S(2)}, u32[]{:S(2)}) collective-permute-start(bf16[128,512]{1,0:T(8,128)(2,1)S(1)} %get-tuple-element.88), channel_id=1, source_target_pairs={{0,8},{2,10},{4,12},{6,14},{8,0},{10,2},{12,4},{14,6},{1,9},{3,11}... | collective-permute-start | bytes 393224 | tf_op jit(solution)/shard_map/ppermute | solution.py:549
  208.7 2.8 %collective-permute-start.34 = (bf16[128,512]{1,0:T(8,128)(2,1)S(1)}, bf16[128,512]{1,0:T(8,128)(2,1)S(1)}, u32[]{:S(2)}, u32[]{:S(2)}) collective-permute-start(bf16[128,512]{1,0:T(8,128)(2,1)S(1)} %get-tuple-element.89), channel_id=1, source_target_pairs={{0,12},{2,14},{4,0},{6,2},{8,4},{10,6},{12,8},{14,10},{1,13},{3,15... | collective-permute-start | bytes 393224 | tf_op jit(solution)/shard_map/ppermute | solution.py:549
  216.4 3.1 %collective-permute-done.36.vis_ref = bf16[64,512]{1,0:T(8,128)(2,1)S(1)} collective-permute-done((bf16[64,512]{1,0:T(8,128)(2,1)S(1)}, bf16[64,512]{1,0:T(8,128)(2,1)S(1)}, u32[]{:S(2)}, u32[]{:S(2)}) %collective-permute-start.36) | collective-permute-done | bytes 65568 | tf_op jit(solution)/shard_map/ppermute | solution.py:33
  220.0 2.2 copy-done.2
  226.9 2.4 %collective-permute-done.38 = bf16[32,2048]{1,0:T(8,128)(2,1)S(1)} collective-permute-done((bf16[32,2048]{1,0:T(8,128)(2,1)S(1)}, bf16[32,2048]{1,0:T(8,128)(2,1)S(1)}, u32[]{:S(2)}, u32[]{:S(2)}) %collective-permute-start.38) | collective-permute-done | bytes 131104 | tf_op jit(solution)/shard_map/ppermute | solution.py:33
  (138 shorter events, 70.5 us)
Async XLA Ops:
  0.7 43.0 %collective-permute-start.1 = (bf16[3072,768]{1,0:T(8,128)(2,1)}, bf16[3072,768]{1,0:T(8,128)(2,1)}, u32[]{:S(2)}, u32[]{:S(2)}) collective-permute-start(bf16[3072,768]{1,0:T(8,128)(2,1)} %refs_0_.13), channel_id=1, source_target_pairs={{0,2},{2,0},{4,6},{6,4},{8,10},{10,8},{12,14},{14,12},{1,3},{3,1},... | collective-permute-start | bytes 14155784 | tf_op jit(solution)/shard_map/ppermute | solution.py:542
  1.2 61.7 %collective-permute-start.10 = (bf16[768,3072]{1,0:T(8,128)(2,1)}, bf16[768,3072]{1,0:T(8,128)(2,1)}, u32[]{:S(2)}, u32[]{:S(2)}) collective-permute-start(bf16[768,3072]{1,0:T(8,128)(2,1)} %refs_0_.15), channel_id=1, source_target_pairs={{0,2},{2,0},{4,6},{6,4},{8,10},{10,8},{12,14},{14,12},{1,3},{3,1},... | collective-permute-start | bytes 14155784 | tf_op jit(solution)/shard_map/ppermute | solution.py:543
  13.4 20.0 %collective-permute-start.4 = (bf16[128,3072]{1,0:T(8,128)(2,1)S(1)}, bf16[128,3072]{1,0:T(8,128)(2,1)S(1)}, u32[]{:S(2)}, u32[]{:S(2)}) collective-permute-start(bf16[128,3072]{1,0:T(8,128)(2,1)S(1)} %get-tuple-element.95.refs_0_.mine_ref), channel_id=1, source_target_pairs={{0,4},{2,6},{4,8},{6,10},{8,12},{10,14},{12,0},{14,2},{1,5},{3,7},... | collective-permute-start | bytes 2359304 | tf_op jit(solution)/shard_map/ppermute | solution.py:549
  15.7 18.3 %collective-permute-start.3 = (bf16[4,8,2048]{2,1,0:T(8,128)(2,1)S(1)}, bf16[4,8,2048]{2,1,0:T(8,128)(2,1)S(1)}, u32[]{:S(2)}, u32[]{:S(2)}) collective-permute-start(bf16[4,8,2048]{2,1,0:T(8,128)(2,1)S(1)} %multiply_convert_fusion), channel_id=1, source_target_pairs={{0,1},{1,0},{2,3},{3,2},{4,5},{5,4},{6,7},{7,6},{8,9},{9,8},{10,11... | collective-permute-start | bytes 393224 | tf_op jit(solution)/shard_map/ppermute | solution.py:33
  33.4 26.3 %collective-permute-start.5 = (bf16[128,3072]{1,0:T(8,128)(2,1)S(1)}, bf16[128,3072]{1,0:T(8,128)(2,1)S(1)}, u32[]{:S(2)}, u32[]{:S(2)}) collective-permute-start(bf16[128,3072]{1,0:T(8,128)(2,1)S(1)} %collective-permute-done.4.mine_ref), channel_id=1, source_target_pairs={{0,4},{2,6},{4,8},{6,10},{8,12},{10,14},{12,0},{14,2},{1,5},{3,7},... | collective-permute-start | bytes 2359304 | tf_op jit(solution)/shard_map/ppermute | solution.py:549
  33.4 22.1 %collective-permute-start.6 = (bf16[128,3072]{1,0:T(8,128)(2,1)S(1)}, bf16[128,3072]{1,0:T(8,128)(2,1)S(1)}, u32[]{:S(2)}, u32[]{:S(2)}) collective-permute-start(bf16[128,3072]{1,0:T(8,128)(2,1)S(1)} %collective-permute-done.4.mine_ref), channel_id=1, source_target_pairs={{0,16},{16,0},{1,17},{17,1},{2,18},{18,2},{3,19},{19,3},{4,20},{20... | collective-permute-start | bytes 2359304 | tf_op jit(solution)/shard_map/ppermute | solution.py:33
  42.1 12.8 %collective-permute-start.7 = (bf16[64,1536]{1,0:T(8,128)(2,1)S(1)}, bf16[64,1536]{1,0:T(8,128)(2,1)S(1)}, u32[]{:S(2)}, u32[]{:S(2)}) collective-permute-start(bf16[64,1536]{1,0:T(8,128)(2,1)S(1)} %get-tuple-element.50), channel_id=1, source_target_pairs={{0,16},{16,0},{1,17},{17,1},{2,18},{18,2},{3,19},{19,3},{4,20},{20... | collective-permute-start | bytes 589832 | tf_op jit(solution)/shard_map/ppermute | solution.py:33
  58.2 16.4 %collective-permute-start.9 = (bf16[256,1536]{1,0:T(8,128)(2,1)S(1)}, bf16[256,1536]{1,0:T(8,128)(2,1)S(1)}, u32[]{:S(2)}, u32[]{:S(2)}) collective-permute-start(bf16[256,1536]{1,0:T(8,128)(2,1)S(1)} %get-tuple-element.52.own_ref), channel_id=1, source_target_pairs={{0,1},{1,0},{2,3},{3,2},{4,5},{5,4},{6,7},{7,6},{8,9},{9,8},{10,11... | collective-permute-start | bytes 2359304 | tf_op jit(solution)/shard_map/ppermute | solution.py:33
  59.8 20.2 %collective-permute-start.11 = (bf16[128,3072]{1,0:T(8,128)(2,1)S(1)}, bf16[128,3072]{1,0:T(8,128)(2,1)S(1)}, u32[]{:S(2)}, u32[]{:S(2)}) collective-permute-start(bf16[128,3072]{1,0:T(8,128)(2,1)S(1)} %shard_map.126.mine_ref), channel_id=1, source_target_pairs={{0,4},{2,6},{4,8},{6,10},{8,12},{10,14},{12,0},{14,2},{1,5},{3,7},... | collective-permute-start | bytes 2359304 | tf_op jit(solution)/shard_map/ppermute | solution.py:549
  60.8 21.6 %collective-permute-start.8 = (bf16[128,3072]{1,0:T(8,128)(2,1)S(1)}, bf16[128,3072]{1,0:T(8,128)(2,1)S(1)}, u32[]{:S(2)}, u32[]{:S(2)}) collective-permute-start(bf16[128,3072]{1,0:T(8,128)(2,1)S(1)} %shard_map.126.mine_ref), channel_id=1, source_target_pairs={{0,16},{16,0},{1,17},{17,1},{2,18},{18,2},{3,19},{19,3},{4,20},{20... | collective-permute-start | bytes 2359304 | tf_op jit(solution)/shard_map/ppermute | solution.py:33
  61.3 21.0 %collective-permute-start.12 = (bf16[64,1664]{1,0:T(8,128)(2,1)S(1)}, bf16[64,1664]{1,0:T(8,128)(2,1)S(1)}, u32[]{:S(2)}, u32[]{:S(2)}) collective-permute-start(bf16[64,1664]{1,0:T(8,128)(2,1)S(1)} %shard_map.124.refs_3_.refs_0_), channel_id=1, source_target_pairs={{0,4},{2,6},{4,8},{6,10},{8,12},{10,14},{12,0},{14,2},{1,5},{3,7},... | collective-permute-start | bytes 638984 | tf_op jit(solution)/shard_map/ppermute | solution.py:549
  77.4 20.5 %collective-permute-start.15 = (bf16[128,3072]{1,0:T(8,128)(2,1)S(1)}, bf16[128,3072]{1,0:T(8,128)(2,1)S(1)}, u32[]{:S(2)}, u32[]{:S(2)}) collective-permute-start(bf16[128,3072]{1,0:T(8,128)(2,1)S(1)} %get-tuple-element.56), channel_id=1, source_target_pairs={{0,16},{16,0},{1,17},{17,1},{2,18},{18,2},{3,19},{19,3},{4,20},{20... | collective-permute-start | bytes 2359304 | tf_op jit(solution)/shard_map/ppermute | solution.py:33
  80.0 29.9 %collective-permute-start.14 = (bf16[128,3072]{1,0:T(8,128)(2,1)S(1)}, bf16[128,3072]{1,0:T(8,128)(2,1)S(1)}, u32[]{:S(2)}, u32[]{:S(2)}) collective-permute-start(bf16[128,3072]{1,0:T(8,128)(2,1)S(1)} %shard_map.129.refs_3_.mine_ref), channel_id=1, source_target_pairs={{0,16},{16,0},{1,17},{17,1},{2,18},{18,2},{3,19},{19,3},{4,20},{20... | collective-permute-start | bytes 2359304 | tf_op jit(solution)/shard_map/ppermute | solution.py:33
  85.0 28.9 %collective-permute-start.13 = (bf16[256,1536]{1,0:T(8,128)(2,1)S(1)}, bf16[256,1536]{1,0:T(8,128)(2,1)S(1)}, u32[]{:S(2)}, u32[]{:S(2)}) collective-permute-start(bf16[256,1536]{1,0:T(8,128)(2,1)S(1)} %get-tuple-element.54.own_ref), channel_id=1, source_target_pairs={{0,1},{1,0},{2,3},{3,2},{4,5},{5,4},{6,7},{7,6},{8,9},{9,8},{10,11... | collective-permute-start | bytes 2359304 | tf_op jit(solution)/shard_map/ppermute | solution.py:33
  85.5 28.5 %collective-permute-start.17 = (bf16[64,1664]{1,0:T(8,128)(2,1)S(1)}, bf16[64,1664]{1,0:T(8,128)(2,1)S(1)}, u32[]{:S(2)}, u32[]{:S(2)}) collective-permute-start(bf16[64,1664]{1,0:T(8,128)(2,1)S(1)} %shard_map.124.refs_3_.refs_0_), channel_id=1, source_target_pairs={{0,12},{2,14},{4,0},{6,2},{8,4},{10,6},{12,8},{14,10},{1,13},{3,15... | collective-permute-start | bytes 638984 | tf_op jit(solution)/shard_map/ppermute | solution.py:549
  87.0 27.0 %collective-permute-start.16 = (bf16[64,1664]{1,0:T(8,128)(2,1)S(1)}, bf16[64,1664]{1,0:T(8,128)(2,1)S(1)}, u32[]{:S(2)}, u32[]{:S(2)}) collective-permute-start(bf16[64,1664]{1,0:T(8,128)(2,1)S(1)} %collective-permute-done.12.refs_4_.refs_1_), channel_id=1, source_target_pairs={{0,4},{2,6},{4,8},{6,10},{8,12},{10,14},{12,0},{14,2},{1,5},{3,7},... | collective-permute-start | bytes 638984 | tf_op jit(solution)/shard_map/ppermute | solution.py:549
  98.1 19.2 %collective-permute-start.18 = (bf16[128,3072]{1,0:T(8,128)(2,1)S(1)}, bf16[128,3072]{1,0:T(8,128)(2,1)S(1)}, u32[]{:S(2)}, u32[]{:S(2)}) collective-permute-start(bf16[128,3072]{1,0:T(8,128)(2,1)S(1)} %get-tuple-element.61), channel_id=1, source_target_pairs={{0,4},{2,6},{4,8},{6,10},{8,12},{10,14},{12,0},{14,2},{1,5},{3,7},... | collective-permute-start | bytes 2359304 | tf_op jit(solution)/shard_map/ppermute | solution.py:549
  112.5 20.5 %collective-permute-start.21 = (bf16[256,1536]{1,0:T(8,128)(2,1)S(1)}, bf16[256,1536]{1,0:T(8,128)(2,1)S(1)}, u32[]{:S(2)}, u32[]{:S(2)}) collective-permute-start(bf16[256,1536]{1,0:T(8,128)(2,1)S(1)} %get-tuple-element.65.own_ref), channel_id=1, source_target_pairs={{0,1},{1,0},{2,3},{3,2},{4,5},{5,4},{6,7},{7,6},{8,9},{9,8},{10,11... | collective-permute-start | bytes 2359304 | tf_op jit(solution)/shard_map/ppermute | solution.py:33
  116.7 20.2 %collective-permute-start.20 = (bf16[128,3072]{1,0:T(8,128)(2,1)S(1)}, bf16[128,3072]{1,0:T(8,128)(2,1)S(1)}, u32[]{:S(2)}, u32[]{:S(2)}) collective-permute-start(bf16[128,3072]{1,0:T(8,128)(2,1)S(1)} %get-tuple-element.64), channel_id=1, source_target_pairs={{0,16},{16,0},{1,17},{17,1},{2,18},{18,2},{3,19},{19,3},{4,20},{20... | collective-permute-start | bytes 2359304 | tf_op jit(solution)/shard_map/ppermute | solution.py:33
  120.0 24.1 %collective-permute-start.19 = (bf16[256,1536]{1,0:T(8,128)(2,1)S(1)}, bf16[256,1536]{1,0:T(8,128)(2,1)S(1)}, u32[]{:S(2)}, u32[]{:S(2)}) collective-permute-start(bf16[256,1536]{1,0:T(8,128)(2,1)S(1)} %get-tuple-element.62.own_ref), channel_id=1, source_target_pairs={{0,1},{1,0},{2,3},{3,2},{4,5},{5,4},{6,7},{7,6},{8,9},{9,8},{10,11... | collective-permute-start | bytes 2359304 | tf_op jit(solution)/shard_map/ppermute | solution.py:33
  135.9 15.4 %collective-permute-start.23 = (bf16[128,3072]{1,0:T(8,128)(2,1)S(1)}, bf16[128,3072]{1,0:T(8,128)(2,1)S(1)}, u32[]{:S(2)}, u32[]{:S(2)}) collective-permute-start(bf16[128,3072]{1,0:T(8,128)(2,1)S(1)} %get-tuple-element.72), channel_id=1, source_target_pairs={{0,16},{16,0},{1,17},{17,1},{2,18},{18,2},{3,19},{19,3},{4,20},{20... | collective-permute-start | bytes 2359304 | tf_op jit(solution)/shard_map/ppermute | solution.py:33
  137.2 16.7 %collective-permute-start.24 = (bf16[128,3072]{1,0:T(8,128)(2,1)S(1)}, bf16[128,3072]{1,0:T(8,128)(2,1)S(1)}, u32[]{:S(2)}, u32[]{:S(2)}) collective-permute-start(bf16[128,3072]{1,0:T(8,128)(2,1)S(1)} %get-tuple-element.73), channel_id=1, source_target_pairs={{0,4},{2,6},{4,8},{6,10},{8,12},{10,14},{12,0},{14,2},{1,5},{3,7},... | collective-permute-start | bytes 2359304 | tf_op jit(solution)/shard_map/ppermute | solution.py:549
  138.5 16.0 %collective-permute-start.26 = (bf16[256,1664]{1,0:T(8,128)(2,1)S(1)}, bf16[256,1664]{1,0:T(8,128)(2,1)S(1)}, u32[]{:S(2)}, u32[]{:S(2)}) collective-permute-start(bf16[256,1664]{1,0:T(8,128)(2,1)S(1)} %shard_map.139.own_ref), channel_id=1, source_target_pairs={{0,2},{2,0},{4,6},{6,4},{8,10},{10,8},{12,14},{14,12},{1,3},{3,1},... | collective-permute-start | bytes 2555912 | tf_op jit(solution)/shard_map/ppermute | solution.py:693
  146.9 17.8 %collective-permute-start.22 = (bf16[128,3072]{1,0:T(8,128)(2,1)S(1)}, bf16[128,3072]{1,0:T(8,128)(2,1)S(1)}, u32[]{:S(2)}, u32[]{:S(2)}) collective-permute-start(bf16[128,3072]{1,0:T(8,128)(2,1)S(1)} %get-tuple-element.70), channel_id=1, source_target_pairs={{0,16},{16,0},{1,17},{17,1},{2,18},{18,2},{3,19},{19,3},{4,20},{20... | collective-permute-start | bytes 2359304 | tf_op jit(solution)/shard_map/ppermute | solution.py:33
  154.2 14.1 %collective-permute-start.25 = (bf16[128,3072]{1,0:T(8,128)(2,1)S(1)}, bf16[128,3072]{1,0:T(8,128)(2,1)S(1)}, u32[]{:S(2)}, u32[]{:S(2)}) collective-permute-start(bf16[128,3072]{1,0:T(8,128)(2,1)S(1)} %get-tuple-element.75), channel_id=1, source_target_pairs={{0,4},{2,6},{4,8},{6,10},{8,12},{10,14},{12,0},{14,2},{1,5},{3,7},... | collective-permute-start | bytes 2359304 | tf_op jit(solution)/shard_map/ppermute | solution.py:549
  169.3 13.7 %collective-permute-start.27 = (bf16[128,3072]{1,0:T(8,128)(2,1)S(1)}, bf16[128,3072]{1,0:T(8,128)(2,1)S(1)}, u32[]{:S(2)}, u32[]{:S(2)}) collective-permute-start(bf16[128,3072]{1,0:T(8,128)(2,1)S(1)} %get-tuple-element.78.rows_ref), channel_id=1, source_target_pairs={{0,16},{16,0},{1,17},{17,1},{2,18},{18,2},{3,19},{19,3},{4,20},{20... | collective-permute-start | bytes 2359304 | tf_op jit(solution)/shard_map/ppermute | solution.py:33
  172.8 13.8 %collective-permute-start.28 = (bf16[128,2048]{1,0:T(8,128)(2,1)S(1)}, bf16[128,2048]{1,0:T(8,128)(2,1)S(1)}, u32[]{:S(2)}, u32[]{:S(2)}) collective-permute-start(bf16[128,2048]{1,0:T(8,128)(2,1)S(1)} %shard_map.143.own_ref), channel_id=1, source_target_pairs={{0,1},{1,0},{2,3},{3,2},{4,5},{5,4},{6,7},{7,6},{8,9},{9,8},{10,11... | collective-permute-start | bytes 1572872 | tf_op jit(solution)/shard_map/ppermute | solution.py:33
  184.9 9.2 %collective-permute-start.29 = (bf16[128,2048]{1,0:T(8,128)(2,1)S(1)}, bf16[128,2048]{1,0:T(8,128)(2,1)S(1)}, u32[]{:S(2)}, u32[]{:S(2)}) collective-permute-start(bf16[128,2048]{1,0:T(8,128)(2,1)S(1)} %shard_map.145.own_ref), channel_id=1, source_target_pairs={{0,1},{1,0},{2,3},{3,2},{4,5},{5,4},{6,7},{7,6},{8,9},{9,8},{10,11... | collective-permute-start | bytes 1572872 | tf_op jit(solution)/shard_map/ppermute | solution.py:33
  188.5 9.6 %collective-permute-start.31 = (bf16[128,1152]{1,0:T(8,128)(2,1)S(1)}, bf16[128,1152]{1,0:T(8,128)(2,1)S(1)}, u32[]{:S(2)}, u32[]{:S(2)}) collective-permute-start(bf16[128,1152]{1,0:T(8,128)(2,1)S(1)} %get-tuple-element.84), channel_id=1, source_target_pairs={{0,16},{16,0},{1,17},{17,1},{2,18},{18,2},{3,19},{19,3},{4,20},{20... | collective-permute-start | bytes 884744 | tf_op jit(solution)/shard_map/ppermute | solution.py:33
  196.0 6.8 %collective-permute-start.30 = (bf16[128,1152]{1,0:T(8,128)(2,1)S(1)}, bf16[128,1152]{1,0:T(8,128)(2,1)S(1)}, u32[]{:S(2)}, u32[]{:S(2)}) collective-permute-start(bf16[128,1152]{1,0:T(8,128)(2,1)S(1)} %get-tuple-element.81), channel_id=1, source_target_pairs={{0,16},{16,0},{1,17},{17,1},{2,18},{18,2},{3,19},{19,3},{4,20},{20... | collective-permute-start | bytes 884744 | tf_op jit(solution)/shard_map/ppermute | solution.py:33
  204.7 6.9 %collective-permute-start.32 = (bf16[128,512]{1,0:T(8,128)(2,1)S(1)}, bf16[128,512]{1,0:T(8,128)(2,1)S(1)}, u32[]{:S(2)}, u32[]{:S(2)}) collective-permute-start(bf16[128,512]{1,0:T(8,128)(2,1)S(1)} %get-tuple-element.87), channel_id=1, source_target_pairs={{0,4},{2,6},{4,8},{6,10},{8,12},{10,14},{12,0},{14,2},{1,5},{3,7},... | collective-permute-start | bytes 393224 | tf_op jit(solution)/shard_map/ppermute | solution.py:549
  205.4 7.6 %collective-permute-start.33 = (bf16[128,512]{1,0:T(8,128)(2,1)S(1)}, bf16[128,512]{1,0:T(8,128)(2,1)S(1)}, u32[]{:S(2)}, u32[]{:S(2)}) collective-permute-start(bf16[128,512]{1,0:T(8,128)(2,1)S(1)} %get-tuple-element.88), channel_id=1, source_target_pairs={{0,8},{2,10},{4,12},{6,14},{8,0},{10,2},{12,4},{14,6},{1,9},{3,11}... | collective-permute-start | bytes 393224 | tf_op jit(solution)/shard_map/ppermute | solution.py:549
  (28 other events, 293.0 us)

commit v4 on v2

--- a/solution.py
+++ b/solution.py
@@ -665,32 +665,35 @@
     blocks[0] = halves_of(my_normed, normed)
     if fast:
         up_weights[-1] = held_call(up_weights[-1], token)
-    up(0)
+        token[:] = [up_weights[-1]]
     forwarded(2)
     messages.append(message_call(caption_lengths, word_kept, word_other, token))
     up(1, messages[0])
     hops()
     if fast:
         down_weights[-1] = held_call(down_weights[-1], token)
-    down(0)
     forwarded(3)
     up(2, blocks[places - 1][0], *messages[1:2])
     down(1)
     up(3)
+    back(1)
     down(2, *messages[2:])
-    back(1)
+    up(0, *[backs[step] for step in backs])
     for step in range(4, places):
         forwarded(step)
         up(step)
         down(step - 1)
     down(places - 1)
+    for step in range(2, places - 1):
+        back(step)
+    down(0)
     word_block = stack_call(messages)
     if cores == 2:
         word_blocks = [word_block, lax.ppermute(word_block, "grp", core_swap)]
     else:
         word_blocks = [word_block]
-    for step in range(2, places):
-        back(step)
+    if places > 2:
+        back(places - 1)
 
     home = [my_tokens, *outs[0], *([backs[places - 1]] if places > 1 else [])]
     cands = groups * cand_local

time: 220 us -> 224 us (1.018)
  waiting for transfers between devices: 121 us -> 126 us
    ppermute x12, waiting for transfers between devices: 33.8 us -> 53.2 us  [to_place(): lax.ppermute(value, 'grp', [(i, (i + step * cores) % groups) for i in ran...]
    ppermute x22, waiting for transfers between devices: 85.5 us -> 72.2 us  [shifted(): lax.ppermute(value, axis, [(i, (i + step) % count) for i in range(count)])]
  transfers between devices with their start and end apart: 39 -> 39, of which waited for: 26 -> 23; matrix products, arithmetic and copies ran while one was open for 3% -> 3% of each run, Pallas kernels for 18% -> 18%
where the time goes in v4:
time: 224 us
  waiting for transfers between devices  126 us (56%)
  Pallas kernels  44.1 us (20%)
  starting transfers between devices  39 us (17%)
  local copies, waits for them, and re-layouts  7.11 us (3%)
  other arithmetic  6.85 us (3%)
    ppermute x22, waiting for transfers between devices, shifted(): lax.ppermute(value, axis, [(i, (i + step) % count) for i in range(count)])  72.2 us
    ppermute x12, waiting for transfers between devices, to_place(): lax.ppermute(value, 'grp', [(i, (i + step * cores) % groups) for i in ran...  53.2 us
    ppermute x22, starting transfers between devices, shifted(): lax.ppermute(value, axis, [(i, (i + step) % count) for i in range(count)])  24.9 us
    ppermute x12, starting transfers between devices, to_place(): lax.ppermute(value, 'grp', [(i, (i + step * cores) % groups) for i in ran...  12.6 us
    pallas_call x4, Pallas kernels, down_call(): pl.pallas_call(functools.partial(down_kernel, cores), in_specs=[VMEM] * (...  11.1 us
    pallas_call x4, Pallas kernels, up_call(): pl.pallas_call(functools.partial(up_kernel, cores), in_specs=[VMEM] * (2...  10.6 us
    unnamed x42, local copies, waits for them, and re-layouts  6.86 us
    pallas_call x3, Pallas kernels, held_call(): pl.pallas_call(hold_kernel, in_specs=[HBM] * (1 + len(after)), out_specs=...  5.13 us
  transfers between devices with their start and end apart: 39, of which 23 were waited for; matrix products, arithmetic and copies ran while one was open for 3% of the time, Pallas kernels for 18%

profile of v4, /device:TPU:0, one launch (start us, length us, event | category | flops | bytes accessed | tf_op | source)
XLA Modules:
  0.0 224.2 jit_solution(9377715517373753178)
XLA Ops:
  4.8 3.0 %collective-permute-start = (f32[2,256]{1,0:T(2,128)S(1)}, f32[2,256]{1,0:T(2,128)S(1)}, u32[]{:S(2)}, u32[]{:S(2)}) collective-permute-start(f32[2,256]{1,0:T(2,128)S(1)} %pad_maximum_fusion.1), channel_id=1, source_target_pairs={{0,1},{1,0},{2,3},{3,2},{4,5},{5,4},{6,7},{7,6},{8,9},{9,8},{10,11... | collective-permute-start | bytes 6152 | tf_op jit(solution)/shard_map/ppermute | solution.py:33
  14.9 17.5 %collective-permute-done.4.mine_ref = bf16[128,3072]{1,0:T(8,128)(2,1)S(1)} collective-permute-done((bf16[128,3072]{1,0:T(8,128)(2,1)S(1)}, bf16[128,3072]{1,0:T(8,128)(2,1)S(1)}, u32[]{:S(2)}, u32[]{:S(2)}) %collective-permute-start.4) | collective-permute-done | bytes 786464 | tf_op jit(solution)/shard_map/ppermute | solution.py:549
  34.1 4.6 %copy-done = bf16[3,2048,1024]{2,1,0:T(8,128)(2,1)S(1)} copy-done((bf16[3,2048,1024]{2,1,0:T(8,128)(2,1)S(1)}, bf16[3,2048,1024]{2,1,0:T(8,128)(2,1)}, u32[]{:S(2)}) %copy-start) | copy-done | bytes 12582936
  38.7 2.9 %shard_map.122 = (bf16[64,1536]{1,0:T(8,128)(2,1)S(1)}, f32[64,1536]{1,0:T(8,128)S(1)}, f32[8,128]{1,0:T(8,128)S(1)}) custom-call(s32[5]{0:T(128)S(1)} %stack.35.vis_ref.spots_ref, bf16[64,2048]{1,0:T(8,128)(2,1)S(1)} %bitcast.41, bf16[3,2048,1024]{2,1,0:T(8,128)(2,1)S(1)} %copy-done, bf16[128,3072]{1,0:T(8,128)(2,1)S(1)} %get-tuple-element.95.refs_0_.mine_ref, ...), custom_call_target="tpu_custom_call" | custom-call | flops 1024 | bytes 1024 | tf_op jit(solution)/shard_map/pallas_call | solution.py:257
  42.1 2.5 %shard_map.123.token_ref.refs_0_.refs_1_.refs_2_ = bf16[3072,768]{1,0:T(8,128)(2,1)S(1)} custom-call(bf16[3072,768]{1,0:T(8,128)(2,1)} %collective-permute-done.1.value_ref, f32[8,128]{1,0:T(8,128)S(1)} %get-tuple-element.48.refs_0_), custom_call_target="tpu_custom_call" | custom-call | flops 1024 | bytes 1024 | tf_op jit(solution)/shard_map/pallas_call | solution.py:88
  44.7 6.8 %collective-permute-done.5.value_ref = bf16[128,3072]{1,0:T(8,128)(2,1)S(1)} collective-permute-done((bf16[128,3072]{1,0:T(8,128)(2,1)S(1)}, bf16[128,3072]{1,0:T(8,128)(2,1)S(1)}, u32[]{:S(2)}, u32[]{:S(2)}) %collective-permute-start.5) | collective-permute-done | bytes 786464 | tf_op jit(solution)/shard_map/ppermute | solution.py:549
  52.9 3.8 %collective-permute-done.8.other_ref = bf16[64,1536]{1,0:T(8,128)(2,1)S(1)} collective-permute-done((bf16[64,1536]{1,0:T(8,128)(2,1)S(1)}, bf16[64,1536]{1,0:T(8,128)(2,1)S(1)}, u32[]{:S(2)}, u32[]{:S(2)}) %collective-permute-start.8) | collective-permute-done | bytes 196640 | tf_op jit(solution)/shard_map/ppermute | solution.py:33
  57.4 2.6 %shard_map.126 = (bf16[256,1536]{1,0:T(8,128)(2,1)S(1)}, f32[8,128]{1,0:T(8,128)S(1)}) custom-call(bf16[128,3072]{1,0:T(8,128)(2,1)S(1)} %collective-permute-done.4.mine_ref, bf16[128,3072]{1,0:T(8,128)(2,1)S(1)} %collective-permute-done.7.theirs_ref, bf16[3072,768]{1,0:T(8,128)(2,1)S(1)} %bitcast.36, ...), custom_call_target="tpu_custom_call" | custom-call | flops 1024 | bytes 1024 | tf_op jit(solution)/shard_map/pallas_call | solution.py:118
  62.3 2.3 %shard_map.129.refs_1_ = bf16[768,3072]{1,0:T(8,128)(2,1)S(1)} custom-call(bf16[768,3072]{1,0:T(8,128)(2,1)} %collective-permute-done.12.value_ref, f32[8,128]{1,0:T(8,128)S(1)} %get-tuple-element.51.token_ref.refs_2_.refs_0_), custom_call_target="tpu_custom_call" | custom-call | flops 1024 | bytes 1024 | tf_op jit(solution)/shard_map/pallas_call | solution.py:88
  64.6 8.4 %collective-permute-done.9.value_ref = bf16[128,3072]{1,0:T(8,128)(2,1)S(1)} collective-permute-done((bf16[128,3072]{1,0:T(8,128)(2,1)S(1)}, bf16[128,3072]{1,0:T(8,128)(2,1)S(1)}, u32[]{:S(2)}, u32[]{:S(2)}) %collective-permute-start.9) | collective-permute-done | bytes 786464 | tf_op jit(solution)/shard_map/ppermute | solution.py:549
  75.4 2.6 %shard_map.128 = (bf16[256,1536]{1,0:T(8,128)(2,1)S(1)}, f32[8,128]{1,0:T(8,128)S(1)}) custom-call(bf16[128,3072]{1,0:T(8,128)(2,1)S(1)} %shard_map.124.mine_ref, bf16[128,3072]{1,0:T(8,128)(2,1)S(1)} %collective-permute-done.6.theirs_ref, bf16[3072,768]{1,0:T(8,128)(2,1)S(1)} %bitcast.36, ...), custom_call_target="tpu_custom_call" | custom-call | flops 1024 | bytes 1024 | tf_op jit(solution)/shard_map/pallas_call | solution.py:118
  78.0 2.8 %shard_map.130 = (bf16[128,3072]{1,0:T(8,128)(2,1)S(1)}, bf16[128,3072]{1,0:T(8,128)(2,1)S(1)}, f32[8,128]{1,0:T(8,128)S(1)}) custom-call(bf16[256,1536]{1,0:T(8,128)(2,1)S(1)} %get-tuple-element.53.own_ref, bf16[256,1536]{1,0:T(8,128)(2,1)S(1)} %collective-permute-done.13.other_ref, bf16[768,3072]{1,0:T(8,128)(2,1)S(1)} %bitcast.34, ...), custom_call_target="tpu_custom_call" | custom-call | flops 1024 | bytes 1024 | tf_op jit(solution)/shard_map/pallas_call | solution.py:169
  82.3 3.0 %collective-permute-start.17 = (bf16[64,1664]{1,0:T(8,128)(2,1)S(1)}, bf16[64,1664]{1,0:T(8,128)(2,1)S(1)}, u32[]{:S(2)}, u32[]{:S(2)}) collective-permute-start(bf16[64,1664]{1,0:T(8,128)(2,1)S(1)} %shard_map.125.refs_3_.refs_0_), channel_id=1, source_target_pairs={{0,12},{2,14},{4,0},{6,2},{8,4},{10,6},{12,8},{14,10},{1,13},{3,15... | collective-permute-start | bytes 638984 | tf_op jit(solution)/shard_map/ppermute | solution.py:549
  85.3 8.2 %collective-permute-done.15.theirs_ref = bf16[128,3072]{1,0:T(8,128)(2,1)S(1)} collective-permute-done((bf16[128,3072]{1,0:T(8,128)(2,1)S(1)}, bf16[128,3072]{1,0:T(8,128)(2,1)S(1)}, u32[]{:S(2)}, u32[]{:S(2)}) %collective-permute-start.15) | collective-permute-done | bytes 786464 | tf_op jit(solution)/shard_map/ppermute | solution.py:33
  93.6 2.6 %shard_map.131 = (bf16[256,1536]{1,0:T(8,128)(2,1)S(1)}, f32[8,128]{1,0:T(8,128)S(1)}) custom-call(bf16[128,3072]{1,0:T(8,128)(2,1)S(1)} %shard_map.127.refs_3_.mine_ref, bf16[128,3072]{1,0:T(8,128)(2,1)S(1)} %collective-permute-done.15.theirs_ref, bf16[3072,768]{1,0:T(8,128)(2,1)S(1)} %bitcast.36, ...), custom_call_target="tpu_custom_call" | custom-call | flops 1024 | bytes 1024 | tf_op jit(solution)/shard_map/pallas_call | solution.py:118
  96.2 8.2 %collective-permute-done.14.refs_1_ = bf16[128,3072]{1,0:T(8,128)(2,1)S(1)} collective-permute-done((bf16[128,3072]{1,0:T(8,128)(2,1)S(1)}, bf16[128,3072]{1,0:T(8,128)(2,1)S(1)}, u32[]{:S(2)}, u32[]{:S(2)}) %collective-permute-start.14) | collective-permute-done | bytes 786464 | tf_op jit(solution)/shard_map/ppermute | solution.py:33
  106.1 2.8 %shard_map.133 = (bf16[128,3072]{1,0:T(8,128)(2,1)S(1)}, bf16[128,3072]{1,0:T(8,128)(2,1)S(1)}, f32[8,128]{1,0:T(8,128)S(1)}) custom-call(bf16[256,1536]{1,0:T(8,128)(2,1)S(1)} %get-tuple-element.52.own_ref, bf16[256,1536]{1,0:T(8,128)(2,1)S(1)} %collective-permute-done.11.other_ref, bf16[768,3072]{1,0:T(8,128)(2,1)S(1)} %bitcast.34, ...), custom_call_target="tpu_custom_call" | custom-call | flops 1024 | bytes 1024 | tf_op jit(solution)/shard_map/pallas_call | solution.py:169
  110.5 12.0 %collective-permute-done.18.refs_3_.refs_2_ = bf16[128,3072]{1,0:T(8,128)(2,1)S(1)} collective-permute-done((bf16[128,3072]{1,0:T(8,128)(2,1)S(1)}, bf16[128,3072]{1,0:T(8,128)(2,1)S(1)}, u32[]{:S(2)}, u32[]{:S(2)}) %collective-permute-start.18) | collective-permute-done | bytes 786464 | tf_op jit(solution)/shard_map/ppermute | solution.py:549
  122.5 2.7 %shard_map.134 = (bf16[256,1536]{1,0:T(8,128)(2,1)S(1)}, f32[8,128]{1,0:T(8,128)S(1)}) custom-call(bf16[128,3072]{1,0:T(8,128)(2,1)S(1)} %get-tuple-element.95.refs_0_.mine_ref, bf16[128,3072]{1,0:T(8,128)(2,1)S(1)} %get-tuple-element.94.theirs_ref, bf16[3072,768]{1,0:T(8,128)(2,1)S(1)} %bitcast.36, ...), custom_call_target="tpu_custom_call" | custom-call | flops 1024 | bytes 1024 | tf_op jit(solution)/shard_map/pallas_call | solution.py:118
  126.2 2.8 %shard_map.135 = (bf16[128,3072]{1,0:T(8,128)(2,1)S(1)}, bf16[128,3072]{1,0:T(8,128)(2,1)S(1)}, f32[8,128]{1,0:T(8,128)S(1)}) custom-call(bf16[256,1536]{1,0:T(8,128)(2,1)S(1)} %get-tuple-element.65.own_ref, bf16[256,1536]{1,0:T(8,128)(2,1)S(1)} %collective-permute-done.21.other_ref, bf16[768,3072]{1,0:T(8,128)(2,1)S(1)} %bitcast.34, ...), custom_call_target="tpu_custom_call" | custom-call | flops 1024 | bytes 1024 | tf_op jit(solution)/shard_map/pallas_call | solution.py:169
  130.6 9.7 %collective-permute-done.19.other_ref = bf16[256,1536]{1,0:T(8,128)(2,1)S(1)} collective-permute-done((bf16[256,1536]{1,0:T(8,128)(2,1)S(1)}, bf16[256,1536]{1,0:T(8,128)(2,1)S(1)}, u32[]{:S(2)}, u32[]{:S(2)}) %collective-permute-start.19) | collective-permute-done | bytes 786464 | tf_op jit(solution)/shard_map/ppermute | solution.py:33
  140.4 2.8 %shard_map.137 = (bf16[128,3072]{1,0:T(8,128)(2,1)S(1)}, bf16[128,3072]{1,0:T(8,128)(2,1)S(1)}, f32[8,128]{1,0:T(8,128)S(1)}) custom-call(bf16[256,1536]{1,0:T(8,128)(2,1)S(1)} %get-tuple-element.62.own_ref, bf16[256,1536]{1,0:T(8,128)(2,1)S(1)} %collective-permute-done.19.other_ref, bf16[768,3072]{1,0:T(8,128)(2,1)S(1)} %bitcast.34, ...), custom_call_target="tpu_custom_call" | custom-call | flops 1024 | bytes 1024 | tf_op jit(solution)/shard_map/pallas_call | solution.py:169
  144.7 2.8 %collective-permute-done.23.refs_1_ = bf16[128,3072]{1,0:T(8,128)(2,1)S(1)} collective-permute-done((bf16[128,3072]{1,0:T(8,128)(2,1)S(1)}, bf16[128,3072]{1,0:T(8,128)(2,1)S(1)}, u32[]{:S(2)}, u32[]{:S(2)}) %collective-permute-start.23) | collective-permute-done | bytes 786464 | tf_op jit(solution)/shard_map/ppermute | solution.py:33
  149.6 11.3 %collective-permute-done.22.refs_2_ = bf16[128,3072]{1,0:T(8,128)(2,1)S(1)} collective-permute-done((bf16[128,3072]{1,0:T(8,128)(2,1)S(1)}, bf16[128,3072]{1,0:T(8,128)(2,1)S(1)}, u32[]{:S(2)}, u32[]{:S(2)}) %collective-permute-start.22) | collective-permute-done | bytes 786464 | tf_op jit(solution)/shard_map/ppermute | solution.py:33
  160.9 2.7 %collective-permute-done.25.refs_3_ = bf16[128,3072]{1,0:T(8,128)(2,1)S(1)} collective-permute-done((bf16[128,3072]{1,0:T(8,128)(2,1)S(1)}, bf16[128,3072]{1,0:T(8,128)(2,1)S(1)}, u32[]{:S(2)}, u32[]{:S(2)}) %collective-permute-start.25) | collective-permute-done | bytes 786464 | tf_op jit(solution)/shard_map/ppermute | solution.py:549
  168.7 9.3 %collective-permute-done.27.rows_ref = bf16[128,3072]{1,0:T(8,128)(2,1)S(1)} collective-permute-done((bf16[128,3072]{1,0:T(8,128)(2,1)S(1)}, bf16[128,3072]{1,0:T(8,128)(2,1)S(1)}, u32[]{:S(2)}, u32[]{:S(2)}) %collective-permute-start.27) | collective-permute-done | bytes 786464 | tf_op jit(solution)/shard_map/ppermute | solution.py:33
  184.3 4.9 %collective-permute-done.29.other_ref = bf16[128,2048]{1,0:T(8,128)(2,1)S(1)} collective-permute-done((bf16[128,2048]{1,0:T(8,128)(2,1)S(1)}, bf16[128,2048]{1,0:T(8,128)(2,1)S(1)}, u32[]{:S(2)}, u32[]{:S(2)}) %collective-permute-start.29) | collective-permute-done | bytes 524320 | tf_op jit(solution)/shard_map/ppermute | solution.py:33
  192.9 4.9 %collective-permute-done.30.refs_1_ = bf16[128,1152]{1,0:T(8,128)(2,1)S(1)} collective-permute-done((bf16[128,1152]{1,0:T(8,128)(2,1)S(1)}, bf16[128,1152]{1,0:T(8,128)(2,1)S(1)}, u32[]{:S(2)}, u32[]{:S(2)}) %collective-permute-start.30) | collective-permute-done | bytes 294944 | tf_op jit(solution)/shard_map/ppermute | solution.py:33
  199.8 2.3 %collective-permute-start.33 = (bf16[128,512]{1,0:T(8,128)(2,1)S(1)}, bf16[128,512]{1,0:T(8,128)(2,1)S(1)}, u32[]{:S(2)}, u32[]{:S(2)}) collective-permute-start(bf16[128,512]{1,0:T(8,128)(2,1)S(1)} %get-tuple-element.88), channel_id=1, source_target_pairs={{0,8},{2,10},{4,12},{6,14},{8,0},{10,2},{12,4},{14,6},{1,9},{3,11}... | collective-permute-start | bytes 393224 | tf_op jit(solution)/shard_map/ppermute | solution.py:549
  202.1 2.6 %collective-permute-start.34 = (bf16[128,512]{1,0:T(8,128)(2,1)S(1)}, bf16[128,512]{1,0:T(8,128)(2,1)S(1)}, u32[]{:S(2)}, u32[]{:S(2)}) collective-permute-start(bf16[128,512]{1,0:T(8,128)(2,1)S(1)} %get-tuple-element.89), channel_id=1, source_target_pairs={{0,12},{2,14},{4,0},{6,2},{8,4},{10,6},{12,8},{14,10},{1,13},{3,15... | collective-permute-start | bytes 393224 | tf_op jit(solution)/shard_map/ppermute | solution.py:549
  210.6 3.0 %collective-permute-done.36.vis_ref = bf16[64,512]{1,0:T(8,128)(2,1)S(1)} collective-permute-done((bf16[64,512]{1,0:T(8,128)(2,1)S(1)}, bf16[64,512]{1,0:T(8,128)(2,1)S(1)}, u32[]{:S(2)}, u32[]{:S(2)}) %collective-permute-start.36) | collective-permute-done | bytes 65568 | tf_op jit(solution)/shard_map/ppermute | solution.py:33
  220.6 2.8 %collective-permute-done.38 = bf16[32,2048]{1,0:T(8,128)(2,1)S(1)} collective-permute-done((bf16[32,2048]{1,0:T(8,128)(2,1)S(1)}, bf16[32,2048]{1,0:T(8,128)(2,1)S(1)}, u32[]{:S(2)}, u32[]{:S(2)}) %collective-permute-start.38) | collective-permute-done | bytes 131104 | tf_op jit(solution)/shard_map/ppermute | solution.py:33
  (137 shorter events, 61.5 us)
Async XLA Ops:
  0.7 41.5 %collective-permute-start.1 = (bf16[3072,768]{1,0:T(8,128)(2,1)}, bf16[3072,768]{1,0:T(8,128)(2,1)}, u32[]{:S(2)}, u32[]{:S(2)}) collective-permute-start(bf16[3072,768]{1,0:T(8,128)(2,1)} %refs_0_.13), channel_id=1, source_target_pairs={{0,2},{2,0},{4,6},{6,4},{8,10},{10,8},{12,14},{14,12},{1,3},{3,1},... | collective-permute-start | bytes 14155784 | tf_op jit(solution)/shard_map/ppermute | solution.py:542
  1.2 61.1 %collective-permute-start.12 = (bf16[768,3072]{1,0:T(8,128)(2,1)}, bf16[768,3072]{1,0:T(8,128)(2,1)}, u32[]{:S(2)}, u32[]{:S(2)}) collective-permute-start(bf16[768,3072]{1,0:T(8,128)(2,1)} %refs_0_.15), channel_id=1, source_target_pairs={{0,2},{2,0},{4,6},{6,4},{8,10},{10,8},{12,14},{14,12},{1,3},{3,1},... | collective-permute-start | bytes 14155784 | tf_op jit(solution)/shard_map/ppermute | solution.py:543
  12.4 20.0 %collective-permute-start.4 = (bf16[128,3072]{1,0:T(8,128)(2,1)S(1)}, bf16[128,3072]{1,0:T(8,128)(2,1)S(1)}, u32[]{:S(2)}, u32[]{:S(2)}) collective-permute-start(bf16[128,3072]{1,0:T(8,128)(2,1)S(1)} %get-tuple-element.95.refs_0_.mine_ref), channel_id=1, source_target_pairs={{0,4},{2,6},{4,8},{6,10},{8,12},{10,14},{12,0},{14,2},{1,5},{3,7},... | collective-permute-start | bytes 2359304 | tf_op jit(solution)/shard_map/ppermute | solution.py:549
  14.1 19.8 %collective-permute-start.3 = (bf16[4,8,2048]{2,1,0:T(8,128)(2,1)S(1)}, bf16[4,8,2048]{2,1,0:T(8,128)(2,1)S(1)}, u32[]{:S(2)}, u32[]{:S(2)}) collective-permute-start(bf16[4,8,2048]{2,1,0:T(8,128)(2,1)S(1)} %fusion.8), channel_id=1, source_target_pairs={{0,1},{1,0},{2,3},{3,2},{4,5},{5,4},{6,7},{7,6},{8,9},{9,8},{10,11... | collective-permute-start | bytes 393224 | tf_op jit(solution)/shard_map/ppermute | solution.py:33
  32.4 19.0 %collective-permute-start.5 = (bf16[128,3072]{1,0:T(8,128)(2,1)S(1)}, bf16[128,3072]{1,0:T(8,128)(2,1)S(1)}, u32[]{:S(2)}, u32[]{:S(2)}) collective-permute-start(bf16[128,3072]{1,0:T(8,128)(2,1)S(1)} %collective-permute-done.4.mine_ref), channel_id=1, source_target_pairs={{0,4},{2,6},{4,8},{6,10},{8,12},{10,14},{12,0},{14,2},{1,5},{3,7},... | collective-permute-start | bytes 2359304 | tf_op jit(solution)/shard_map/ppermute | solution.py:549
  32.4 24.9 %collective-permute-start.7 = (bf16[128,3072]{1,0:T(8,128)(2,1)S(1)}, bf16[128,3072]{1,0:T(8,128)(2,1)S(1)}, u32[]{:S(2)}, u32[]{:S(2)}) collective-permute-start(bf16[128,3072]{1,0:T(8,128)(2,1)S(1)} %collective-permute-done.4.mine_ref), channel_id=1, source_target_pairs={{0,16},{16,0},{1,17},{17,1},{2,18},{18,2},{3,19},{19,3},{4,20},{20... | collective-permute-start | bytes 2359304 | tf_op jit(solution)/shard_map/ppermute | solution.py:33
  41.5 15.2 %collective-permute-start.8 = (bf16[64,1536]{1,0:T(8,128)(2,1)S(1)}, bf16[64,1536]{1,0:T(8,128)(2,1)S(1)}, u32[]{:S(2)}, u32[]{:S(2)}) collective-permute-start(bf16[64,1536]{1,0:T(8,128)(2,1)S(1)} %get-tuple-element.50), channel_id=1, source_target_pairs={{0,16},{16,0},{1,17},{17,1},{2,18},{18,2},{3,19},{19,3},{4,20},{20... | collective-permute-start | bytes 589832 | tf_op jit(solution)/shard_map/ppermute | solution.py:33
  51.5 23.9 %collective-permute-start.6 = (bf16[128,3072]{1,0:T(8,128)(2,1)S(1)}, bf16[128,3072]{1,0:T(8,128)(2,1)S(1)}, u32[]{:S(2)}, u32[]{:S(2)}) collective-permute-start(bf16[128,3072]{1,0:T(8,128)(2,1)S(1)} %shard_map.124.mine_ref), channel_id=1, source_target_pairs={{0,16},{16,0},{1,17},{17,1},{2,18},{18,2},{3,19},{19,3},{4,20},{20... | collective-permute-start | bytes 2359304 | tf_op jit(solution)/shard_map/ppermute | solution.py:33
  52.9 20.1 %collective-permute-start.9 = (bf16[128,3072]{1,0:T(8,128)(2,1)S(1)}, bf16[128,3072]{1,0:T(8,128)(2,1)S(1)}, u32[]{:S(2)}, u32[]{:S(2)}) collective-permute-start(bf16[128,3072]{1,0:T(8,128)(2,1)S(1)} %shard_map.124.mine_ref), channel_id=1, source_target_pairs={{0,4},{2,6},{4,8},{6,10},{8,12},{10,14},{12,0},{14,2},{1,5},{3,7},... | collective-permute-start | bytes 2359304 | tf_op jit(solution)/shard_map/ppermute | solution.py:549
  60.0 17.9 %collective-permute-start.13 = (bf16[256,1536]{1,0:T(8,128)(2,1)S(1)}, bf16[256,1536]{1,0:T(8,128)(2,1)S(1)}, u32[]{:S(2)}, u32[]{:S(2)}) collective-permute-start(bf16[256,1536]{1,0:T(8,128)(2,1)S(1)} %get-tuple-element.53.own_ref), channel_id=1, source_target_pairs={{0,1},{1,0},{2,3},{3,2},{4,5},{5,4},{6,7},{7,6},{8,9},{9,8},{10,11... | collective-permute-start | bytes 2359304 | tf_op jit(solution)/shard_map/ppermute | solution.py:33
  60.6 14.7 %collective-permute-start.10 = (bf16[64,1664]{1,0:T(8,128)(2,1)S(1)}, bf16[64,1664]{1,0:T(8,128)(2,1)S(1)}, u32[]{:S(2)}, u32[]{:S(2)}) collective-permute-start(bf16[64,1664]{1,0:T(8,128)(2,1)S(1)} %shard_map.125.refs_3_.refs_0_), channel_id=1, source_target_pairs={{0,4},{2,6},{4,8},{6,10},{8,12},{10,14},{12,0},{14,2},{1,5},{3,7},... | collective-permute-start | bytes 638984 | tf_op jit(solution)/shard_map/ppermute | solution.py:549
  73.1 20.5 %collective-permute-start.15 = (bf16[128,3072]{1,0:T(8,128)(2,1)S(1)}, bf16[128,3072]{1,0:T(8,128)(2,1)S(1)}, u32[]{:S(2)}, u32[]{:S(2)}) collective-permute-start(bf16[128,3072]{1,0:T(8,128)(2,1)S(1)} %shard_map.127.refs_3_.mine_ref), channel_id=1, source_target_pairs={{0,16},{16,0},{1,17},{17,1},{2,18},{18,2},{3,19},{19,3},{4,20},{20... | collective-permute-start | bytes 2359304 | tf_op jit(solution)/shard_map/ppermute | solution.py:33
  80.8 23.6 %collective-permute-start.14 = (bf16[128,3072]{1,0:T(8,128)(2,1)S(1)}, bf16[128,3072]{1,0:T(8,128)(2,1)S(1)}, u32[]{:S(2)}, u32[]{:S(2)}) collective-permute-start(bf16[128,3072]{1,0:T(8,128)(2,1)S(1)} %get-tuple-element.56), channel_id=1, source_target_pairs={{0,16},{16,0},{1,17},{17,1},{2,18},{18,2},{3,19},{19,3},{4,20},{20... | collective-permute-start | bytes 2359304 | tf_op jit(solution)/shard_map/ppermute | solution.py:33
  81.4 24.7 %collective-permute-start.11 = (bf16[256,1536]{1,0:T(8,128)(2,1)S(1)}, bf16[256,1536]{1,0:T(8,128)(2,1)S(1)}, u32[]{:S(2)}, u32[]{:S(2)}) collective-permute-start(bf16[256,1536]{1,0:T(8,128)(2,1)S(1)} %get-tuple-element.52.own_ref), channel_id=1, source_target_pairs={{0,1},{1,0},{2,3},{3,2},{4,5},{5,4},{6,7},{7,6},{8,9},{9,8},{10,11... | collective-permute-start | bytes 2359304 | tf_op jit(solution)/shard_map/ppermute | solution.py:33
  82.3 23.8 %collective-permute-start.17 = (bf16[64,1664]{1,0:T(8,128)(2,1)S(1)}, bf16[64,1664]{1,0:T(8,128)(2,1)S(1)}, u32[]{:S(2)}, u32[]{:S(2)}) collective-permute-start(bf16[64,1664]{1,0:T(8,128)(2,1)S(1)} %shard_map.125.refs_3_.refs_0_), channel_id=1, source_target_pairs={{0,12},{2,14},{4,0},{6,2},{8,4},{10,6},{12,8},{14,10},{1,13},{3,15... | collective-permute-start | bytes 638984 | tf_op jit(solution)/shard_map/ppermute | solution.py:549
  85.3 20.8 %collective-permute-start.16 = (bf16[64,1664]{1,0:T(8,128)(2,1)S(1)}, bf16[64,1664]{1,0:T(8,128)(2,1)S(1)}, u32[]{:S(2)}, u32[]{:S(2)}) collective-permute-start(bf16[64,1664]{1,0:T(8,128)(2,1)S(1)} %collective-permute-done.10.refs_4_.refs_1_), channel_id=1, source_target_pairs={{0,4},{2,6},{4,8},{6,10},{8,12},{10,14},{12,0},{14,2},{1,5},{3,7},... | collective-permute-start | bytes 638984 | tf_op jit(solution)/shard_map/ppermute | solution.py:549
  104.6 17.9 %collective-permute-start.18 = (bf16[128,3072]{1,0:T(8,128)(2,1)S(1)}, bf16[128,3072]{1,0:T(8,128)(2,1)S(1)}, u32[]{:S(2)}, u32[]{:S(2)}) collective-permute-start(bf16[128,3072]{1,0:T(8,128)(2,1)S(1)} %get-tuple-element.61), channel_id=1, source_target_pairs={{0,4},{2,6},{4,8},{6,10},{8,12},{10,14},{12,0},{14,2},{1,5},{3,7},... | collective-permute-start | bytes 2359304 | tf_op jit(solution)/shard_map/ppermute | solution.py:549
  105.6 20.6 %collective-permute-start.21 = (bf16[256,1536]{1,0:T(8,128)(2,1)S(1)}, bf16[256,1536]{1,0:T(8,128)(2,1)S(1)}, u32[]{:S(2)}, u32[]{:S(2)}) collective-permute-start(bf16[256,1536]{1,0:T(8,128)(2,1)S(1)} %get-tuple-element.65.own_ref), channel_id=1, source_target_pairs={{0,1},{1,0},{2,3},{3,2},{4,5},{5,4},{6,7},{7,6},{8,9},{9,8},{10,11... | collective-permute-start | bytes 2359304 | tf_op jit(solution)/shard_map/ppermute | solution.py:33
  108.9 21.2 %collective-permute-start.20 = (bf16[128,3072]{1,0:T(8,128)(2,1)S(1)}, bf16[128,3072]{1,0:T(8,128)(2,1)S(1)}, u32[]{:S(2)}, u32[]{:S(2)}) collective-permute-start(bf16[128,3072]{1,0:T(8,128)(2,1)S(1)} %get-tuple-element.64), channel_id=1, source_target_pairs={{0,16},{16,0},{1,17},{17,1},{2,18},{18,2},{3,19},{19,3},{4,20},{20... | collective-permute-start | bytes 2359304 | tf_op jit(solution)/shard_map/ppermute | solution.py:33
  125.2 15.2 %collective-permute-start.19 = (bf16[256,1536]{1,0:T(8,128)(2,1)S(1)}, bf16[256,1536]{1,0:T(8,128)(2,1)S(1)}, u32[]{:S(2)}, u32[]{:S(2)}) collective-permute-start(bf16[256,1536]{1,0:T(8,128)(2,1)S(1)} %get-tuple-element.62.own_ref), channel_id=1, source_target_pairs={{0,1},{1,0},{2,3},{3,2},{4,5},{5,4},{6,7},{7,6},{8,9},{9,8},{10,11... | collective-permute-start | bytes 2359304 | tf_op jit(solution)/shard_map/ppermute | solution.py:33
  129.0 18.6 %collective-permute-start.23 = (bf16[128,3072]{1,0:T(8,128)(2,1)S(1)}, bf16[128,3072]{1,0:T(8,128)(2,1)S(1)}, u32[]{:S(2)}, u32[]{:S(2)}) collective-permute-start(bf16[128,3072]{1,0:T(8,128)(2,1)S(1)} %get-tuple-element.72), channel_id=1, source_target_pairs={{0,16},{16,0},{1,17},{17,1},{2,18},{18,2},{3,19},{19,3},{4,20},{20... | collective-permute-start | bytes 2359304 | tf_op jit(solution)/shard_map/ppermute | solution.py:33
  130.4 17.2 %collective-permute-start.24 = (bf16[128,3072]{1,0:T(8,128)(2,1)S(1)}, bf16[128,3072]{1,0:T(8,128)(2,1)S(1)}, u32[]{:S(2)}, u32[]{:S(2)}) collective-permute-start(bf16[128,3072]{1,0:T(8,128)(2,1)S(1)} %get-tuple-element.73), channel_id=1, source_target_pairs={{0,4},{2,6},{4,8},{6,10},{8,12},{10,14},{12,0},{14,2},{1,5},{3,7},... | collective-permute-start | bytes 2359304 | tf_op jit(solution)/shard_map/ppermute | solution.py:549
  130.6 17.6 %collective-permute-start.26 = (bf16[256,1664]{1,0:T(8,128)(2,1)S(1)}, bf16[256,1664]{1,0:T(8,128)(2,1)S(1)}, u32[]{:S(2)}, u32[]{:S(2)}) collective-permute-start(bf16[256,1664]{1,0:T(8,128)(2,1)S(1)} %shard_map.139.own_ref), channel_id=1, source_target_pairs={{0,2},{2,0},{4,6},{6,4},{8,10},{10,8},{12,14},{14,12},{1,3},{3,1},... | collective-permute-start | bytes 2555912 | tf_op jit(solution)/shard_map/ppermute | solution.py:692
  143.2 17.8 %collective-permute-start.22 = (bf16[128,3072]{1,0:T(8,128)(2,1)S(1)}, bf16[128,3072]{1,0:T(8,128)(2,1)S(1)}, u32[]{:S(2)}, u32[]{:S(2)}) collective-permute-start(bf16[128,3072]{1,0:T(8,128)(2,1)S(1)} %get-tuple-element.70), channel_id=1, source_target_pairs={{0,16},{16,0},{1,17},{17,1},{2,18},{18,2},{3,19},{19,3},{4,20},{20... | collective-permute-start | bytes 2359304 | tf_op jit(solution)/shard_map/ppermute | solution.py:33
  147.9 15.8 %collective-permute-start.25 = (bf16[128,3072]{1,0:T(8,128)(2,1)S(1)}, bf16[128,3072]{1,0:T(8,128)(2,1)S(1)}, u32[]{:S(2)}, u32[]{:S(2)}) collective-permute-start(bf16[128,3072]{1,0:T(8,128)(2,1)S(1)} %get-tuple-element.75), channel_id=1, source_target_pairs={{0,4},{2,6},{4,8},{6,10},{8,12},{10,14},{12,0},{14,2},{1,5},{3,7},... | collective-permute-start | bytes 2359304 | tf_op jit(solution)/shard_map/ppermute | solution.py:549
  164.7 13.4 %collective-permute-start.27 = (bf16[128,3072]{1,0:T(8,128)(2,1)S(1)}, bf16[128,3072]{1,0:T(8,128)(2,1)S(1)}, u32[]{:S(2)}, u32[]{:S(2)}) collective-permute-start(bf16[128,3072]{1,0:T(8,128)(2,1)S(1)} %get-tuple-element.78.rows_ref), channel_id=1, source_target_pairs={{0,16},{16,0},{1,17},{17,1},{2,18},{18,2},{3,19},{19,3},{4,20},{20... | collective-permute-start | bytes 2359304 | tf_op jit(solution)/shard_map/ppermute | solution.py:33
  167.8 13.5 %collective-permute-start.28 = (bf16[128,2048]{1,0:T(8,128)(2,1)S(1)}, bf16[128,2048]{1,0:T(8,128)(2,1)S(1)}, u32[]{:S(2)}, u32[]{:S(2)}) collective-permute-start(bf16[128,2048]{1,0:T(8,128)(2,1)S(1)} %shard_map.143.own_ref), channel_id=1, source_target_pairs={{0,1},{1,0},{2,3},{3,2},{4,5},{5,4},{6,7},{7,6},{8,9},{9,8},{10,11... | collective-permute-start | bytes 1572872 | tf_op jit(solution)/shard_map/ppermute | solution.py:33
  179.9 9.2 %collective-permute-start.29 = (bf16[128,2048]{1,0:T(8,128)(2,1)S(1)}, bf16[128,2048]{1,0:T(8,128)(2,1)S(1)}, u32[]{:S(2)}, u32[]{:S(2)}) collective-permute-start(bf16[128,2048]{1,0:T(8,128)(2,1)S(1)} %shard_map.145.own_ref), channel_id=1, source_target_pairs={{0,1},{1,0},{2,3},{3,2},{4,5},{5,4},{6,7},{7,6},{8,9},{9,8},{10,11... | collective-permute-start | bytes 1572872 | tf_op jit(solution)/shard_map/ppermute | solution.py:33
  183.2 9.7 %collective-permute-start.31 = (bf16[128,1152]{1,0:T(8,128)(2,1)S(1)}, bf16[128,1152]{1,0:T(8,128)(2,1)S(1)}, u32[]{:S(2)}, u32[]{:S(2)}) collective-permute-start(bf16[128,1152]{1,0:T(8,128)(2,1)S(1)} %get-tuple-element.84), channel_id=1, source_target_pairs={{0,16},{16,0},{1,17},{17,1},{2,18},{18,2},{3,19},{19,3},{4,20},{20... | collective-permute-start | bytes 884744 | tf_op jit(solution)/shard_map/ppermute | solution.py:33
  191.1 6.8 %collective-permute-start.30 = (bf16[128,1152]{1,0:T(8,128)(2,1)S(1)}, bf16[128,1152]{1,0:T(8,128)(2,1)S(1)}, u32[]{:S(2)}, u32[]{:S(2)}) collective-permute-start(bf16[128,1152]{1,0:T(8,128)(2,1)S(1)} %get-tuple-element.81), channel_id=1, source_target_pairs={{0,16},{16,0},{1,17},{17,1},{2,18},{18,2},{3,19},{19,3},{4,20},{20... | collective-permute-start | bytes 884744 | tf_op jit(solution)/shard_map/ppermute | solution.py:33
  199.7 7.0 %collective-permute-start.32 = (bf16[128,512]{1,0:T(8,128)(2,1)S(1)}, bf16[128,512]{1,0:T(8,128)(2,1)S(1)}, u32[]{:S(2)}, u32[]{:S(2)}) collective-permute-start(bf16[128,512]{1,0:T(8,128)(2,1)S(1)} %get-tuple-element.87), channel_id=1, source_target_pairs={{0,4},{2,6},{4,8},{6,10},{8,12},{10,14},{12,0},{14,2},{1,5},{3,7},... | collective-permute-start | bytes 393224 | tf_op jit(solution)/shard_map/ppermute | solution.py:549
  199.8 8.7 %collective-permute-start.33 = (bf16[128,512]{1,0:T(8,128)(2,1)S(1)}, bf16[128,512]{1,0:T(8,128)(2,1)S(1)}, u32[]{:S(2)}, u32[]{:S(2)}) collective-permute-start(bf16[128,512]{1,0:T(8,128)(2,1)S(1)} %get-tuple-element.88), channel_id=1, source_target_pairs={{0,8},{2,10},{4,12},{6,14},{8,0},{10,2},{12,4},{14,6},{1,9},{3,11}... | collective-permute-start | bytes 393224 | tf_op jit(solution)/shard_map/ppermute | solution.py:549
  (28 other events, 268.6 us)

commit v5 on v2

--- a/solution.py
+++ b/solution.py
@@ -391,7 +391,7 @@
 
 
 def attend_kernel(places, word_rows, width, spots_ref, counts_ref, near_ref, *refs):
-    parts, outs, result_ref = refs[:6], refs[6 : 6 + places], refs[-1]
+    parts, outs, result_ref = refs[:6], refs[-1 - places : -1], refs[-1]
     near_rows = near_ref.shape[0]
     share = result_ref.shape[1]
     place, core, group = spots_ref[1], spots_ref[2], spots_ref[4]
@@ -440,17 +440,17 @@
         out_ref[...] = slim(dot(slim(jnp.where(put, 1.0, 0.0)), result_ref[...]))
 
 
-def attend_call(spots, counts, near, pieces, places, word_rows, width):
+def attend_call(spots, counts, near, pieces, places, word_rows, width, after):
     share = pieces[0].shape[1] // 2
     return pl.pallas_call(
         functools.partial(attend_kernel, places, word_rows, width),
-        in_specs=[SMEM, SMEM] + [VMEM] * (1 + len(pieces)),
+        in_specs=[SMEM, SMEM] + [VMEM] * (1 + len(pieces)) + [HBM] * len(after),
         out_specs=[VMEM] * places,
         out_shape=[jax.ShapeDtypeStruct((2 * word_rows, share), jnp.bfloat16)] * places,
         scratch_shapes=[pltpu.VMEM((near.shape[0], share), jnp.bfloat16)],
         compiler_params=PARAMS,
         cost_estimate=LIGHT,
-    )(spots, counts, near, *pieces)
+    )(spots, counts, near, *pieces, *after)
 
 
 def land_kernel(*refs):
@@ -699,8 +699,7 @@
         near, near_token = near_call(
             spots, cand_counts, *word_blocks, places, most * CAP, token
         )
-        final_weight = held_call(out_weight, [near_token])
-        my_vision, _ = add_call(home, [near_token, final_weight])
+        my_vision, _ = add_call(home, [near_token])
         other_vision = shifted(my_vision, "vis", 1)
         pieces = []
         for block in (my_vision, other_vision):
@@ -711,7 +710,10 @@
         parts = []
         for here, there in ((0, 1), (1, 0)):
             parts += [pieces[here][0], got[there], pieces[here][2]]
-        placed = attend_call(spots, cand_counts, near, parts, places, word_rows, width)
+        final_weight = held_call(out_weight, [pieces[1][1]])
+        placed = attend_call(
+            spots, cand_counts, near, parts, places, word_rows, width, [final_weight]
+        )
         landed = [to_place(part, step) if step else part for step, part in enumerate(placed)]
         kept, given = land_call(landed)
         across_both = [

time: 220 us -> 220 us (level)
  no operation moved by 1% of the time
where the time goes in v5:
time: 220 us; the launch traced here: 219 us
  waiting for transfers between devices  121 us (55%)
  Pallas kernels  44.2 us (20%)
  starting transfers between devices  38.3 us (17%)
  local copies, waits for them, and re-layouts  8.32 us (4%)
  other arithmetic  6.85 us (3%)
    ppermute x22, waiting for transfers between devices, shifted(): lax.ppermute(value, axis, [(i, (i + step) % count) for i in range(count)])  85.4 us
    ppermute x12, waiting for transfers between devices, to_place(): lax.ppermute(value, 'grp', [(i, (i + step * cores) % groups) for i in ran...  33.8 us
    ppermute x22, starting transfers between devices, shifted(): lax.ppermute(value, axis, [(i, (i + step) % count) for i in range(count)])  26 us
    ppermute x12, starting transfers between devices, to_place(): lax.ppermute(value, 'grp', [(i, (i + step * cores) % groups) for i in ran...  11.5 us
    pallas_call x4, Pallas kernels, down_call(): pl.pallas_call(functools.partial(down_kernel, cores), in_specs=[VMEM] * (...  11.1 us
    pallas_call x4, Pallas kernels, up_call(): pl.pallas_call(functools.partial(up_kernel, cores), in_specs=[VMEM] * (2...  10.6 us
    unnamed x42, local copies, waits for them, and re-layouts  8.07 us
    pallas_call x3, Pallas kernels, held_call(): pl.pallas_call(hold_kernel, in_specs=[HBM] * (1 + len(after)), out_specs=...  5.28 us
  transfers between devices with their start and end apart: 39, of which 26 were waited for; matrix products, arithmetic and copies ran while one was open for 3% of the time, Pallas kernels for 18%

profile of v5, /device:TPU:0, one launch (start us, length us, event | category | flops | bytes accessed | tf_op | source)
XLA Modules:
  0.0 219.4 jit_solution(3905319032377624362)
XLA Ops:
  4.8 3.0 %collective-permute-start = (f32[2,256]{1,0:T(2,128)S(1)}, f32[2,256]{1,0:T(2,128)S(1)}, u32[]{:S(2)}, u32[]{:S(2)}) collective-permute-start(f32[2,256]{1,0:T(2,128)S(1)} %pad_maximum_fusion.1), channel_id=1, source_target_pairs={{0,1},{1,0},{2,3},{3,2},{4,5},{5,4},{6,7},{7,6},{8,9},{9,8},{10,11... | collective-permute-start | bytes 6152 | tf_op jit(solution)/shard_map/ppermute | solution.py:33
  9.4 2.1 collective-permute-done.2
  14.9 17.5 %collective-permute-done.6.mine_ref = bf16[128,3072]{1,0:T(8,128)(2,1)S(1)} collective-permute-done((bf16[128,3072]{1,0:T(8,128)(2,1)S(1)}, bf16[128,3072]{1,0:T(8,128)(2,1)S(1)}, u32[]{:S(2)}, u32[]{:S(2)}) %collective-permute-start.6) | collective-permute-done | bytes 786464 | tf_op jit(solution)/shard_map/ppermute | solution.py:549
  34.1 4.6 %copy-done = bf16[3,2048,1024]{2,1,0:T(8,128)(2,1)S(1)} copy-done((bf16[3,2048,1024]{2,1,0:T(8,128)(2,1)S(1)}, bf16[3,2048,1024]{2,1,0:T(8,128)(2,1)}, u32[]{:S(2)}) %copy-start) | copy-done | bytes 12582936
  38.7 2.9 %shard_map.122 = (bf16[64,1536]{1,0:T(8,128)(2,1)S(1)}, f32[64,1536]{1,0:T(8,128)S(1)}, f32[8,128]{1,0:T(8,128)S(1)}) custom-call(s32[5]{0:T(128)S(1)} %stack.35.vis_ref.spots_ref, bf16[64,2048]{1,0:T(8,128)(2,1)S(1)} %bitcast.41, bf16[3,2048,1024]{2,1,0:T(8,128)(2,1)S(1)} %copy-done, bf16[128,3072]{1,0:T(8,128)(2,1)S(1)} %get-tuple-element.95.refs_0_.mine_ref, ...), custom_call_target="tpu_custom_call" | custom-call | flops 1024 | bytes 1024 | tf_op jit(solution)/shard_map/pallas_call | solution.py:257
  42.1 2.5 %shard_map.123.refs_1_ = bf16[3072,768]{1,0:T(8,128)(2,1)S(1)} custom-call(bf16[3072,768]{1,0:T(8,128)(2,1)} %collective-permute-done.1.value_ref, f32[8,128]{1,0:T(8,128)S(1)} %get-tuple-element.48.refs_0_.refs_2_), custom_call_target="tpu_custom_call" | custom-call | flops 1024 | bytes 1024 | tf_op jit(solution)/shard_map/pallas_call | solution.py:88
  45.9 2.7 %shard_map.124 = (bf16[256,1536]{1,0:T(8,128)(2,1)S(1)}, f32[8,128]{1,0:T(8,128)S(1)}) custom-call(bf16[128,3072]{1,0:T(8,128)(2,1)S(1)} %get-tuple-element.95.refs_0_.mine_ref, bf16[128,3072]{1,0:T(8,128)(2,1)S(1)} %get-tuple-element.94.theirs_ref, bf16[3072,768]{1,0:T(8,128)(2,1)S(1)} %bitcast.36, bf16[3072,768]{1,0:T(8,128)(2,1)S(1)} %shard_map.123.refs_1_, ...), custom_call_target="tpu_custom_call" | custom-call | flops 1024 | bytes 1024 | tf_op jit(solution)/shard_map/pallas_call | solution.py:118
  49.1 3.6 %collective-permute-done.10.value_ref = bf16[128,3072]{1,0:T(8,128)(2,1)S(1)} collective-permute-done((bf16[128,3072]{1,0:T(8,128)(2,1)S(1)}, bf16[128,3072]{1,0:T(8,128)(2,1)S(1)}, u32[]{:S(2)}, u32[]{:S(2)}) %collective-permute-start.10) | collective-permute-done | bytes 786464 | tf_op jit(solution)/shard_map/ppermute | solution.py:549
  56.4 2.6 %shard_map.126 = (bf16[256,1536]{1,0:T(8,128)(2,1)S(1)}, f32[8,128]{1,0:T(8,128)S(1)}) custom-call(bf16[128,3072]{1,0:T(8,128)(2,1)S(1)} %collective-permute-done.6.mine_ref, bf16[128,3072]{1,0:T(8,128)(2,1)S(1)} %collective-permute-done.7.theirs_ref, bf16[3072,768]{1,0:T(8,128)(2,1)S(1)} %bitcast.36, bf16[3072,768]{1,0:T(8,128)(2,1)S(1)} %shard_map.123.refs_1_, ...), custom_call_target="tpu_custom_call" | custom-call | flops 1024 | bytes 1024 | tf_op jit(solution)/shard_map/pallas_call | solution.py:118
  59.7 2.5 %shard_map.127.refs_1_ = bf16[768,3072]{1,0:T(8,128)(2,1)S(1)} custom-call(bf16[768,3072]{1,0:T(8,128)(2,1)} %collective-permute-done.5.value_ref, f32[8,128]{1,0:T(8,128)S(1)} %get-tuple-element.53.refs_0_.refs_2_), custom_call_target="tpu_custom_call" | custom-call | flops 1024 | bytes 1024 | tf_op jit(solution)/shard_map/pallas_call | solution.py:88
  62.2 6.9 %collective-permute-done.4.other_ref = bf16[256,1536]{1,0:T(8,128)(2,1)S(1)} collective-permute-done((bf16[256,1536]{1,0:T(8,128)(2,1)S(1)}, bf16[256,1536]{1,0:T(8,128)(2,1)S(1)}, u32[]{:S(2)}, u32[]{:S(2)}) %collective-permute-start.4) | collective-permute-done | bytes 786464 | tf_op jit(solution)/shard_map/ppermute | solution.py:33
  69.1 2.8 %shard_map.128 = (bf16[128,3072]{1,0:T(8,128)(2,1)S(1)}, bf16[128,3072]{1,0:T(8,128)(2,1)S(1)}, f32[8,128]{1,0:T(8,128)S(1)}) custom-call(bf16[256,1536]{1,0:T(8,128)(2,1)S(1)} %get-tuple-element.49.own_ref, bf16[256,1536]{1,0:T(8,128)(2,1)S(1)} %collective-permute-done.4.other_ref, bf16[768,3072]{1,0:T(8,128)(2,1)S(1)} %bitcast.34, ...), custom_call_target="tpu_custom_call" | custom-call | flops 1024 | bytes 1024 | tf_op jit(solution)/shard_map/pallas_call | solution.py:169
  75.1 2.6 %shard_map.131 = (bf16[256,1536]{1,0:T(8,128)(2,1)S(1)}, f32[8,128]{1,0:T(8,128)S(1)}) custom-call(bf16[128,3072]{1,0:T(8,128)(2,1)S(1)} %shard_map.129.mine_ref, bf16[128,3072]{1,0:T(8,128)(2,1)S(1)} %collective-permute-done.14.theirs_ref, bf16[3072,768]{1,0:T(8,128)(2,1)S(1)} %bitcast.36, bf16[3072,768]{1,0:T(8,128)(2,1)S(1)} %shard_map.123.refs_1_, ...), custom_call_target="tpu_custom_call" | custom-call | flops 1024 | bytes 1024 | tf_op jit(solution)/shard_map/pallas_call | solution.py:118
  78.3 7.6 %collective-permute-done.13.other_ref = bf16[256,1536]{1,0:T(8,128)(2,1)S(1)} collective-permute-done((bf16[256,1536]{1,0:T(8,128)(2,1)S(1)}, bf16[256,1536]{1,0:T(8,128)(2,1)S(1)}, u32[]{:S(2)}, u32[]{:S(2)}) %collective-permute-start.13) | collective-permute-done | bytes 786464 | tf_op jit(solution)/shard_map/ppermute | solution.py:33
  85.9 2.8 %shard_map.132 = (bf16[128,3072]{1,0:T(8,128)(2,1)S(1)}, bf16[128,3072]{1,0:T(8,128)(2,1)S(1)}, f32[8,128]{1,0:T(8,128)S(1)}) custom-call(bf16[256,1536]{1,0:T(8,128)(2,1)S(1)} %get-tuple-element.57.own_ref, bf16[256,1536]{1,0:T(8,128)(2,1)S(1)} %collective-permute-done.13.other_ref, bf16[768,3072]{1,0:T(8,128)(2,1)S(1)} %bitcast.34, ...), custom_call_target="tpu_custom_call" | custom-call | flops 1024 | bytes 1024 | tf_op jit(solution)/shard_map/pallas_call | solution.py:169
  90.3 3.8 %collective-permute-start.20 = (bf16[64,1664]{1,0:T(8,128)(2,1)S(1)}, bf16[64,1664]{1,0:T(8,128)(2,1)S(1)}, u32[]{:S(2)}, u32[]{:S(2)}) collective-permute-start(bf16[64,1664]{1,0:T(8,128)(2,1)S(1)} %shard_map.125.refs_3_.refs_0_), channel_id=1, source_target_pairs={{0,12},{2,14},{4,0},{6,2},{8,4},{10,6},{12,8},{14,10},{1,13},{3,15... | collective-permute-start | bytes 638984 | tf_op jit(solution)/shard_map/ppermute | solution.py:549
  94.1 2.6 %shard_map.133 = (bf16[256,1536]{1,0:T(8,128)(2,1)S(1)}, f32[8,128]{1,0:T(8,128)S(1)}) custom-call(bf16[128,3072]{1,0:T(8,128)(2,1)S(1)} %shard_map.130.refs_3_.mine_ref, bf16[128,3072]{1,0:T(8,128)(2,1)S(1)} %collective-permute-done.12.theirs_ref, bf16[3072,768]{1,0:T(8,128)(2,1)S(1)} %bitcast.36, bf16[3072,768]{1,0:T(8,128)(2,1)S(1)} %shard_map.123.refs_1_, ...), custom_call_target="tpu_custom_call" | custom-call | flops 1024 | bytes 1024 | tf_op jit(solution)/shard_map/pallas_call | solution.py:118
  97.5 4.2 %collective-permute-done.19.refs_3_.refs_2_ = bf16[64,1664]{1,0:T(8,128)(2,1)S(1)} collective-permute-done((bf16[64,1664]{1,0:T(8,128)(2,1)S(1)}, bf16[64,1664]{1,0:T(8,128)(2,1)S(1)}, u32[]{:S(2)}, u32[]{:S(2)}) %collective-permute-start.19) | collective-permute-done | bytes 213024 | tf_op jit(solution)/shard_map/ppermute | solution.py:549
  102.8 2.8 %shard_map.134 = (bf16[128,3072]{1,0:T(8,128)(2,1)S(1)}, bf16[128,3072]{1,0:T(8,128)(2,1)S(1)}, f32[8,128]{1,0:T(8,128)S(1)}) custom-call(bf16[256,1536]{1,0:T(8,128)(2,1)S(1)} %get-tuple-element.63.own_ref, bf16[256,1536]{1,0:T(8,128)(2,1)S(1)} %collective-permute-done.18.other_ref, bf16[768,3072]{1,0:T(8,128)(2,1)S(1)} %bitcast.34, ...), custom_call_target="tpu_custom_call" | custom-call | flops 1024 | bytes 1024 | tf_op jit(solution)/shard_map/pallas_call | solution.py:169
  108.9 6.9 %collective-permute-done.16.other_ref = bf16[256,1536]{1,0:T(8,128)(2,1)S(1)} collective-permute-done((bf16[256,1536]{1,0:T(8,128)(2,1)S(1)}, bf16[256,1536]{1,0:T(8,128)(2,1)S(1)}, u32[]{:S(2)}, u32[]{:S(2)}) %collective-permute-start.16) | collective-permute-done | bytes 786464 | tf_op jit(solution)/shard_map/ppermute | solution.py:33
  115.8 2.8 %shard_map.136 = (bf16[128,3072]{1,0:T(8,128)(2,1)S(1)}, bf16[128,3072]{1,0:T(8,128)(2,1)S(1)}, f32[8,128]{1,0:T(8,128)S(1)}) custom-call(bf16[256,1536]{1,0:T(8,128)(2,1)S(1)} %get-tuple-element.60.own_ref, bf16[256,1536]{1,0:T(8,128)(2,1)S(1)} %collective-permute-done.16.other_ref, bf16[768,3072]{1,0:T(8,128)(2,1)S(1)} %bitcast.34, ...), custom_call_target="tpu_custom_call" | custom-call | flops 1024 | bytes 1024 | tf_op jit(solution)/shard_map/pallas_call | solution.py:169
  120.2 4.8 %collective-permute-done.22.refs_1_ = bf16[128,3072]{1,0:T(8,128)(2,1)S(1)} collective-permute-done((bf16[128,3072]{1,0:T(8,128)(2,1)S(1)}, bf16[128,3072]{1,0:T(8,128)(2,1)S(1)}, u32[]{:S(2)}, u32[]{:S(2)}) %collective-permute-start.22) | collective-permute-done | bytes 786464 | tf_op jit(solution)/shard_map/ppermute | solution.py:33
  127.0 14.8 %collective-permute-done.21.refs_1_ = bf16[128,3072]{1,0:T(8,128)(2,1)S(1)} collective-permute-done((bf16[128,3072]{1,0:T(8,128)(2,1)S(1)}, bf16[128,3072]{1,0:T(8,128)(2,1)S(1)}, u32[]{:S(2)}, u32[]{:S(2)}) %collective-permute-start.21) | collective-permute-done | bytes 786464 | tf_op jit(solution)/shard_map/ppermute | solution.py:33
  143.3 11.7 %collective-permute-done.9.refs_2_ = bf16[128,3072]{1,0:T(8,128)(2,1)S(1)} collective-permute-done((bf16[128,3072]{1,0:T(8,128)(2,1)S(1)}, bf16[128,3072]{1,0:T(8,128)(2,1)S(1)}, u32[]{:S(2)}, u32[]{:S(2)}) %collective-permute-start.9) | collective-permute-done | bytes 786464 | tf_op jit(solution)/shard_map/ppermute | solution.py:33
  161.2 10.7 %collective-permute-done.27.rows_ref = bf16[128,3072]{1,0:T(8,128)(2,1)S(1)} collective-permute-done((bf16[128,3072]{1,0:T(8,128)(2,1)S(1)}, bf16[128,3072]{1,0:T(8,128)(2,1)S(1)}, u32[]{:S(2)}, u32[]{:S(2)}) %collective-permute-start.27) | collective-permute-done | bytes 786464 | tf_op jit(solution)/shard_map/ppermute | solution.py:33
  177.8 5.2 %collective-permute-done.29.other_ref = bf16[128,2048]{1,0:T(8,128)(2,1)S(1)} collective-permute-done((bf16[128,2048]{1,0:T(8,128)(2,1)S(1)}, bf16[128,2048]{1,0:T(8,128)(2,1)S(1)}, u32[]{:S(2)}, u32[]{:S(2)}) %collective-permute-start.29) | collective-permute-done | bytes 524320 | tf_op jit(solution)/shard_map/ppermute | solution.py:33
  186.8 4.9 %collective-permute-done.30.refs_1_ = bf16[128,1152]{1,0:T(8,128)(2,1)S(1)} collective-permute-done((bf16[128,1152]{1,0:T(8,128)(2,1)S(1)}, bf16[128,1152]{1,0:T(8,128)(2,1)S(1)}, u32[]{:S(2)}, u32[]{:S(2)}) %collective-permute-start.30) | collective-permute-done | bytes 294944 | tf_op jit(solution)/shard_map/ppermute | solution.py:33
  195.0 2.1 collective-permute-start.33
  200.5 2.8 %collective-permute-done.33.refs_2_ = bf16[128,512]{1,0:T(8,128)(2,1)S(1)} collective-permute-done((bf16[128,512]{1,0:T(8,128)(2,1)S(1)}, bf16[128,512]{1,0:T(8,128)(2,1)S(1)}, u32[]{:S(2)}, u32[]{:S(2)}) %collective-permute-start.33) | collective-permute-done | bytes 131104 | tf_op jit(solution)/shard_map/ppermute | solution.py:549
  205.5 2.6 %collective-permute-done.36.vis_ref = bf16[64,512]{1,0:T(8,128)(2,1)S(1)} collective-permute-done((bf16[64,512]{1,0:T(8,128)(2,1)S(1)}, bf16[64,512]{1,0:T(8,128)(2,1)S(1)}, u32[]{:S(2)}, u32[]{:S(2)}) %collective-permute-start.36) | collective-permute-done | bytes 65568 | tf_op jit(solution)/shard_map/ppermute | solution.py:33
  209.5 2.2 copy-done.2
  215.2 3.5 %collective-permute-done.38 = bf16[32,2048]{1,0:T(8,128)(2,1)S(1)} collective-permute-done((bf16[32,2048]{1,0:T(8,128)(2,1)S(1)}, bf16[32,2048]{1,0:T(8,128)(2,1)S(1)}, u32[]{:S(2)}, u32[]{:S(2)}) %collective-permute-start.38) | collective-permute-done | bytes 131104 | tf_op jit(solution)/shard_map/ppermute | solution.py:33
  (137 shorter events, 63.1 us)
Async XLA Ops:
  0.7 41.5 %collective-permute-start.1 = (bf16[3072,768]{1,0:T(8,128)(2,1)}, bf16[3072,768]{1,0:T(8,128)(2,1)}, u32[]{:S(2)}, u32[]{:S(2)}) collective-permute-start(bf16[3072,768]{1,0:T(8,128)(2,1)} %refs_0_.13), channel_id=1, source_target_pairs={{0,2},{2,0},{4,6},{6,4},{8,10},{10,8},{12,14},{14,12},{1,3},{3,1},... | collective-permute-start | bytes 14155784 | tf_op jit(solution)/shard_map/ppermute | solution.py:542
  1.2 58.5 %collective-permute-start.5 = (bf16[768,3072]{1,0:T(8,128)(2,1)}, bf16[768,3072]{1,0:T(8,128)(2,1)}, u32[]{:S(2)}, u32[]{:S(2)}) collective-permute-start(bf16[768,3072]{1,0:T(8,128)(2,1)} %refs_0_.15), channel_id=1, source_target_pairs={{0,2},{2,0},{4,6},{6,4},{8,10},{10,8},{12,14},{14,12},{1,3},{3,1},... | collective-permute-start | bytes 14155784 | tf_op jit(solution)/shard_map/ppermute | solution.py:543
  12.4 20.0 %collective-permute-start.6 = (bf16[128,3072]{1,0:T(8,128)(2,1)S(1)}, bf16[128,3072]{1,0:T(8,128)(2,1)S(1)}, u32[]{:S(2)}, u32[]{:S(2)}) collective-permute-start(bf16[128,3072]{1,0:T(8,128)(2,1)S(1)} %get-tuple-element.95.refs_0_.mine_ref), channel_id=1, source_target_pairs={{0,4},{2,6},{4,8},{6,10},{8,12},{10,14},{12,0},{14,2},{1,5},{3,7},... | collective-permute-start | bytes 2359304 | tf_op jit(solution)/shard_map/ppermute | solution.py:549
  14.1 19.8 %collective-permute-start.3 = (bf16[4,8,2048]{2,1,0:T(8,128)(2,1)S(1)}, bf16[4,8,2048]{2,1,0:T(8,128)(2,1)S(1)}, u32[]{:S(2)}, u32[]{:S(2)}) collective-permute-start(bf16[4,8,2048]{2,1,0:T(8,128)(2,1)S(1)} %fusion.8), channel_id=1, source_target_pairs={{0,1},{1,0},{2,3},{3,2},{4,5},{5,4},{6,7},{7,6},{8,9},{9,8},{10,11... | collective-permute-start | bytes 393224 | tf_op jit(solution)/shard_map/ppermute | solution.py:33
  32.4 24.0 %collective-permute-start.7 = (bf16[128,3072]{1,0:T(8,128)(2,1)S(1)}, bf16[128,3072]{1,0:T(8,128)(2,1)S(1)}, u32[]{:S(2)}, u32[]{:S(2)}) collective-permute-start(bf16[128,3072]{1,0:T(8,128)(2,1)S(1)} %collective-permute-done.6.mine_ref), channel_id=1, source_target_pairs={{0,16},{16,0},{1,17},{17,1},{2,18},{18,2},{3,19},{19,3},{4,20},{20... | collective-permute-start | bytes 2359304 | tf_op jit(solution)/shard_map/ppermute | solution.py:33
  33.9 18.8 %collective-permute-start.10 = (bf16[128,3072]{1,0:T(8,128)(2,1)S(1)}, bf16[128,3072]{1,0:T(8,128)(2,1)S(1)}, u32[]{:S(2)}, u32[]{:S(2)}) collective-permute-start(bf16[128,3072]{1,0:T(8,128)(2,1)S(1)} %collective-permute-done.6.mine_ref), channel_id=1, source_target_pairs={{0,4},{2,6},{4,8},{6,10},{8,12},{10,14},{12,0},{14,2},{1,5},{3,7},... | collective-permute-start | bytes 2359304 | tf_op jit(solution)/shard_map/ppermute | solution.py:549
  41.5 12.8 %collective-permute-start.8 = (bf16[64,1536]{1,0:T(8,128)(2,1)S(1)}, bf16[64,1536]{1,0:T(8,128)(2,1)S(1)}, u32[]{:S(2)}, u32[]{:S(2)}) collective-permute-start(bf16[64,1536]{1,0:T(8,128)(2,1)S(1)} %get-tuple-element.52), channel_id=1, source_target_pairs={{0,16},{16,0},{1,17},{17,1},{2,18},{18,2},{3,19},{19,3},{4,20},{20... | collective-permute-start | bytes 589832 | tf_op jit(solution)/shard_map/ppermute | solution.py:33
  48.5 20.5 %collective-permute-start.4 = (bf16[256,1536]{1,0:T(8,128)(2,1)S(1)}, bf16[256,1536]{1,0:T(8,128)(2,1)S(1)}, u32[]{:S(2)}, u32[]{:S(2)}) collective-permute-start(bf16[256,1536]{1,0:T(8,128)(2,1)S(1)} %get-tuple-element.49.own_ref), channel_id=1, source_target_pairs={{0,1},{1,0},{2,3},{3,2},{4,5},{5,4},{6,7},{7,6},{8,9},{9,8},{10,11... | collective-permute-start | bytes 2359304 | tf_op jit(solution)/shard_map/ppermute | solution.py:33
  52.7 20.1 %collective-permute-start.11 = (bf16[128,3072]{1,0:T(8,128)(2,1)S(1)}, bf16[128,3072]{1,0:T(8,128)(2,1)S(1)}, u32[]{:S(2)}, u32[]{:S(2)}) collective-permute-start(bf16[128,3072]{1,0:T(8,128)(2,1)S(1)} %shard_map.129.mine_ref), channel_id=1, source_target_pairs={{0,4},{2,6},{4,8},{6,10},{8,12},{10,14},{12,0},{14,2},{1,5},{3,7},... | collective-permute-start | bytes 2359304 | tf_op jit(solution)/shard_map/ppermute | solution.py:549
  54.3 20.7 %collective-permute-start.14 = (bf16[128,3072]{1,0:T(8,128)(2,1)S(1)}, bf16[128,3072]{1,0:T(8,128)(2,1)S(1)}, u32[]{:S(2)}, u32[]{:S(2)}) collective-permute-start(bf16[128,3072]{1,0:T(8,128)(2,1)S(1)} %shard_map.129.mine_ref), channel_id=1, source_target_pairs={{0,16},{16,0},{1,17},{17,1},{2,18},{18,2},{3,19},{19,3},{4,20},{20... | collective-permute-start | bytes 2359304 | tf_op jit(solution)/shard_map/ppermute | solution.py:33
  59.1 26.8 %collective-permute-start.13 = (bf16[256,1536]{1,0:T(8,128)(2,1)S(1)}, bf16[256,1536]{1,0:T(8,128)(2,1)S(1)}, u32[]{:S(2)}, u32[]{:S(2)}) collective-permute-start(bf16[256,1536]{1,0:T(8,128)(2,1)S(1)} %get-tuple-element.57.own_ref), channel_id=1, source_target_pairs={{0,1},{1,0},{2,3},{3,2},{4,5},{5,4},{6,7},{7,6},{8,9},{9,8},{10,11... | collective-permute-start | bytes 2359304 | tf_op jit(solution)/shard_map/ppermute | solution.py:33
  59.7 15.4 %collective-permute-start.15 = (bf16[64,1664]{1,0:T(8,128)(2,1)S(1)}, bf16[64,1664]{1,0:T(8,128)(2,1)S(1)}, u32[]{:S(2)}, u32[]{:S(2)}) collective-permute-start(bf16[64,1664]{1,0:T(8,128)(2,1)S(1)} %shard_map.125.refs_3_.refs_0_), channel_id=1, source_target_pairs={{0,4},{2,6},{4,8},{6,10},{8,12},{10,14},{12,0},{14,2},{1,5},{3,7},... | collective-permute-start | bytes 638984 | tf_op jit(solution)/shard_map/ppermute | solution.py:549
  72.8 21.3 %collective-permute-start.12 = (bf16[128,3072]{1,0:T(8,128)(2,1)S(1)}, bf16[128,3072]{1,0:T(8,128)(2,1)S(1)}, u32[]{:S(2)}, u32[]{:S(2)}) collective-permute-start(bf16[128,3072]{1,0:T(8,128)(2,1)S(1)} %shard_map.130.refs_3_.mine_ref), channel_id=1, source_target_pairs={{0,16},{16,0},{1,17},{17,1},{2,18},{18,2},{3,19},{19,3},{4,20},{20... | collective-permute-start | bytes 2359304 | tf_op jit(solution)/shard_map/ppermute | solution.py:33
  77.7 25.1 %collective-permute-start.18 = (bf16[256,1536]{1,0:T(8,128)(2,1)S(1)}, bf16[256,1536]{1,0:T(8,128)(2,1)S(1)}, u32[]{:S(2)}, u32[]{:S(2)}) collective-permute-start(bf16[256,1536]{1,0:T(8,128)(2,1)S(1)} %get-tuple-element.63.own_ref), channel_id=1, source_target_pairs={{0,1},{1,0},{2,3},{3,2},{4,5},{5,4},{6,7},{7,6},{8,9},{9,8},{10,11... | collective-permute-start | bytes 2359304 | tf_op jit(solution)/shard_map/ppermute | solution.py:33
  88.7 19.4 %collective-permute-start.17 = (bf16[128,3072]{1,0:T(8,128)(2,1)S(1)}, bf16[128,3072]{1,0:T(8,128)(2,1)S(1)}, u32[]{:S(2)}, u32[]{:S(2)}) collective-permute-start(bf16[128,3072]{1,0:T(8,128)(2,1)S(1)} %get-tuple-element.62), channel_id=1, source_target_pairs={{0,16},{16,0},{1,17},{17,1},{2,18},{18,2},{3,19},{19,3},{4,20},{20... | collective-permute-start | bytes 2359304 | tf_op jit(solution)/shard_map/ppermute | solution.py:33
  90.3 7.2 %collective-permute-start.20 = (bf16[64,1664]{1,0:T(8,128)(2,1)S(1)}, bf16[64,1664]{1,0:T(8,128)(2,1)S(1)}, u32[]{:S(2)}, u32[]{:S(2)}) collective-permute-start(bf16[64,1664]{1,0:T(8,128)(2,1)S(1)} %shard_map.125.refs_3_.refs_0_), channel_id=1, source_target_pairs={{0,12},{2,14},{4,0},{6,2},{8,4},{10,6},{12,8},{14,10},{1,13},{3,15... | collective-permute-start | bytes 638984 | tf_op jit(solution)/shard_map/ppermute | solution.py:549
  94.1 7.6 %collective-permute-start.19 = (bf16[64,1664]{1,0:T(8,128)(2,1)S(1)}, bf16[64,1664]{1,0:T(8,128)(2,1)S(1)}, u32[]{:S(2)}, u32[]{:S(2)}) collective-permute-start(bf16[64,1664]{1,0:T(8,128)(2,1)S(1)} %collective-permute-done.15.refs_4_.refs_1_), channel_id=1, source_target_pairs={{0,4},{2,6},{4,8},{6,10},{8,12},{10,14},{12,0},{14,2},{1,5},{3,7},... | collective-permute-start | bytes 638984 | tf_op jit(solution)/shard_map/ppermute | solution.py:549
  96.7 19.1 %collective-permute-start.16 = (bf16[256,1536]{1,0:T(8,128)(2,1)S(1)}, bf16[256,1536]{1,0:T(8,128)(2,1)S(1)}, u32[]{:S(2)}, u32[]{:S(2)}) collective-permute-start(bf16[256,1536]{1,0:T(8,128)(2,1)S(1)} %get-tuple-element.60.own_ref), channel_id=1, source_target_pairs={{0,1},{1,0},{2,3},{3,2},{4,5},{5,4},{6,7},{7,6},{8,9},{9,8},{10,11... | collective-permute-start | bytes 2359304 | tf_op jit(solution)/shard_map/ppermute | solution.py:33
  105.6 19.4 %collective-permute-start.22 = (bf16[128,3072]{1,0:T(8,128)(2,1)S(1)}, bf16[128,3072]{1,0:T(8,128)(2,1)S(1)}, u32[]{:S(2)}, u32[]{:S(2)}) collective-permute-start(bf16[128,3072]{1,0:T(8,128)(2,1)S(1)} %get-tuple-element.70), channel_id=1, source_target_pairs={{0,16},{16,0},{1,17},{17,1},{2,18},{18,2},{3,19},{19,3},{4,20},{20... | collective-permute-start | bytes 2359304 | tf_op jit(solution)/shard_map/ppermute | solution.py:33
  108.3 16.7 %collective-permute-start.23 = (bf16[128,3072]{1,0:T(8,128)(2,1)S(1)}, bf16[128,3072]{1,0:T(8,128)(2,1)S(1)}, u32[]{:S(2)}, u32[]{:S(2)}) collective-permute-start(bf16[128,3072]{1,0:T(8,128)(2,1)S(1)} %get-tuple-element.71), channel_id=1, source_target_pairs={{0,4},{2,6},{4,8},{6,10},{8,12},{10,14},{12,0},{14,2},{1,5},{3,7},... | collective-permute-start | bytes 2359304 | tf_op jit(solution)/shard_map/ppermute | solution.py:549
  118.6 23.2 %collective-permute-start.21 = (bf16[128,3072]{1,0:T(8,128)(2,1)S(1)}, bf16[128,3072]{1,0:T(8,128)(2,1)S(1)}, u32[]{:S(2)}, u32[]{:S(2)}) collective-permute-start(bf16[128,3072]{1,0:T(8,128)(2,1)S(1)} %get-tuple-element.68), channel_id=1, source_target_pairs={{0,16},{16,0},{1,17},{17,1},{2,18},{18,2},{3,19},{19,3},{4,20},{20... | collective-permute-start | bytes 2359304 | tf_op jit(solution)/shard_map/ppermute | solution.py:33
  125.3 16.5 %collective-permute-start.24 = (bf16[128,3072]{1,0:T(8,128)(2,1)S(1)}, bf16[128,3072]{1,0:T(8,128)(2,1)S(1)}, u32[]{:S(2)}, u32[]{:S(2)}) collective-permute-start(bf16[128,3072]{1,0:T(8,128)(2,1)S(1)} %get-tuple-element.73), channel_id=1, source_target_pairs={{0,4},{2,6},{4,8},{6,10},{8,12},{10,14},{12,0},{14,2},{1,5},{3,7},... | collective-permute-start | bytes 2359304 | tf_op jit(solution)/shard_map/ppermute | solution.py:549
  125.4 16.8 %collective-permute-start.26 = (bf16[256,1664]{1,0:T(8,128)(2,1)S(1)}, bf16[256,1664]{1,0:T(8,128)(2,1)S(1)}, u32[]{:S(2)}, u32[]{:S(2)}) collective-permute-start(bf16[256,1664]{1,0:T(8,128)(2,1)S(1)} %shard_map.139.own_ref), channel_id=1, source_target_pairs={{0,2},{2,0},{4,6},{6,4},{8,10},{10,8},{12,14},{14,12},{1,3},{3,1},... | collective-permute-start | bytes 2555912 | tf_op jit(solution)/shard_map/ppermute | solution.py:689
  125.5 29.5 %collective-permute-start.9 = (bf16[128,3072]{1,0:T(8,128)(2,1)S(1)}, bf16[128,3072]{1,0:T(8,128)(2,1)S(1)}, u32[]{:S(2)}, u32[]{:S(2)}) collective-permute-start(bf16[128,3072]{1,0:T(8,128)(2,1)S(1)} %get-tuple-element.55), channel_id=1, source_target_pairs={{0,16},{16,0},{1,17},{17,1},{2,18},{18,2},{3,19},{19,3},{4,20},{20... | collective-permute-start | bytes 2359304 | tf_op jit(solution)/shard_map/ppermute | solution.py:33
  142.1 14.1 %collective-permute-start.25 = (bf16[128,3072]{1,0:T(8,128)(2,1)S(1)}, bf16[128,3072]{1,0:T(8,128)(2,1)S(1)}, u32[]{:S(2)}, u32[]{:S(2)}) collective-permute-start(bf16[128,3072]{1,0:T(8,128)(2,1)S(1)} %get-tuple-element.75), channel_id=1, source_target_pairs={{0,4},{2,6},{4,8},{6,10},{8,12},{10,14},{12,0},{14,2},{1,5},{3,7},... | collective-permute-start | bytes 2359304 | tf_op jit(solution)/shard_map/ppermute | solution.py:549
  157.2 14.7 %collective-permute-start.27 = (bf16[128,3072]{1,0:T(8,128)(2,1)S(1)}, bf16[128,3072]{1,0:T(8,128)(2,1)S(1)}, u32[]{:S(2)}, u32[]{:S(2)}) collective-permute-start(bf16[128,3072]{1,0:T(8,128)(2,1)S(1)} %get-tuple-element.78.rows_ref), channel_id=1, source_target_pairs={{0,16},{16,0},{1,17},{17,1},{2,18},{18,2},{3,19},{19,3},{4,20},{20... | collective-permute-start | bytes 2359304 | tf_op jit(solution)/shard_map/ppermute | solution.py:33
  160.6 14.2 %collective-permute-start.28 = (bf16[128,2048]{1,0:T(8,128)(2,1)S(1)}, bf16[128,2048]{1,0:T(8,128)(2,1)S(1)}, u32[]{:S(2)}, u32[]{:S(2)}) collective-permute-start(bf16[128,2048]{1,0:T(8,128)(2,1)S(1)} %shard_map.142.own_ref), channel_id=1, source_target_pairs={{0,1},{1,0},{2,3},{3,2},{4,5},{5,4},{6,7},{7,6},{8,9},{9,8},{10,11... | collective-permute-start | bytes 1572872 | tf_op jit(solution)/shard_map/ppermute | solution.py:33
  173.8 9.2 %collective-permute-start.29 = (bf16[128,2048]{1,0:T(8,128)(2,1)S(1)}, bf16[128,2048]{1,0:T(8,128)(2,1)S(1)}, u32[]{:S(2)}, u32[]{:S(2)}) collective-permute-start(bf16[128,2048]{1,0:T(8,128)(2,1)S(1)} %shard_map.144.own_ref), channel_id=1, source_target_pairs={{0,1},{1,0},{2,3},{3,2},{4,5},{5,4},{6,7},{7,6},{8,9},{9,8},{10,11... | collective-permute-start | bytes 1572872 | tf_op jit(solution)/shard_map/ppermute | solution.py:33
  176.7 10.1 %collective-permute-start.31 = (bf16[128,1152]{1,0:T(8,128)(2,1)S(1)}, bf16[128,1152]{1,0:T(8,128)(2,1)S(1)}, u32[]{:S(2)}, u32[]{:S(2)}) collective-permute-start(bf16[128,1152]{1,0:T(8,128)(2,1)S(1)} %get-tuple-element.84), channel_id=1, source_target_pairs={{0,16},{16,0},{1,17},{17,1},{2,18},{18,2},{3,19},{19,3},{4,20},{20... | collective-permute-start | bytes 884744 | tf_op jit(solution)/shard_map/ppermute | solution.py:33
  184.9 6.8 %collective-permute-start.30 = (bf16[128,1152]{1,0:T(8,128)(2,1)S(1)}, bf16[128,1152]{1,0:T(8,128)(2,1)S(1)}, u32[]{:S(2)}, u32[]{:S(2)}) collective-permute-start(bf16[128,1152]{1,0:T(8,128)(2,1)S(1)} %get-tuple-element.81.refs_0_), channel_id=1, source_target_pairs={{0,16},{16,0},{1,17},{17,1},{2,18},{18,2},{3,19},{19,3},{4,20},{20... | collective-permute-start | bytes 884744 | tf_op jit(solution)/shard_map/ppermute | solution.py:33
  193.6 6.9 %collective-permute-start.32 = (bf16[128,512]{1,0:T(8,128)(2,1)S(1)}, bf16[128,512]{1,0:T(8,128)(2,1)S(1)}, u32[]{:S(2)}, u32[]{:S(2)}) collective-permute-start(bf16[128,512]{1,0:T(8,128)(2,1)S(1)} %get-tuple-element.87), channel_id=1, source_target_pairs={{0,4},{2,6},{4,8},{6,10},{8,12},{10,14},{12,0},{14,2},{1,5},{3,7},... | collective-permute-start | bytes 393224 | tf_op jit(solution)/shard_map/ppermute | solution.py:549
  195.0 8.3 %collective-permute-start.33 = (bf16[128,512]{1,0:T(8,128)(2,1)S(1)}, bf16[128,512]{1,0:T(8,128)(2,1)S(1)}, u32[]{:S(2)}, u32[]{:S(2)}) collective-permute-start(bf16[128,512]{1,0:T(8,128)(2,1)S(1)} %get-tuple-element.88), channel_id=1, source_target_pairs={{0,8},{2,10},{4,12},{6,14},{8,0},{10,2},{12,4},{14,6},{1,9},{3,11}... | collective-permute-start | bytes 393224 | tf_op jit(solution)/shard_map/ppermute | solution.py:549
  (28 other events, 317.3 us)
